TPU v7x, 32 devices: a whole 2x2x4 slice. The times are simulated.
32 devices in a mesh: slab: 8 (over z, y), quad: 4 (over x, core).
Axes of the slice: x: 2, y: 2, z: 4, core: 2. Of those that a mesh axis runs over, the one named last changes fastest.
Arguments:
- grain_cell: int32 [4, 262144], P(None, ('slab', 'quad')), may hold values from 0 to 254, as said below
- grain_count: int32 [32], P(('slab', 'quad')), may hold values from 2048 to 8192, as said below
- grain_weight: float32 [262144], P(('slab', 'quad')), may hold values from 0.05 to 0.95
- grain_volume: float32 [262144], P(('slab', 'quad')), may hold values from 0.02 to 0.4
- grain_velocity: float32 [3, 262144], P(None, ('slab', 'quad')), may hold values from -6 to 6
Outputs:
- pressure: float32 [32, 64, 256], P('slab', 'quad')
- drag: float32 [3, 262144], P(None, ('slab', 'quad'))
Inputs may be any that keep to these rules, and one draw needn't show every extreme that they name: grain_cell[0] < 4, grain_cell[1] < 4, grain_cell[2] < 16, grain_cell[3] <= 254; among the slots of one device at most 4096 name the same quarter, and on every device exactly 4096 name one quarter. `grain_count`: some device has all 8192 slots occupied.
All inputs are finite; a program needn't handle non-finite values.
Results may differ from a plain program's by a relative error of at most 0.00002.
Values sent between devices are 32-bit elements; how exact they have to be, the bound alone decides.
No kernel may reach another device: no remote copies, remote signals or barrier semaphores. Data moves between devices by JAX's collectives and lax.ppermute only.
A program may use at most 128 MiB of HBM per device.

v0:
```python
import functools

import jax
import jax.numpy as jnp
from jax import lax
from jax.experimental import pallas as pl
from jax.experimental.pallas import tpu as pltpu
from jax.sharding import PartitionSpec as P

CH = 4
CA = 16
CB = 256
ITERS = 12
LANES = 128
SUBLANES = 8
DEPTH = 3
FIRST = CH * DEPTH + 1

damping = 0.05
source_gain = 4.0

VMEM = pl.BlockSpec(memory_space=pltpu.VMEM)
SMEM = pl.BlockSpec(memory_space=pltpu.SMEM)
HBM = pl.BlockSpec(memory_space=pltpu.HBM)
LIMIT = pltpu.CompilerParams(vmem_limit_bytes=48 * 1024 * 1024)


def reach(distance):
    needed = ITERS - 1 - CH * (max(distance, 1) - 1)
    return 1 << (needed - 1).bit_length()


def lanes_of(shape):
    return lax.broadcasted_iota(jnp.int32, shape, len(shape) - 1)


def turned(value, shift):
    shift %= LANES
    return pltpu.roll(value, shift, value.ndim - 1) if shift else value


def pack_own(window, own):
    pieces = LANES // own
    tall = window.shape[1] // pieces
    lane = lanes_of((window.shape[0], tall, LANES))
    result = window[:, :tall]
    for piece in range(1, pieces):
        part = turned(window[:, piece * tall : (piece + 1) * tall], piece * own)
        result = jnp.where(lane < piece * own, result, part)
    return result


def unpack_own(packed, own):
    pieces = LANES // own
    return jnp.concatenate([turned(packed, -piece * own) for piece in range(pieces)], axis=1)


def strip_plan(across, fields, halo):
    rows = across * 2 * halo // LANES
    return (1, rows) if rows >= SUBLANES else (fields, rows * fields)


def packed_rows(across, fields, halo, own):
    shared, rows = strip_plan(across, fields, halo)
    return fields * CH * across * own // LANES + (fields // shared) * CH * rows


def pack(windows, halo, own):
    across = windows[0].shape[1]
    shared, rows = strip_plan(across, len(windows), halo)
    pieces = [pack_own(window, own) for window in windows]
    lane = lanes_of(windows[0].shape)
    joined = [
        jnp.where(lane >= LANES - halo, window, turned(window, LANES - 2 * halo - own))
        for window in windows
    ]
    lane = lanes_of((CH, rows, LANES))
    for first in range(0, len(windows), shared):
        strip, at = None, 0
        for value in joined[first : first + shared]:
            for row in range(0, across, rows):
                part = turned(value[:, row : row + rows], at + 2 * halo)
                strip = part if strip is None else jnp.where(lane < at, strip, part)
                at += 2 * halo
        pieces.append(strip)
    return jnp.concatenate([piece.reshape(-1, LANES) for piece in pieces], axis=0)


def unpack(value, fields, across, halo, own):
    shared, rows = strip_plan(across, fields, halo)
    tall = across * own // LANES
    count = fields * CH * tall
    owned = value[:count].reshape(fields, CH, tall, LANES)
    strips = value[count:].reshape(fields // shared, CH, rows, LANES)
    lane = lanes_of((CH, rows, LANES))
    windows = []
    for field in range(fields):
        window = unpack_own(owned[field], own)
        strip = strips[field // shared]
        at = (field % shared) * across // rows * 2 * halo
        blocks = []
        for row in range(0, across, rows):
            right = turned(strip, own - at)
            left = turned(strip, -2 * halo - at)
            block = jnp.where(lane < own + halo, right, 0.0)
            block = jnp.where(lane >= LANES - halo, left, block)
            blocks.append(jnp.where(lane < own, window[:, row : row + rows], block))
            at += 2 * halo
        windows.append(jnp.concatenate(blocks, axis=1))
    return windows


def halves(value):
    high = value.astype(jnp.bfloat16)
    low = (value - high.astype(jnp.float32)).astype(jnp.bfloat16)
    return high, low


def short_iota(shape):
    return lax.broadcasted_iota(jnp.int32, shape, 0).astype(jnp.int16)


def row_of(cell_ref, span, across):
    return cell_ref[1:2, span] * across + cell_ref[0:1, span] * CA + cell_ref[2:3, span]


def one_hot(rows, index):
    one, zero = jnp.bfloat16(1), jnp.bfloat16(0)
    return jnp.where(rows == index.astype(jnp.int16), one, zero)


def mass_of(count_ref, volume_ref, first, span):
    volume = volume_ref[0:1, span]
    slot = lax.broadcasted_iota(jnp.int32, volume.shape, 1) + first
    return jnp.where(slot < count_ref[0], volume, 0.0)


def deposit_kernel(quads, chunk, place_ref, count_ref, *refs):
    sources, outs = refs[:4], refs[4:6]
    cell_ref, weight_ref, volume_ref, velocity_ref, sems = refs[6:]
    copies = [
        pltpu.make_async_copy(source, target, sems.at[index])
        for index, (source, target) in enumerate(
            zip(sources, (cell_ref, weight_ref, volume_ref, velocity_ref))
        )
    ]
    for copy in copies:
        copy.start()
    across = quads * CA
    rows = CH * across
    grains = weight_ref.shape[1]
    own = CB // quads
    row_iota = short_iota((rows, chunk))
    col_iota = short_iota((CB, chunk))
    total = jnp.zeros((4 * CB, rows), jnp.float32)
    for copy in copies:
        copy.wait()
    for first in range(0, grains, chunk):
        span = pl.ds(first, chunk)
        mass = mass_of(count_ref, volume_ref, first, span)
        moment = mass * velocity_ref[0:1, span]
        lower = weight_ref[0:1, span]
        upper = 1.0 - lower
        hot = one_hot(row_iota, row_of(cell_ref, span, across))
        col = cell_ref[3:4, span]
        at_lower = col_iota == col.astype(jnp.int16)
        at_upper = col_iota == (col + 1).astype(jnp.int16)
        parts = []
        for amount in (mass, moment):
            for low, high in zip(halves(amount * lower), halves(amount * upper)):
                parts.append(jnp.where(at_lower, low, jnp.where(at_upper, high, jnp.bfloat16(0))))
        spread = jnp.concatenate(parts, axis=0)
        total = total + lax.dot_general(
            spread, hot, (((1,), (1,)), ((), ())), preferred_element_type=jnp.float32
        )
    lane = lanes_of((CH, across, LANES))
    fields = [
        (total[base : base + CB] + total[base + CB : base + 2 * CB]).T
        for base in range(0, 4 * CB, 2 * CB)
    ]
    for step in range(quads):
        target = place_ref[0] ^ step
        windows = []
        for field in fields:
            moved = pltpu.roll(field, lax.rem(CB - target * own, CB), 1)
            moved = moved.reshape(CH, across, CB)
            near, past = moved[:, :, :LANES], moved[:, :, CB - LANES :]
            windows.append(jnp.where(lane < (LANES + own) // 2, near, past))
        outs[step % 2][step // 2] = pack(windows, reach(0), own)


def coefficient_kernel(quads, place_ref, kept_ref, got_ref, *refs):
    outs, solid_ref = refs[:-1], refs[-1]
    across, own = quads * CA, CB // quads
    total = kept_ref[0] + got_ref[0]
    solid_ref[...] = total[: solid_ref.shape[0] * solid_ref.shape[1]].reshape(solid_ref.shape)
    solid, moment = unpack(total, 2, across, reach(0), own)
    lane = lanes_of(solid.shape)
    column = jnp.where(lane < (LANES + own) // 2, lane, lane - LANES) + place_ref[0] * own
    inside = (column >= 0) & (column < CB)
    voidage = 1.0 / (1.0 + solid)
    scale = 1.0 / (6.0 * voidage + damping)
    offset = jnp.where(inside, source_gain * moment * scale, 0.0)
    gain = jnp.where(inside, voidage * scale, 0.0)
    for distance, out in enumerate(outs):
        out[...] = pack((offset, gain), reach(distance + 1), own)


def sweep_over(sweeps, layers, across, old, new, offset_ref, gain_ref):
    row = lax.broadcasted_iota(jnp.int32, (across, LANES), 0)
    for sweep in range(1, sweeps + 1):
        for layer in range(sweep, layers - sweep):
            centre = old[layer]
            total = old[layer - 1] + old[layer + 1]
            total = total + turned(centre, 1) + turned(centre, -1)
            total = total + jnp.where(row == 0, 0.0, pltpu.roll(centre, 1, 0))
            total = total + jnp.where(row == across - 1, 0.0, pltpu.roll(centre, across - 1, 0))
            new[layer] = offset_ref[layer] + gain_ref[layer] * total
        old, new = new, old
    return old


def slot_of(slab, distance, matching):
    upward = lax.rem(lax.div(slab, distance), 2) ^ matching
    return distance * (1 - 2 * upward)


def swap_plan(depth):
    return [(distance, matching) for distance in range(1, depth + 1) for matching in range(2)]


def relax_kernel(quads, slab_ref, own_ref, *refs):
    *parts, out_ref, offset_ref, gain_ref, even_ref, odd_ref = refs
    across, own = quads * CA, CB // quads
    layers = CH * (1 + len(parts))
    plan = [(DEPTH, own_ref, 1)] + [
        (DEPTH + slot_of(slab_ref[0], distance, matching), part, distance)
        for part, (distance, matching) in zip(parts, swap_plan(DEPTH))
    ]
    for slot, part, distance in plan:
        span = pl.ds(slot * CH, CH)
        offset, gain = unpack(part[...], 2, across, reach(distance), own)
        offset_ref[span] = offset
        even_ref[span] = offset
        gain_ref[span] = gain
    sweeps = min(FIRST, ITERS) - 1
    last = sweep_over(sweeps, layers, across, even_ref, odd_ref, offset_ref, gain_ref)
    if FIRST < ITERS:
        out_ref[...] = pack([last[DEPTH * CH : (DEPTH + 1) * CH]], SUBLANES, own)
    else:
        out_ref[...] = pack_own(last[DEPTH * CH - 1 : (DEPTH + 1) * CH + 1], own)


def finish_kernel(quads, slab_ref, *refs):
    *parts, out_ref, offset_ref, gain_ref, even_ref, odd_ref = refs
    across, own = quads * CA, CB // quads
    slots = [1] + [1 + slot_of(slab_ref[0], *swap) for swap in swap_plan(1)]
    for slot, coef, pressure in zip(slots, parts[:3], parts[3:]):
        span = pl.ds(slot * CH, CH)
        offset_ref[span], gain_ref[span] = unpack(coef[...], 2, across, reach(1), own)
        (even_ref[span],) = unpack(pressure[...], 1, across, SUBLANES, own)
    last = sweep_over(ITERS - FIRST, 3 * CH, across, even_ref, odd_ref, offset_ref, gain_ref)
    out_ref[...] = pack_own(last[CH - 1 : 2 * CH + 1], own)


def halving(quads):
    return [1 << bit for bit in reversed(range(quads.bit_length() - 1))]


def whole_table(quads, place_ref, parts, gathered):
    own = CB // quads
    pieces = LANES // own
    offsets = [0]
    for bit in halving(quads):
        offsets += [offset ^ bit for offset in offsets]
    for half, part in enumerate(parts):
        for index in range(quads // 2):
            gathered[place_ref[0] ^ offsets[half * (quads // 2) + index]] = part[index]
    lane = lanes_of(gathered.shape[1:])
    bands = []
    for piece in range(pieces):
        columns = []
        for first in range(0, quads, pieces):
            block = None
            for near in range(pieces):
                part = turned(gathered[first + near], (near - piece) * own)
                block = part if block is None else jnp.where(lane < near * own, block, part)
            columns.append(block)
        bands.append(jnp.concatenate(columns, axis=2))
    return jnp.concatenate(bands, axis=1)


def blend_of(col_iota, cell_ref, weight_ref, span):
    lower = weight_ref[0:1, span]
    at = cell_ref[3:4, span]
    return jnp.where(col_iota == at, lower, jnp.where(col_iota == at + 1, 1.0 - lower, 0.0))


def sample(pieces, hot, blend, fields):
    twice = jnp.concatenate([hot, hot], axis=0)
    picked = jnp.dot(pieces, twice, preferred_element_type=jnp.float32)
    return [
        jnp.sum(picked[field * CB : (field + 1) * CB] * blend, axis=0, keepdims=True)
        for field in range(fields)
    ]


def factor_kernel(quads, chunk, place_ref, count_ref, cell_ref, weight_ref, volume_ref, *refs):
    *parts, factor_ref, gathered = refs
    across = quads * CA
    rows = CH * across
    solid = whole_table(quads, place_ref, parts, gathered)
    pieces = jnp.concatenate(halves(solid.reshape(rows, CB).T), axis=1)
    row_iota = short_iota((rows, chunk))
    col_iota = lax.broadcasted_iota(jnp.int32, (CB, chunk), 0)
    for first in range(0, weight_ref.shape[1], chunk):
        span = pl.ds(first, chunk)
        mass = mass_of(count_ref, volume_ref, first, span)
        hot = one_hot(row_iota, row_of(cell_ref, span, across))
        blend = blend_of(col_iota, cell_ref, weight_ref, span)
        (sampled,) = sample(pieces, hot, blend, 1)
        factor_ref[0:1, span] = mass * (1.0 + sampled) ** 2


def drag_kernel(quads, chunk, place_ref, cell_ref, weight_ref, velocity_ref, factor_ref, *refs):
    *parts, pressure_ref, drag_ref, gathered = refs
    across = quads * CA
    rows = CH * across
    pressure = whole_table(quads, place_ref, parts, gathered)
    centre = pressure[1 : CH + 1]
    shape = centre.shape
    row = lax.broadcasted_iota(jnp.int32, shape, 1)
    col = lax.broadcasted_iota(jnp.int32, shape, 2)
    after = jnp.where(row == across - 1, 0.0, pltpu.roll(centre, across - 1, 1))
    before = jnp.where(row == 0, 0.0, pltpu.roll(centre, 1, 1))
    right = jnp.where(col == CB - 1, 0.0, pltpu.roll(centre, CB - 1, 2))
    left = jnp.where(col == 0, 0.0, pltpu.roll(centre, 1, 2))
    fields = (
        -0.5 * (pressure[2:] - pressure[:-2]),
        -0.5 * (after - before),
        -0.5 * (right - left),
    )
    pieces = halves(jnp.concatenate([field.reshape(rows, CB).T for field in fields], axis=0))
    pieces = jnp.concatenate(pieces, axis=1)
    whole = pltpu.roll(centre, lax.rem(across - place_ref[0] * CA, across), 1)
    pressure_ref[...] = whole[:, :CA]

    row_iota = short_iota((rows, chunk))
    col_iota = lax.broadcasted_iota(jnp.int32, (CB, chunk), 0)
    for first in range(0, weight_ref.shape[1], chunk):
        span = pl.ds(first, chunk)
        hot = one_hot(row_iota, row_of(cell_ref, span, across))
        blend = blend_of(col_iota, cell_ref, weight_ref, span)
        sampled = sample(pieces, hot, blend, 3)
        for component in range(3):
            one = pl.ds(component, 1)
            drag_ref[one, span] = factor_ref[0:1, span] * (
                sampled[component] - velocity_ref[one, span]
            )


def body(grain_cell, grain_count, grain_weight, grain_volume, grain_velocity):
    quads = lax.axis_size("quad")
    slabs = lax.axis_size("slab")
    grains = grain_weight.shape[0]
    across = quads * CA
    own = CB // quads
    tall = across * own // LANES
    place = lax.axis_index("quad").astype(jnp.int32).reshape(1)
    level = lax.axis_index("slab").astype(jnp.int32).reshape(1)
    weight = grain_weight.reshape(1, grains)
    volume = grain_volume.reshape(1, grains)

    def cells(*shape):
        return jax.ShapeDtypeStruct(shape, jnp.float32)

    def over_quad(step, value):
        pairs = [(index, index ^ step) for index in range(quads)]
        return lax.ppermute(value, "quad", pairs)

    def swapped(distance, matching, value):
        lower = [
            index
            for index in range(slabs - distance)
            if (index // distance) % 2 == matching
        ]
        pairs = [(index, index + distance) for index in lower]
        return lax.ppermute(value, "slab", pairs + [(high, low) for low, high in pairs])

    *early, last = halving(quads)

    def nearly_all(value):
        held = value[None]
        for bit in early:
            held = jnp.concatenate([held, over_quad(bit, held)], axis=0)
        return held

    def pinned(value):
        return pltpu.with_memory_space_constraint(value, pltpu.HBM)

    kept, sent = pl.pallas_call(
        functools.partial(deposit_kernel, quads, min(grains, 2048)),
        out_shape=[cells(quads // 2, packed_rows(across, 2, reach(0), own), LANES)] * 2,
        in_specs=[SMEM, SMEM] + [HBM] * 4,
        out_specs=[VMEM] * 2,
        scratch_shapes=[
            pltpu.VMEM((4, grains), jnp.int32),
            pltpu.VMEM((1, grains), jnp.float32),
            pltpu.VMEM((1, grains), jnp.float32),
            pltpu.VMEM((3, grains), jnp.float32),
            pltpu.SemaphoreType.DMA((4,)),
        ],
        compiler_params=LIMIT,
        name="deposit",
    )(
        place,
        grain_count,
        pinned(grain_cell),
        pinned(weight),
        pinned(volume),
        pinned(grain_velocity),
    )

    bit = 1
    got = over_quad(bit, sent)
    while kept.shape[0] > 1:
        bit *= 2
        total = kept + got
        kept, sent = total[0::2], total[1::2]
        got = over_quad(bit, sent)
    *coefs, solid = pl.pallas_call(
        functools.partial(coefficient_kernel, quads),
        out_shape=[
            cells(packed_rows(across, 2, reach(distance), own), LANES)
            for distance in range(1, DEPTH + 1)
        ]
        + [cells(CH, tall, LANES)],
        in_specs=[SMEM] + [VMEM] * 2,
        out_specs=[VMEM] * (DEPTH + 1),
        compiler_params=LIMIT,
        name="coefficients",
    )(place, kept, got)

    stack = [coefs[0]] + [
        swapped(distance, matching, coefs[distance - 1])
        for distance, matching in swap_plan(DEPTH)
    ]
    solids = nearly_all(solid)
    solids = [solids, over_quad(last, solids)]
    stack, solids = lax.optimization_barrier((stack, solids))
    layers = CH * len(stack)
    two_rounds = FIRST < ITERS
    centre = pl.pallas_call(
        functools.partial(relax_kernel, quads),
        out_shape=cells(packed_rows(across, 1, SUBLANES, own), LANES)
        if two_rounds
        else cells(CH + 2, tall, LANES),
        in_specs=[SMEM] + [VMEM] * len(stack),
        out_specs=VMEM,
        scratch_shapes=[pltpu.VMEM((layers, across, LANES), jnp.float32)] * 4,
        compiler_params=LIMIT,
        name="relax",
    )(level, *stack)
    mine = centre
    if two_rounds:
        pressures = [centre] + [swapped(*swap, centre) for swap in swap_plan(1)]
        mine = pl.pallas_call(
            functools.partial(finish_kernel, quads),
            out_shape=cells(CH + 2, tall, LANES),
            in_specs=[SMEM] + [VMEM] * 6,
            out_specs=VMEM,
            scratch_shapes=[pltpu.VMEM((3 * CH, across, LANES), jnp.float32)] * 4,
            compiler_params=LIMIT,
            name="finish",
        )(level, *stack[:3], *pressures)

    factor = pl.pallas_call(
        functools.partial(factor_kernel, quads, min(grains, 512)),
        out_shape=cells(1, grains),
        in_specs=[SMEM, SMEM] + [VMEM] * 5,
        out_specs=VMEM,
        scratch_shapes=[pltpu.VMEM((quads,) + solid.shape, jnp.float32)],
        compiler_params=LIMIT,
        cost_estimate=pl.CostEstimate(
            flops=4 * CB * CH * across * grains, bytes_accessed=2**20, transcendentals=0
        ),
        name="factor",
    )(place, grain_count, grain_cell, weight, volume, *solids)

    held, factor = lax.optimization_barrier((nearly_all(mine), factor))
    gathered = [held, over_quad(last, held)]
    pressure, drag = pl.pallas_call(
        functools.partial(drag_kernel, quads, min(grains, 256)),
        out_shape=[cells(CH, CA, CB), cells(3, grains)],
        in_specs=[SMEM] + [VMEM] * 6,
        out_specs=[VMEM] * 2,
        scratch_shapes=[pltpu.VMEM((quads,) + mine.shape, jnp.float32)],
        compiler_params=LIMIT,
        name="drag",
    )(place, grain_cell, weight, grain_velocity, factor, *gathered)
    return pressure, drag


def solution(mesh):
    placed = (
        P(None, ("slab", "quad")),
        P(("slab", "quad")),
        P(("slab", "quad")),
        P(("slab", "quad")),
        P(None, ("slab", "quad")),
    )
    return jax.shard_map(
        body,
        mesh=mesh,
        in_specs=placed,
        out_specs=(P("slab", "quad", None), P(None, ("slab", "quad"))),
        check_vma=False,
    )
```

profile of v0, /device:TPU:9, one launch (start us, length us, event | category | flops | bytes accessed | tf_op | source)
XLA Modules:
  0.0 60.8 jit_solution(16442125549221141424)
XLA Ops:
  1.3 6.8 %deposit.1 = (f32[2,384,128]{2,1,0:T(8,128)S(1)}, f32[2,384,128]{2,1,0:T(8,128)S(1)}) custom-call(s32[1]{0:T(128)} %bitcast.place_ref, s32[1]{0:T(128)S(6)} %copy.7.count_ref, s32[4,8192]{1,0:T(4,128)} %cell_ref.3, f32[1,8192]{1,0:T(1,128)} %bitcast.8, f32[1,8192]{1,0:T(1,128)} %bitcast.13, f32[3,8192]{1,0:T(4,128)} %velocity_ref.1), custom_call_target="tpu_custom_call" | custom-call | tf_op jit(solution)/shard_map/deposit/pallas_call | solution.py:401
  8.1 0.7 %collective-permute-start = (f32[2,384,128]{2,1,0:T(8,128)S(1)}, f32[2,384,128]{2,1,0:T(8,128)S(1)}, u32[]{:S(2)}, u32[]{:S(2)}) collective-permute-start(f32[2,384,128]{2,1,0:T(8,128)S(1)} %get-tuple-element.20), channel_id=1, source_target_pairs={{0,1},{1,0},{2,3},{3,2},{4,5},{5,4},{6,7},{7,6},{8,9},{9,8},{10,11... | collective-permute-start | bytes 1179656 | tf_op jit(solution)/shard_map/ppermute | solution.py:379
  8.8 1.3 %collective-permute-done = f32[2,384,128]{2,1,0:T(8,128)S(1)} collective-permute-done((f32[2,384,128]{2,1,0:T(8,128)S(1)}, f32[2,384,128]{2,1,0:T(8,128)S(1)}, u32[]{:S(2)}, u32[]{:S(2)}) %collective-permute-start) | collective-permute-done | bytes 393248 | tf_op jit(solution)/shard_map/ppermute | solution.py:379
  10.3 1.3 %collective-permute-start.1 = (f32[1,384,128]{2,1,0:T(8,128)S(1)}, f32[1,384,128]{2,1,0:T(8,128)S(1)}, u32[]{:S(2)}, u32[]{:S(2)}) collective-permute-start(f32[1,384,128]{2,1,0:T(8,128)S(1)} %get-tuple-element.36), channel_id=1, source_target_pairs={{0,2},{1,3},{2,0},{3,1},{4,6},{5,7},{6,4},{7,5},{8,10},{9,11},{10,... | collective-permute-start | bytes 589832 | tf_op jit(solution)/shard_map/ppermute | solution.py:379
  11.5 4.9 %collective-permute-done.1.got_ref = f32[1,384,128]{2,1,0:T(8,128)S(1)} collective-permute-done((f32[1,384,128]{2,1,0:T(8,128)S(1)}, f32[1,384,128]{2,1,0:T(8,128)S(1)}, u32[]{:S(2)}, u32[]{:S(2)}) %collective-permute-start.1) | collective-permute-done | bytes 196640 | tf_op jit(solution)/shard_map/ppermute | solution.py:379
  16.4 0.7 %coefficients.1 = (f32[384,128]{1,0:T(8,128)S(1)}, f32[320,128]{1,0:T(8,128)S(1)}, f32[288,128]{1,0:T(8,128)S(1)}, f32[4,32,128]{2,1,0:T(8,128)S(1)}) custom-call(s32[1]{0:T(128)} %bitcast.place_ref, f32[1,384,128]{2,1,0:T(8,128)S(1)} %get-tuple-element.37.kept_ref, f32[1,384,128]{2,1,0:T(8,128)S(1)} %collective-permute-done.1.got_ref), custom_call_target="tpu_custom_call" | custom-call | tf_op jit(solution)/shard_map/coefficients/pallas_call | solution.py:431
  17.1 0.7 %collective-permute-start.7 = (f32[288,128]{1,0:T(8,128)S(1)}, f32[288,128]{1,0:T(8,128)S(1)}, u32[]{:S(2)}, u32[]{:S(2)}) collective-permute-start(f32[288,128]{1,0:T(8,128)S(1)} %get-tuple-element.23), channel_id=1, source_target_pairs={{12,24},{16,28},{24,12},{28,16},{13,25},{17,29},{25,13},{29,17},{1... | collective-permute-start | bytes 442376 | tf_op jit(solution)/shard_map/ppermute | solution.py:388
  17.8 1.3 %collective-permute-start.8 = (f32[1,4,32,128]{3,2,1,0:T(8,128)S(1)}, f32[1,4,32,128]{3,2,1,0:T(8,128)S(1)}, u32[]{:S(2)}, u32[]{:S(2)}) collective-permute-start(f32[1,4,32,128]{3,2,1,0:T(8,128)S(1)} %bitcast.11), channel_id=1, source_target_pairs={{0,2},{1,3},{2,0},{3,1},{4,6},{5,7},{6,4},{7,5},{8,10},{9,11},{10,... | collective-permute-start | bytes 196616 | tf_op jit(solution)/shard_map/ppermute | solution.py:379
  19.1 4.1 %collective-permute-start.6 = (f32[288,128]{1,0:T(8,128)S(1)}, f32[288,128]{1,0:T(8,128)S(1)}, u32[]{:S(2)}, u32[]{:S(2)}) collective-permute-start(f32[288,128]{1,0:T(8,128)S(1)} %get-tuple-element.23), channel_id=1, source_target_pairs={{0,12},{4,16},{8,20},{12,0},{16,4},{20,8},{1,13},{5,17},{9,21},{13... | collective-permute-start | bytes 442376 | tf_op jit(solution)/shard_map/ppermute | solution.py:388
  23.3 4.5 %collective-permute-start.5 = (f32[320,128]{1,0:T(8,128)S(1)}, f32[320,128]{1,0:T(8,128)S(1)}, u32[]{:S(2)}, u32[]{:S(2)}) collective-permute-start(f32[320,128]{1,0:T(8,128)S(1)} %get-tuple-element.22), channel_id=1, source_target_pairs={{8,16},{12,20},{16,8},{20,12},{9,17},{13,21},{17,9},{21,13},{10,18... | collective-permute-start | bytes 491528 | tf_op jit(solution)/shard_map/ppermute | solution.py:388
  27.7 0.1 collective-permute-start.4
  27.8 0.0 collective-permute-done.8
  27.8 3.2 %collective-permute-start.3 = (f32[384,128]{1,0:T(8,128)S(1)}, f32[384,128]{1,0:T(8,128)S(1)}, u32[]{:S(2)}, u32[]{:S(2)}) collective-permute-start(f32[384,128]{1,0:T(8,128)S(1)} %get-tuple-element.25.own_ref), channel_id=1, source_target_pairs={{4,8},{12,16},{20,24},{8,4},{16,12},{24,20},{5,9},{13,17},{21,25},... | collective-permute-start | bytes 589832 | tf_op jit(solution)/shard_map/ppermute | solution.py:388
  31.0 0.0 collective-permute-done.7.refs_5_
  31.0 0.2 collective-permute-start.2
  31.2 0.0 collective-permute-done.6.refs_4_
  31.2 2.6 %collective-permute-start.9 = (f32[2,4,32,128]{3,2,1,0:T(8,128)S(1)}, f32[2,4,32,128]{3,2,1,0:T(8,128)S(1)}, u32[]{:S(2)}, u32[]{:S(2)}) collective-permute-start(f32[2,4,32,128]{3,2,1,0:T(8,128)S(1)} %pad_maximum_fusion.1.refs_0_), channel_id=1, source_target_pairs={{0,1},{1,0},{2,3},{3,2},{4,5},{5,4},{6,7},{7,6},{8,9},{9,8},{10,11... | collective-permute-start | bytes 393224 | tf_op jit(solution)/shard_map/ppermute | solution.py:379
  33.8 0.0 collective-permute-done.5.refs_3_
  33.8 0.2 collective-permute-done.4.refs_2_
  34.0 0.8 %collective-permute-done.9.refs_1_ = f32[2,4,32,128]{3,2,1,0:T(8,128)S(1)} collective-permute-done((f32[2,4,32,128]{3,2,1,0:T(8,128)S(1)}, f32[2,4,32,128]{3,2,1,0:T(8,128)S(1)}, u32[]{:S(2)}, u32[]{:S(2)}) %collective-permute-start.9) | collective-permute-done | bytes 131104 | tf_op jit(solution)/shard_map/ppermute | solution.py:379
  34.8 2.7 %collective-permute-done.3.refs_1_ = f32[384,128]{1,0:T(8,128)S(1)} collective-permute-done((f32[384,128]{1,0:T(8,128)S(1)}, f32[384,128]{1,0:T(8,128)S(1)}, u32[]{:S(2)}, u32[]{:S(2)}) %collective-permute-start.3) | collective-permute-done | bytes 196640 | tf_op jit(solution)/shard_map/ppermute | solution.py:388
  37.5 3.2 %collective-permute-done.2.refs_0_ = f32[384,128]{1,0:T(8,128)S(1)} collective-permute-done((f32[384,128]{1,0:T(8,128)S(1)}, f32[384,128]{1,0:T(8,128)S(1)}, u32[]{:S(2)}, u32[]{:S(2)}) %collective-permute-start.2) | collective-permute-done | bytes 196640 | tf_op jit(solution)/shard_map/ppermute | solution.py:388
  40.6 0.0 copy-start
  40.6 0.0 copy-start.2
  40.7 0.0 copy-start.3
  40.7 4.2 %relax.1 = f32[6,32,128]{2,1,0:T(8,128)S(1)} custom-call(s32[1]{0:T(128)} %bitcast.2.slab_ref, f32[384,128]{1,0:T(8,128)S(1)} %get-tuple-element.25.own_ref, f32[384,128]{1,0:T(8,128)S(1)} %collective-permute-done.2.refs_0_, f32[384,128]{1,0:T(8,128)S(1)} %collective-permute-done.3.refs_1_, f32[320,128]{1,0:T(8,128)S(1)} %collective-permute-done.4.refs_2_, ...), custom_call_target="tpu_custom_call" | custom-call | tf_op jit(solution)/shard_map/relax/pallas_call | solution.py:453
  44.9 0.3 collective-permute-start.10
  45.2 0.0 copy-done
  45.2 0.0 copy-done.2
  45.2 0.0 copy-done.3
  45.2 3.1 %factor.1.factor_ref = f32[1,8192]{1,0:T(1,128)S(1)} custom-call(s32[1]{0:T(128)} %bitcast.place_ref, s32[1]{0:T(128)S(6)} %copy.7.count_ref, s32[4,8192]{1,0:T(4,128)S(1)} %copy-done, f32[1,8192]{1,0:T(1,128)S(1)} %bitcast.9, f32[1,8192]{1,0:T(1,128)S(1)} %bitcast.14, f32[2,4,32,128]{3,2,1,0:T(8,128)S(1)} %pad_maximum_fusion.1.refs_0_, ...), custom_call_target="tpu_custom_call" | custom-call | flops 2147483648 | bytes 1048576 | tf_op jit(solution)/shard_map/factor/pallas_call | solution.py:477
  48.3 0.0 copy-start.1
  48.3 0.1 collective-permute-done.10
  48.4 3.1 %collective-permute-start.11 = (f32[2,6,32,128]{3,2,1,0:T(8,128)S(1)}, f32[2,6,32,128]{3,2,1,0:T(8,128)S(1)}, u32[]{:S(2)}, u32[]{:S(2)}) collective-permute-start(f32[2,6,32,128]{3,2,1,0:T(8,128)S(1)} %pad_maximum_fusion.refs_0_), channel_id=1, source_target_pairs={{0,1},{1,0},{2,3},{3,2},{4,5},{5,4},{6,7},{7,6},{8,9},{9,8},{10,11... | collective-permute-start | bytes 589832 | tf_op jit(solution)/shard_map/ppermute | solution.py:379
  51.5 1.1 %collective-permute-done.11.refs_1_ = f32[2,6,32,128]{3,2,1,0:T(8,128)S(1)} collective-permute-done((f32[2,6,32,128]{3,2,1,0:T(8,128)S(1)}, f32[2,6,32,128]{3,2,1,0:T(8,128)S(1)}, u32[]{:S(2)}, u32[]{:S(2)}) %collective-permute-start.11) | collective-permute-done | bytes 196640 | tf_op jit(solution)/shard_map/ppermute | solution.py:379
  52.6 0.0 copy-done.1
  52.6 8.2 %drag.1 = (f32[4,16,256]{2,1,0:T(8,128)}, f32[3,8192]{1,0:T(4,128)}) custom-call(s32[1]{0:T(128)} %bitcast.place_ref, s32[4,8192]{1,0:T(4,128)S(1)} %copy-done, f32[1,8192]{1,0:T(1,128)S(1)} %bitcast.10, f32[3,8192]{1,0:T(4,128)S(1)} %copy-done.1, f32[1,8192]{1,0:T(1,128)S(1)} %factor.1.factor_ref, f32[2,6,32,128]{3,2,1,0:T(8,128)S(1)} %pad_maximum_fusion.refs_0_, ...), custom_call_target="tpu_custom_call" | custom-call | tf_op jit(solution)/shard_map/drag/pallas_call | solution.py:492
  (4 shorter events, 0.1 us)
Async XLA Ops:
  8.1 2.1 %collective-permute-start = (f32[2,384,128]{2,1,0:T(8,128)S(1)}, f32[2,384,128]{2,1,0:T(8,128)S(1)}, u32[]{:S(2)}, u32[]{:S(2)}) collective-permute-start(f32[2,384,128]{2,1,0:T(8,128)S(1)} %get-tuple-element.20), channel_id=1, source_target_pairs={{0,1},{1,0},{2,3},{3,2},{4,5},{5,4},{6,7},{7,6},{8,9},{9,8},{10,11... | collective-permute-start | bytes 1179656 | tf_op jit(solution)/shard_map/ppermute | solution.py:379
  10.3 6.2 %collective-permute-start.1 = (f32[1,384,128]{2,1,0:T(8,128)S(1)}, f32[1,384,128]{2,1,0:T(8,128)S(1)}, u32[]{:S(2)}, u32[]{:S(2)}) collective-permute-start(f32[1,384,128]{2,1,0:T(8,128)S(1)} %get-tuple-element.36), channel_id=1, source_target_pairs={{0,2},{1,3},{2,0},{3,1},{4,6},{5,7},{6,4},{7,5},{8,10},{9,11},{10,... | collective-permute-start | bytes 589832 | tf_op jit(solution)/shard_map/ppermute | solution.py:379
  17.1 13.9 %collective-permute-start.7 = (f32[288,128]{1,0:T(8,128)S(1)}, f32[288,128]{1,0:T(8,128)S(1)}, u32[]{:S(2)}, u32[]{:S(2)}) collective-permute-start(f32[288,128]{1,0:T(8,128)S(1)} %get-tuple-element.23), channel_id=1, source_target_pairs={{12,24},{16,28},{24,12},{28,16},{13,25},{17,29},{25,13},{29,17},{1... | collective-permute-start | bytes 442376 | tf_op jit(solution)/shard_map/ppermute | solution.py:388
  17.8 10.0 %collective-permute-start.8 = (f32[1,4,32,128]{3,2,1,0:T(8,128)S(1)}, f32[1,4,32,128]{3,2,1,0:T(8,128)S(1)}, u32[]{:S(2)}, u32[]{:S(2)}) collective-permute-start(f32[1,4,32,128]{3,2,1,0:T(8,128)S(1)} %bitcast.11), channel_id=1, source_target_pairs={{0,2},{1,3},{2,0},{3,1},{4,6},{5,7},{6,4},{7,5},{8,10},{9,11},{10,... | collective-permute-start | bytes 196616 | tf_op jit(solution)/shard_map/ppermute | solution.py:379
  19.1 12.1 %collective-permute-start.6 = (f32[288,128]{1,0:T(8,128)S(1)}, f32[288,128]{1,0:T(8,128)S(1)}, u32[]{:S(2)}, u32[]{:S(2)}) collective-permute-start(f32[288,128]{1,0:T(8,128)S(1)} %get-tuple-element.23), channel_id=1, source_target_pairs={{0,12},{4,16},{8,20},{12,0},{16,4},{20,8},{1,13},{5,17},{9,21},{13... | collective-permute-start | bytes 442376 | tf_op jit(solution)/shard_map/ppermute | solution.py:388
  23.3 10.5 %collective-permute-start.5 = (f32[320,128]{1,0:T(8,128)S(1)}, f32[320,128]{1,0:T(8,128)S(1)}, u32[]{:S(2)}, u32[]{:S(2)}) collective-permute-start(f32[320,128]{1,0:T(8,128)S(1)} %get-tuple-element.22), channel_id=1, source_target_pairs={{8,16},{12,20},{16,8},{20,12},{9,17},{13,21},{17,9},{21,13},{10,18... | collective-permute-start | bytes 491528 | tf_op jit(solution)/shard_map/ppermute | solution.py:388
  27.7 6.3 %collective-permute-start.4 = (f32[320,128]{1,0:T(8,128)S(1)}, f32[320,128]{1,0:T(8,128)S(1)}, u32[]{:S(2)}, u32[]{:S(2)}) collective-permute-start(f32[320,128]{1,0:T(8,128)S(1)} %get-tuple-element.22), channel_id=1, source_target_pairs={{0,8},{4,12},{16,24},{20,28},{8,0},{12,4},{24,16},{28,20},{1,9},{5... | collective-permute-start | bytes 491528 | tf_op jit(solution)/shard_map/ppermute | solution.py:388
  27.8 9.7 %collective-permute-start.3 = (f32[384,128]{1,0:T(8,128)S(1)}, f32[384,128]{1,0:T(8,128)S(1)}, u32[]{:S(2)}, u32[]{:S(2)}) collective-permute-start(f32[384,128]{1,0:T(8,128)S(1)} %get-tuple-element.25.own_ref), channel_id=1, source_target_pairs={{4,8},{12,16},{20,24},{8,4},{16,12},{24,20},{5,9},{13,17},{21,25},... | collective-permute-start | bytes 589832 | tf_op jit(solution)/shard_map/ppermute | solution.py:388
  31.0 9.6 %collective-permute-start.2 = (f32[384,128]{1,0:T(8,128)S(1)}, f32[384,128]{1,0:T(8,128)S(1)}, u32[]{:S(2)}, u32[]{:S(2)}) collective-permute-start(f32[384,128]{1,0:T(8,128)S(1)} %get-tuple-element.25.own_ref), channel_id=1, source_target_pairs={{0,4},{8,12},{16,20},{24,28},{4,0},{12,8},{20,16},{28,24},{1,5},{9... | collective-permute-start | bytes 589832 | tf_op jit(solution)/shard_map/ppermute | solution.py:388
  31.2 3.6 %collective-permute-start.9 = (f32[2,4,32,128]{3,2,1,0:T(8,128)S(1)}, f32[2,4,32,128]{3,2,1,0:T(8,128)S(1)}, u32[]{:S(2)}, u32[]{:S(2)}) collective-permute-start(f32[2,4,32,128]{3,2,1,0:T(8,128)S(1)} %pad_maximum_fusion.1.refs_0_), channel_id=1, source_target_pairs={{0,1},{1,0},{2,3},{3,2},{4,5},{5,4},{6,7},{7,6},{8,9},{9,8},{10,11... | collective-permute-start | bytes 393224 | tf_op jit(solution)/shard_map/ppermute | solution.py:379
  40.6 4.5 %copy-start = (s32[4,8192]{1,0:T(4,128)S(1)}, s32[4,8192]{1,0:T(4,128)}, u32[]{:S(2)}) copy-start(s32[4,8192]{1,0:T(4,128)} %cell_ref.3) | copy-start | bytes 393220
  40.6 4.5 %copy-start.2 = (f32[8192]{0:T(1024)S(1)}, f32[8192]{0:T(1024)}, u32[]{:S(2)}) copy-start(f32[8192]{0:T(1024)} %param.7) | copy-start | bytes 98308
  40.7 4.5 %copy-start.3 = (f32[8192]{0:T(1024)S(1)}, f32[8192]{0:T(1024)}, u32[]{:S(2)}) copy-start(f32[8192]{0:T(1024)} %param.8) | copy-start | bytes 98308
  44.9 3.5 %collective-permute-start.10 = (f32[1,6,32,128]{3,2,1,0:T(8,128)S(1)}, f32[1,6,32,128]{3,2,1,0:T(8,128)S(1)}, u32[]{:S(2)}, u32[]{:S(2)}) collective-permute-start(f32[1,6,32,128]{3,2,1,0:T(8,128)S(1)} %bitcast.6), channel_id=1, source_target_pairs={{0,2},{1,3},{2,0},{3,1},{4,6},{5,7},{6,4},{7,5},{8,10},{9,11},{10,... | collective-permute-start | bytes 294920 | tf_op jit(solution)/shard_map/ppermute | solution.py:379
  48.3 4.3 %copy-start.1 = (f32[3,8192]{1,0:T(4,128)S(1)}, f32[3,8192]{1,0:T(4,128)}, u32[]{:S(2)}) copy-start(f32[3,8192]{1,0:T(4,128)} %velocity_ref.1) | copy-start | bytes 294916
  48.4 4.1 %collective-permute-start.11 = (f32[2,6,32,128]{3,2,1,0:T(8,128)S(1)}, f32[2,6,32,128]{3,2,1,0:T(8,128)S(1)}, u32[]{:S(2)}, u32[]{:S(2)}) collective-permute-start(f32[2,6,32,128]{3,2,1,0:T(8,128)S(1)} %pad_maximum_fusion.refs_0_), channel_id=1, source_target_pairs={{0,1},{1,0},{2,3},{3,2},{4,5},{5,4},{6,7},{7,6},{8,9},{9,8},{10,11... | collective-permute-start | bytes 589832 | tf_op jit(solution)/shard_map/ppermute | solution.py:379
where the time goes:
time: 61.5 us; the launch traced here: 60.8 us
  Pallas kernels  23.1 us (38%)
  starting transfers between devices  21.9 us (36%)
  waiting for transfers between devices  14.3 us (23%)
  between operations  1.41 us (2%)
    ppermute x6, starting transfers between devices, swapped(): lax.ppermute(value, 'slab', pairs + [(high, low) for low, high in pairs])  12.7 us
    ppermute x6, starting transfers between devices, over_quad(): return lax.ppermute(value, 'quad', pairs)  9.25 us
    pallas_call x1, Pallas kernels, body(): pl.pallas_call(functools.partial(drag_kernel, quads, min(grains, 256)), o...  8.25 us
    ppermute x6, waiting for transfers between devices, over_quad(): return lax.ppermute(value, 'quad', pairs)  8.16 us
    pallas_call x1, Pallas kernels, body(): pl.pallas_call(functools.partial(deposit_kernel, quads, min(grains, 2048)...  6.8 us
    ppermute x6, waiting for transfers between devices, swapped(): lax.ppermute(value, 'slab', pairs + [(high, low) for low, high in pairs])  6.13 us
    pallas_call x1, Pallas kernels, body(): pl.pallas_call(functools.partial(relax_kernel, quads), out_shape=cells(pa...  4.21 us
    pallas_call x1, Pallas kernels, body(): pl.pallas_call(functools.partial(factor_kernel, quads, min(grains, 512)),...  3.11 us
  transfers between devices with their start and end apart: 12, of which 8 were waited for; matrix products, arithmetic and copies ran while one was open for 0% of the time, Pallas kernels for 5%

commit v1 on v0

--- a/solution.py
+++ b/solution.py
@@ -13,7 +13,7 @@
 ITERS = 12
 LANES = 128
 SUBLANES = 8
-DEPTH = 3
+DEPTH = 2
 FIRST = CH * DEPTH + 1
 
 damping = 0.05
@@ -229,6 +229,12 @@
     return [(distance, matching) for distance in range(1, depth + 1) for matching in range(2)]
 
 
+def framed(last, first, own):
+    inner = pack([last[first : first + CH]], SUBLANES, own)
+    outer = [pack_own(last[layer : layer + 1], own)[0] for layer in (first - 1, first + CH)]
+    return jnp.concatenate([inner] + outer, axis=0)
+
+
 def relax_kernel(quads, slab_ref, own_ref, *refs):
     *parts, out_ref, offset_ref, gain_ref, even_ref, odd_ref = refs
     across, own = quads * CA, CB // quads
@@ -248,7 +254,7 @@
     if FIRST < ITERS:
         out_ref[...] = pack([last[DEPTH * CH : (DEPTH + 1) * CH]], SUBLANES, own)
     else:
-        out_ref[...] = pack_own(last[DEPTH * CH - 1 : (DEPTH + 1) * CH + 1], own)
+        out_ref[...] = framed(last, DEPTH * CH, own)
 
 
 def finish_kernel(quads, slab_ref, *refs):
@@ -260,22 +266,25 @@
         offset_ref[span], gain_ref[span] = unpack(coef[...], 2, across, reach(1), own)
         (even_ref[span],) = unpack(pressure[...], 1, across, SUBLANES, own)
     last = sweep_over(ITERS - FIRST, 3 * CH, across, even_ref, odd_ref, offset_ref, gain_ref)
-    out_ref[...] = pack_own(last[CH - 1 : 2 * CH + 1], own)
+    out_ref[...] = framed(last, CH, own)
 
 
 def halving(quads):
     return [1 << bit for bit in reversed(range(quads.bit_length() - 1))]
+
+
+def place_offsets(quads):
+    offsets = [0]
+    for bit in halving(quads):
+        offsets += [offset ^ bit for offset in offsets]
+    return offsets
 
 
 def whole_table(quads, place_ref, parts, gathered):
     own = CB // quads
     pieces = LANES // own
-    offsets = [0]
-    for bit in halving(quads):
-        offsets += [offset ^ bit for offset in offsets]
-    for half, part in enumerate(parts):
-        for index in range(quads // 2):
-            gathered[place_ref[0] ^ offsets[half * (quads // 2) + index]] = part[index]
+    for offset, part in zip(place_offsets(quads), parts):
+        gathered[place_ref[0] ^ offset] = part
     lane = lanes_of(gathered.shape[1:])
     bands = []
     for piece in range(pieces):
@@ -290,25 +299,25 @@
     return jnp.concatenate(bands, axis=1)
 
 
-def blend_of(col_iota, cell_ref, weight_ref, span):
-    lower = weight_ref[0:1, span]
-    at = cell_ref[3:4, span]
+def blend_of(col_iota, at, lower):
     return jnp.where(col_iota == at, lower, jnp.where(col_iota == at + 1, 1.0 - lower, 0.0))
 
 
-def sample(pieces, hot, blend, fields):
+def picked_by(pieces, hot):
     twice = jnp.concatenate([hot, hot], axis=0)
-    picked = jnp.dot(pieces, twice, preferred_element_type=jnp.float32)
-    return [
-        jnp.sum(picked[field * CB : (field + 1) * CB] * blend, axis=0, keepdims=True)
-        for field in range(fields)
-    ]
+    return jnp.dot(pieces, twice, preferred_element_type=jnp.float32)
+
+
+def blended(picked, blend, field):
+    size = blend.shape[0]
+    return jnp.sum(picked[field * size : (field + 1) * size] * blend, axis=0, keepdims=True)
 
 
 def factor_kernel(quads, chunk, place_ref, count_ref, cell_ref, weight_ref, volume_ref, *refs):
-    *parts, factor_ref, gathered = refs
+    *halfs, factor_ref, gathered = refs
     across = quads * CA
     rows = CH * across
+    parts = [half[index] for half in halfs for index in range(quads // 2)]
     solid = whole_table(quads, place_ref, parts, gathered)
     pieces = jnp.concatenate(halves(solid.reshape(rows, CB).T), axis=1)
     row_iota = short_iota((rows, chunk))
@@ -317,46 +326,88 @@
         span = pl.ds(first, chunk)
         mass = mass_of(count_ref, volume_ref, first, span)
         hot = one_hot(row_iota, row_of(cell_ref, span, across))
-        blend = blend_of(col_iota, cell_ref, weight_ref, span)
-        (sampled,) = sample(pieces, hot, blend, 1)
+        blend = blend_of(col_iota, cell_ref[3:4, span], weight_ref[0:1, span])
+        sampled = blended(picked_by(pieces, hot), blend, 0)
         factor_ref[0:1, span] = mass * (1.0 + sampled) ** 2
 
 
-def drag_kernel(quads, chunk, place_ref, cell_ref, weight_ref, velocity_ref, factor_ref, *refs):
-    *parts, pressure_ref, drag_ref, gathered = refs
-    across = quads * CA
-    rows = CH * across
-    pressure = whole_table(quads, place_ref, parts, gathered)
-    centre = pressure[1 : CH + 1]
-    shape = centre.shape
-    row = lax.broadcasted_iota(jnp.int32, shape, 1)
-    col = lax.broadcasted_iota(jnp.int32, shape, 2)
-    after = jnp.where(row == across - 1, 0.0, pltpu.roll(centre, across - 1, 1))
-    before = jnp.where(row == 0, 0.0, pltpu.roll(centre, 1, 1))
-    right = jnp.where(col == CB - 1, 0.0, pltpu.roll(centre, CB - 1, 2))
-    left = jnp.where(col == 0, 0.0, pltpu.roll(centre, 1, 2))
+def velocity_table(value, across, own):
+    tall = across * own // LANES
+    count = packed_rows(across, 1, SUBLANES, own)
+    (inner,) = unpack(value[:count], 1, across, SUBLANES, own)
+    outer = unpack_own(value[count:].reshape(2, tall, LANES), own)
+    row = lax.broadcasted_iota(jnp.int32, inner.shape, 1)
+    above = jnp.concatenate([inner[1:], outer[1:]], axis=0)
+    below = jnp.concatenate([outer[:1], inner[:-1]], axis=0)
+    after = jnp.where(row == across - 1, 0.0, pltpu.roll(inner, across - 1, 1))
+    before = jnp.where(row == 0, 0.0, pltpu.roll(inner, 1, 1))
     fields = (
-        -0.5 * (pressure[2:] - pressure[:-2]),
+        -0.5 * (above - below),
         -0.5 * (after - before),
-        -0.5 * (right - left),
+        -0.5 * (turned(inner, -1) - turned(inner, 1)),
     )
-    pieces = halves(jnp.concatenate([field.reshape(rows, CB).T for field in fields], axis=0))
-    pieces = jnp.concatenate(pieces, axis=1)
-    whole = pltpu.roll(centre, lax.rem(across - place_ref[0] * CA, across), 1)
-    pressure_ref[...] = whole[:, :CA]
-
-    row_iota = short_iota((rows, chunk))
-    col_iota = lax.broadcasted_iota(jnp.int32, (CB, chunk), 0)
+    columns = [field.reshape(CH * across, LANES).T[:own] for field in fields]
+    return jnp.concatenate(halves(jnp.concatenate(columns, axis=0)), axis=1)
+
+
+def velocity_chunk(quads, place_ref, tables, offsets, cell_ref, weight_ref, row_iota, span):
+    across, own = quads * CA, CB // quads
+    hot = one_hot(row_iota, row_of(cell_ref, span, across))
+    lower = weight_ref[0:1, span]
+    picked = picked_by(tables, hot)
+    col_iota = lax.broadcasted_iota(jnp.int32, (own, picked.shape[1]), 0)
+    sums = [0.0] * 3
+    for index, offset in enumerate(offsets):
+        at = cell_ref[3:4, span] - (place_ref[0] ^ offset) * own
+        blend = blend_of(col_iota, at, lower)
+        for component in range(3):
+            sums[component] += blended(picked, blend, 3 * index + component)
+    return sums
+
+
+def sampled_kernel(quads, chunk, offset, index, place_ref, cell_ref, weight_ref, held_ref, *refs):
+    *earlier, out_ref = refs
+    across, own = quads * CA, CB // quads
+    table = velocity_table(held_ref[index], across, own)
+    row_iota = short_iota((CH * across, chunk))
     for first in range(0, weight_ref.shape[1], chunk):
         span = pl.ds(first, chunk)
-        hot = one_hot(row_iota, row_of(cell_ref, span, across))
-        blend = blend_of(col_iota, cell_ref, weight_ref, span)
-        sampled = sample(pieces, hot, blend, 3)
-        for component in range(3):
+        sums = velocity_chunk(
+            quads, place_ref, table, [offset], cell_ref, weight_ref, row_iota, span
+        )
+        for component, value in enumerate(sums):
+            one = pl.ds(component, 1)
+            for partial in earlier:
+                value = value + partial[one, span]
+            out_ref[one, span] = value
+
+
+def drag_kernel(quads, chunk, place_ref, cell_ref, weight_ref, velocity_ref, factor_ref, *refs):
+    sampled_ref, held_ref, got_ref, pressure_ref, drag_ref, gathered = refs
+    across, own = quads * CA, CB // quads
+    half = quads // 2
+    offsets = place_offsets(quads)[half:]
+    tables = [velocity_table(got_ref[index], across, own) for index in range(half)]
+    tables = jnp.concatenate(tables, axis=0)
+    row_iota = short_iota((CH * across, chunk))
+    for first in range(0, weight_ref.shape[1], chunk):
+        span = pl.ds(first, chunk)
+        sums = velocity_chunk(
+            quads, place_ref, tables, offsets, cell_ref, weight_ref, row_iota, span
+        )
+        for component, value in enumerate(sums):
             one = pl.ds(component, 1)
             drag_ref[one, span] = factor_ref[0:1, span] * (
-                sampled[component] - velocity_ref[one, span]
+                value + sampled_ref[one, span] - velocity_ref[one, span]
             )
+    shape = gathered.shape[1:]
+    count = CH * shape[1]
+    parts = [
+        ref[index][:count].reshape(shape) for ref in (held_ref, got_ref) for index in range(half)
+    ]
+    pressure = whole_table(quads, place_ref, parts, gathered)
+    mine = pltpu.roll(pressure, lax.rem(across - place_ref[0] * CA, across), 1)
+    pressure_ref[...] = mine[:, :CA]
 
 
 def body(grain_cell, grain_count, grain_weight, grain_volume, grain_velocity):
@@ -448,32 +499,6 @@
     solids = nearly_all(solid)
     solids = [solids, over_quad(last, solids)]
     stack, solids = lax.optimization_barrier((stack, solids))
-    layers = CH * len(stack)
-    two_rounds = FIRST < ITERS
-    centre = pl.pallas_call(
-        functools.partial(relax_kernel, quads),
-        out_shape=cells(packed_rows(across, 1, SUBLANES, own), LANES)
-        if two_rounds
-        else cells(CH + 2, tall, LANES),
-        in_specs=[SMEM] + [VMEM] * len(stack),
-        out_specs=VMEM,
-        scratch_shapes=[pltpu.VMEM((layers, across, LANES), jnp.float32)] * 4,
-        compiler_params=LIMIT,
-        name="relax",
-    )(level, *stack)
-    mine = centre
-    if two_rounds:
-        pressures = [centre] + [swapped(*swap, centre) for swap in swap_plan(1)]
-        mine = pl.pallas_call(
-            functools.partial(finish_kernel, quads),
-            out_shape=cells(CH + 2, tall, LANES),
-            in_specs=[SMEM] + [VMEM] * 6,
-            out_specs=VMEM,
-            scratch_shapes=[pltpu.VMEM((3 * CH, across, LANES), jnp.float32)] * 4,
-            compiler_params=LIMIT,
-            name="finish",
-        )(level, *stack[:3], *pressures)
-
     factor = pl.pallas_call(
         functools.partial(factor_kernel, quads, min(grains, 512)),
         out_shape=cells(1, grains),
@@ -487,17 +512,69 @@
         name="factor",
     )(place, grain_count, grain_cell, weight, volume, *solids)
 
-    held, factor = lax.optimization_barrier((nearly_all(mine), factor))
-    gathered = [held, over_quad(last, held)]
+    frame = cells(packed_rows(across, 1, SUBLANES, own) + 2 * tall, LANES)
+    layers = CH * len(stack)
+    two_rounds = FIRST < ITERS
+    centre = pl.pallas_call(
+        functools.partial(relax_kernel, quads),
+        out_shape=cells(packed_rows(across, 1, SUBLANES, own), LANES)
+        if two_rounds
+        else frame,
+        in_specs=[SMEM] + [VMEM] * len(stack),
+        out_specs=VMEM,
+        scratch_shapes=[pltpu.VMEM((layers, across, LANES), jnp.float32)] * 4,
+        compiler_params=LIMIT,
+        name="relax",
+    )(level, *stack)
+    mine = centre
+    if two_rounds:
+        pressures = [centre] + [swapped(*swap, centre) for swap in swap_plan(1)]
+        pressures, factor = lax.optimization_barrier((pressures, factor))
+        mine = pl.pallas_call(
+            functools.partial(finish_kernel, quads),
+            out_shape=frame,
+            in_specs=[SMEM] + [VMEM] * 6,
+            out_specs=VMEM,
+            scratch_shapes=[pltpu.VMEM((3 * CH, across, LANES), jnp.float32)] * 4,
+            compiler_params=LIMIT,
+            name="finish",
+        )(level, *stack[:3], *pressures)
+
+    grain_chunk = min(grains, 512)
+
+    def sampled_from(held, index, *earlier):
+        return pl.pallas_call(
+            functools.partial(
+                sampled_kernel, quads, grain_chunk, place_offsets(quads)[index], index
+            ),
+            out_shape=cells(3, grains),
+            in_specs=[SMEM] + [VMEM] * (3 + len(earlier)),
+            out_specs=VMEM,
+            compiler_params=LIMIT,
+            cost_estimate=pl.CostEstimate(
+                flops=12 * own * CH * across * grains, bytes_accessed=2**20, transcendentals=0
+            ),
+            name="sampled",
+        )(place, grain_cell, weight, held, *earlier)
+
+    held = mine[None]
+    partial = sampled_from(held, 0)
+    for bit in early:
+        known = held.shape[0]
+        held = jnp.concatenate([held, over_quad(bit, held)], axis=0)
+        held, partial = lax.optimization_barrier((held, partial))
+        for index in range(known, held.shape[0]):
+            partial = sampled_from(held, index, partial)
+    got = over_quad(last, held)
     pressure, drag = pl.pallas_call(
-        functools.partial(drag_kernel, quads, min(grains, 256)),
+        functools.partial(drag_kernel, quads, grain_chunk),
         out_shape=[cells(CH, CA, CB), cells(3, grains)],
-        in_specs=[SMEM] + [VMEM] * 6,
+        in_specs=[SMEM] + [VMEM] * 7,
         out_specs=[VMEM] * 2,
-        scratch_shapes=[pltpu.VMEM((quads,) + mine.shape, jnp.float32)],
+        scratch_shapes=[pltpu.VMEM((quads, CH, tall, LANES), jnp.float32)],
         compiler_params=LIMIT,
         name="drag",
-    )(place, grain_cell, weight, grain_velocity, factor, *gathered)
+    )(place, grain_cell, weight, grain_velocity, factor, partial, held, got)
     return pressure, drag
 
 

time: 61.5 us -> 61.4 us (level)
  the two profiles are of different devices: /device:TPU:9 before, /device:TPU:1 now
where the time goes in v1:
time: 61.4 us; the launch traced here: 61.3 us
  Pallas kernels  23.2 us (38%)
  starting transfers between devices  23.1 us (38%)
  waiting for transfers between devices  13.4 us (22%)
  between operations  1.42 us (2%)
    ppermute x6, starting transfers between devices, swapped(): lax.ppermute(value, 'slab', pairs + [(high, low) for low, high in pairs])  13.2 us
    ppermute x6, starting transfers between devices, over_quad(): return lax.ppermute(value, 'quad', pairs)  9.94 us
    ppermute x6, waiting for transfers between devices, over_quad(): return lax.ppermute(value, 'quad', pairs)  8.82 us
    pallas_call x1, Pallas kernels, body(): pl.pallas_call(functools.partial(deposit_kernel, quads, min(grains, 2048)...  6.8 us
    pallas_call x1, Pallas kernels, body(): pl.pallas_call(functools.partial(drag_kernel, quads, grain_chunk), out_sh...  4.88 us
    ppermute x6, waiting for transfers between devices, swapped(): lax.ppermute(value, 'slab', pairs + [(high, low) for low, high in pairs])  4.59 us
    pallas_call x2, Pallas kernels, sampled_from(): pl.pallas_call(functools.partial(sampled_kernel, quads, grain_chunk, plac...  4.38 us
    pallas_call x1, Pallas kernels, body(): pl.pallas_call(functools.partial(factor_kernel, quads, min(grains, 512)),...  3.1 us
  transfers between devices with their start and end apart: 12, of which 5 were waited for; matrix products, arithmetic and copies ran while one was open for 0% of the time, Pallas kernels for 12%

profile of v1, /device:TPU:1, one launch (start us, length us, event | category | flops | bytes accessed | tf_op | source)
XLA Modules:
  0.0 61.3 jit_solution(7806691915805818092)
XLA Ops:
  1.3 6.8 %deposit.1 = (f32[2,384,128]{2,1,0:T(8,128)S(1)}, f32[2,384,128]{2,1,0:T(8,128)S(1)}) custom-call(s32[1]{0:T(128)} %bitcast.place_ref, s32[1]{0:T(128)S(6)} %copy.7.count_ref, s32[4,8192]{1,0:T(4,128)} %cell_ref.7, f32[1,8192]{1,0:T(1,128)} %bitcast.9, f32[1,8192]{1,0:T(1,128)} %bitcast.16, f32[3,8192]{1,0:T(4,128)} %velocity_ref.1), custom_call_target="tpu_custom_call" | custom-call | tf_op jit(solution)/shard_map/deposit/pallas_call | solution.py:452
  8.1 0.1 collective-permute-start
  8.2 1.7 %collective-permute-done = f32[2,384,128]{2,1,0:T(8,128)S(1)} collective-permute-done((f32[2,384,128]{2,1,0:T(8,128)S(1)}, f32[2,384,128]{2,1,0:T(8,128)S(1)}, u32[]{:S(2)}, u32[]{:S(2)}) %collective-permute-start) | collective-permute-done | bytes 393248 | tf_op jit(solution)/shard_map/ppermute | solution.py:430
  10.0 2.4 %collective-permute-start.1 = (f32[1,384,128]{2,1,0:T(8,128)S(1)}, f32[1,384,128]{2,1,0:T(8,128)S(1)}, u32[]{:S(2)}, u32[]{:S(2)}) collective-permute-start(f32[1,384,128]{2,1,0:T(8,128)S(1)} %get-tuple-element.38), channel_id=1, source_target_pairs={{0,2},{1,3},{2,0},{3,1},{4,6},{5,7},{6,4},{7,5},{8,10},{9,11},{10,... | collective-permute-start | bytes 589832 | tf_op jit(solution)/shard_map/ppermute | solution.py:430
  12.4 5.0 %collective-permute-done.1.got_ref = f32[1,384,128]{2,1,0:T(8,128)S(1)} collective-permute-done((f32[1,384,128]{2,1,0:T(8,128)S(1)}, f32[1,384,128]{2,1,0:T(8,128)S(1)}, u32[]{:S(2)}, u32[]{:S(2)}) %collective-permute-start.1) | collective-permute-done | bytes 196640 | tf_op jit(solution)/shard_map/ppermute | solution.py:430
  17.3 0.5 coefficients.1
  17.9 1.2 %collective-permute-start.6 = (f32[1,4,32,128]{3,2,1,0:T(8,128)S(1)}, f32[1,4,32,128]{3,2,1,0:T(8,128)S(1)}, u32[]{:S(2)}, u32[]{:S(2)}) collective-permute-start(f32[1,4,32,128]{3,2,1,0:T(8,128)S(1)} %bitcast.14), channel_id=1, source_target_pairs={{0,2},{1,3},{2,0},{3,1},{4,6},{5,7},{6,4},{7,5},{8,10},{9,11},{10,... | collective-permute-start | bytes 196616 | tf_op jit(solution)/shard_map/ppermute | solution.py:430
  19.1 0.7 %collective-permute-start.5 = (f32[320,128]{1,0:T(8,128)S(1)}, f32[320,128]{1,0:T(8,128)S(1)}, u32[]{:S(2)}, u32[]{:S(2)}) collective-permute-start(f32[320,128]{1,0:T(8,128)S(1)} %get-tuple-element.23), channel_id=1, source_target_pairs={{8,16},{12,20},{16,8},{20,12},{9,17},{13,21},{17,9},{21,13},{10,18... | collective-permute-start | bytes 491528 | tf_op jit(solution)/shard_map/ppermute | solution.py:439
  19.8 3.9 %collective-permute-start.4 = (f32[320,128]{1,0:T(8,128)S(1)}, f32[320,128]{1,0:T(8,128)S(1)}, u32[]{:S(2)}, u32[]{:S(2)}) collective-permute-start(f32[320,128]{1,0:T(8,128)S(1)} %get-tuple-element.23), channel_id=1, source_target_pairs={{0,8},{4,12},{16,24},{20,28},{8,0},{12,4},{24,16},{28,20},{1,9},{5... | collective-permute-start | bytes 491528 | tf_op jit(solution)/shard_map/ppermute | solution.py:439
  23.7 0.7 %collective-permute-start.3 = (f32[384,128]{1,0:T(8,128)S(1)}, f32[384,128]{1,0:T(8,128)S(1)}, u32[]{:S(2)}, u32[]{:S(2)}) collective-permute-start(f32[384,128]{1,0:T(8,128)S(1)} %get-tuple-element.25.own_ref.refs_0_), channel_id=1, source_target_pairs={{4,8},{12,16},{20,24},{8,4},{16,12},{24,20},{5,9},{13,17},{21,25},... | collective-permute-start | bytes 589832 | tf_op jit(solution)/shard_map/ppermute | solution.py:439
  24.3 2.5 %collective-permute-start.2 = (f32[384,128]{1,0:T(8,128)S(1)}, f32[384,128]{1,0:T(8,128)S(1)}, u32[]{:S(2)}, u32[]{:S(2)}) collective-permute-start(f32[384,128]{1,0:T(8,128)S(1)} %get-tuple-element.25.own_ref.refs_0_), channel_id=1, source_target_pairs={{0,4},{8,12},{16,20},{24,28},{4,0},{12,8},{20,16},{28,24},{1,5},{9... | collective-permute-start | bytes 589832 | tf_op jit(solution)/shard_map/ppermute | solution.py:439
  26.9 0.0 collective-permute-done.6
  26.9 2.4 %collective-permute-start.7 = (f32[2,4,32,128]{3,2,1,0:T(8,128)S(1)}, f32[2,4,32,128]{3,2,1,0:T(8,128)S(1)}, u32[]{:S(2)}, u32[]{:S(2)}) collective-permute-start(f32[2,4,32,128]{3,2,1,0:T(8,128)S(1)} %pad_maximum_fusion.1.refs_0_), channel_id=1, source_target_pairs={{0,1},{1,0},{2,3},{3,2},{4,5},{5,4},{6,7},{7,6},{8,9},{9,8},{10,11... | collective-permute-start | bytes 393224 | tf_op jit(solution)/shard_map/ppermute | solution.py:430
  29.3 0.0 collective-permute-done.5.refs_3_
  29.3 0.0 collective-permute-done.4.refs_2_
  29.3 1.0 %collective-permute-done.7.refs_1_ = f32[2,4,32,128]{3,2,1,0:T(8,128)S(1)} collective-permute-done((f32[2,4,32,128]{3,2,1,0:T(8,128)S(1)}, f32[2,4,32,128]{3,2,1,0:T(8,128)S(1)}, u32[]{:S(2)}, u32[]{:S(2)}) %collective-permute-start.7) | collective-permute-done | bytes 131104 | tf_op jit(solution)/shard_map/ppermute | solution.py:430
  30.3 0.0 collective-permute-done.3.refs_1_.refs_2_
  30.3 4.6 %collective-permute-done.2.refs_0_.refs_1_ = f32[384,128]{1,0:T(8,128)S(1)} collective-permute-done((f32[384,128]{1,0:T(8,128)S(1)}, f32[384,128]{1,0:T(8,128)S(1)}, u32[]{:S(2)}, u32[]{:S(2)}) %collective-permute-start.2) | collective-permute-done | bytes 196640 | tf_op jit(solution)/shard_map/ppermute | solution.py:439
  34.9 0.0 copy-start
  34.9 0.0 copy-start.2
  34.9 0.0 copy-start.3
  34.9 2.4 %relax.1.refs_3_ = f32[160,128]{1,0:T(8,128)S(1)} custom-call(s32[1]{0:T(128)} %bitcast.2.slab_ref, f32[384,128]{1,0:T(8,128)S(1)} %get-tuple-element.25.own_ref.refs_0_, f32[384,128]{1,0:T(8,128)S(1)} %collective-permute-done.2.refs_0_.refs_1_, f32[384,128]{1,0:T(8,128)S(1)} %collective-permute-done.3.refs_1_.refs_2_, ...), custom_call_target="tpu_custom_call" | custom-call | tf_op jit(solution)/shard_map/relax/pallas_call | solution.py:518
  37.2 0.8 %collective-permute-start.9 = (f32[160,128]{1,0:T(8,128)S(1)}, f32[160,128]{1,0:T(8,128)S(1)}, u32[]{:S(2)}, u32[]{:S(2)}) collective-permute-start(f32[160,128]{1,0:T(8,128)S(1)} %relax.1.refs_3_), channel_id=1, source_target_pairs={{4,8},{12,16},{20,24},{8,4},{16,12},{24,20},{5,9},{13,17},{21,25},... | collective-permute-start | bytes 245768 | tf_op jit(solution)/shard_map/ppermute | solution.py:439
  38.1 4.6 %collective-permute-start.8 = (f32[160,128]{1,0:T(8,128)S(1)}, f32[160,128]{1,0:T(8,128)S(1)}, u32[]{:S(2)}, u32[]{:S(2)}) collective-permute-start(f32[160,128]{1,0:T(8,128)S(1)} %relax.1.refs_3_), channel_id=1, source_target_pairs={{0,4},{8,12},{16,20},{24,28},{4,0},{12,8},{20,16},{28,24},{1,5},{9... | collective-permute-start | bytes 245768 | tf_op jit(solution)/shard_map/ppermute | solution.py:439
  42.7 0.0 copy-done
  42.7 0.0 copy-done.2
  42.7 0.0 copy-done.3
  42.7 3.1 %factor.1.factor_ref = f32[1,8192]{1,0:T(1,128)S(1)} custom-call(s32[1]{0:T(128)} %bitcast.place_ref, s32[1]{0:T(128)S(6)} %copy.7.count_ref, s32[4,8192]{1,0:T(4,128)S(1)} %copy-done, f32[1,8192]{1,0:T(1,128)S(1)} %bitcast.10, f32[1,8192]{1,0:T(1,128)S(1)} %bitcast.17, f32[2,4,32,128]{3,2,1,0:T(8,128)S(1)} %pad_maximum_fusion.1.refs_0_, ...), custom_call_target="tpu_custom_call" | custom-call | flops 2147483648 | bytes 1048576 | tf_op jit(solution)/shard_map/factor/pallas_call | solution.py:502
  45.8 0.0 collective-permute-done.9.refs_5_
  45.8 0.0 collective-permute-done.8.refs_4_
  45.8 1.1 %finish.1 = f32[224,128]{1,0:T(8,128)S(1)} custom-call(s32[1]{0:T(128)} %bitcast.2.slab_ref, f32[384,128]{1,0:T(8,128)S(1)} %get-tuple-element.25.own_ref.refs_0_, f32[384,128]{1,0:T(8,128)S(1)} %collective-permute-done.2.refs_0_.refs_1_, f32[384,128]{1,0:T(8,128)S(1)} %collective-permute-done.3.refs_1_.refs_2_, f32[160,128]{1,0:T(8,128)S(1)} %relax.1.refs_3_, ...), custom_call_target="tpu_custom_call" | custom-call | tf_op jit(solution)/shard_map/finish/pallas_call | solution.py:533
  46.9 0.3 collective-permute-start.10
  47.3 2.2 %sampled.2.refs_0_ = f32[3,8192]{1,0:T(4,128)S(1)} custom-call(s32[1]{0:T(128)} %bitcast.place_ref, s32[4,8192]{1,0:T(4,128)S(1)} %copy-done, f32[1,8192]{1,0:T(1,128)S(1)} %bitcast.11, f32[1,224,128]{2,1,0:T(8,128)S(1)} %bitcast.7), custom_call_target="tpu_custom_call" | custom-call | flops 1610612736 | bytes 1048576 | tf_op jit(solution)/shard_map/sampled/pallas_call | solution.py:546
  49.4 1.2 %collective-permute-done.10 = f32[1,224,128]{2,1,0:T(8,128)S(1)} collective-permute-done((f32[1,224,128]{2,1,0:T(8,128)S(1)}, f32[1,224,128]{2,1,0:T(8,128)S(1)}, u32[]{:S(2)}, u32[]{:S(2)}) %collective-permute-start.10) | collective-permute-done | bytes 114720 | tf_op jit(solution)/shard_map/ppermute | solution.py:430
  50.7 0.0 copy-start.1
  50.7 3.5 %collective-permute-start.11 = (f32[2,224,128]{2,1,0:T(8,128)S(1)}, f32[2,224,128]{2,1,0:T(8,128)S(1)}, u32[]{:S(2)}, u32[]{:S(2)}) collective-permute-start(f32[2,224,128]{2,1,0:T(8,128)S(1)} %pad_maximum_fusion.held_ref.refs_1_), channel_id=1, source_target_pairs={{0,1},{1,0},{2,3},{3,2},{4,5},{5,4},{6,7},{7,6},{8,9},{9,8},{10,11... | collective-permute-start | bytes 688136 | tf_op jit(solution)/shard_map/ppermute | solution.py:430
  54.2 2.2 %sampled.3.refs_0_ = f32[3,8192]{1,0:T(4,128)S(1)} custom-call(s32[1]{0:T(128)} %bitcast.place_ref, s32[4,8192]{1,0:T(4,128)S(1)} %copy-done, f32[1,8192]{1,0:T(1,128)S(1)} %bitcast.12, f32[2,224,128]{2,1,0:T(8,128)S(1)} %pad_maximum_fusion.held_ref.refs_1_, f32[3,8192]{1,0:T(4,128)S(1)} %sampled.2.refs_0_), custom_call_target="tpu_custom_call" | custom-call | flops 1610612736 | bytes 1048576 | tf_op jit(solution)/shard_map/sampled/pallas_call | solution.py:546
  56.4 0.0 collective-permute-done.11.refs_2_
  56.4 0.0 copy-done.1
  56.4 4.9 %drag.1 = (f32[4,16,256]{2,1,0:T(8,128)}, f32[3,8192]{1,0:T(4,128)}) custom-call(s32[1]{0:T(128)} %bitcast.place_ref, s32[4,8192]{1,0:T(4,128)S(1)} %copy-done, f32[1,8192]{1,0:T(1,128)S(1)} %bitcast.13, f32[3,8192]{1,0:T(4,128)S(1)} %copy-done.1, f32[1,8192]{1,0:T(1,128)S(1)} %factor.1.factor_ref, f32[3,8192]{1,0:T(4,128)S(1)} %sampled.3.refs_0_, ...), custom_call_target="tpu_custom_call" | custom-call | tf_op jit(solution)/shard_map/drag/pallas_call | solution.py:569
  (4 shorter events, 0.1 us)
Async XLA Ops:
  8.1 1.8 %collective-permute-start = (f32[2,384,128]{2,1,0:T(8,128)S(1)}, f32[2,384,128]{2,1,0:T(8,128)S(1)}, u32[]{:S(2)}, u32[]{:S(2)}) collective-permute-start(f32[2,384,128]{2,1,0:T(8,128)S(1)} %get-tuple-element.21), channel_id=1, source_target_pairs={{0,1},{1,0},{2,3},{3,2},{4,5},{5,4},{6,7},{7,6},{8,9},{9,8},{10,11... | collective-permute-start | bytes 1179656 | tf_op jit(solution)/shard_map/ppermute | solution.py:430
  10.0 7.4 %collective-permute-start.1 = (f32[1,384,128]{2,1,0:T(8,128)S(1)}, f32[1,384,128]{2,1,0:T(8,128)S(1)}, u32[]{:S(2)}, u32[]{:S(2)}) collective-permute-start(f32[1,384,128]{2,1,0:T(8,128)S(1)} %get-tuple-element.38), channel_id=1, source_target_pairs={{0,2},{1,3},{2,0},{3,1},{4,6},{5,7},{6,4},{7,5},{8,10},{9,11},{10,... | collective-permute-start | bytes 589832 | tf_op jit(solution)/shard_map/ppermute | solution.py:430
  17.9 9.0 %collective-permute-start.6 = (f32[1,4,32,128]{3,2,1,0:T(8,128)S(1)}, f32[1,4,32,128]{3,2,1,0:T(8,128)S(1)}, u32[]{:S(2)}, u32[]{:S(2)}) collective-permute-start(f32[1,4,32,128]{3,2,1,0:T(8,128)S(1)} %bitcast.14), channel_id=1, source_target_pairs={{0,2},{1,3},{2,0},{3,1},{4,6},{5,7},{6,4},{7,5},{8,10},{9,11},{10,... | collective-permute-start | bytes 196616 | tf_op jit(solution)/shard_map/ppermute | solution.py:430
  19.1 10.2 %collective-permute-start.5 = (f32[320,128]{1,0:T(8,128)S(1)}, f32[320,128]{1,0:T(8,128)S(1)}, u32[]{:S(2)}, u32[]{:S(2)}) collective-permute-start(f32[320,128]{1,0:T(8,128)S(1)} %get-tuple-element.23), channel_id=1, source_target_pairs={{8,16},{12,20},{16,8},{20,12},{9,17},{13,21},{17,9},{21,13},{10,18... | collective-permute-start | bytes 491528 | tf_op jit(solution)/shard_map/ppermute | solution.py:439
  19.8 9.5 %collective-permute-start.4 = (f32[320,128]{1,0:T(8,128)S(1)}, f32[320,128]{1,0:T(8,128)S(1)}, u32[]{:S(2)}, u32[]{:S(2)}) collective-permute-start(f32[320,128]{1,0:T(8,128)S(1)} %get-tuple-element.23), channel_id=1, source_target_pairs={{0,8},{4,12},{16,24},{20,28},{8,0},{12,4},{24,16},{28,20},{1,9},{5... | collective-permute-start | bytes 491528 | tf_op jit(solution)/shard_map/ppermute | solution.py:439
  23.7 6.6 %collective-permute-start.3 = (f32[384,128]{1,0:T(8,128)S(1)}, f32[384,128]{1,0:T(8,128)S(1)}, u32[]{:S(2)}, u32[]{:S(2)}) collective-permute-start(f32[384,128]{1,0:T(8,128)S(1)} %get-tuple-element.25.own_ref.refs_0_), channel_id=1, source_target_pairs={{4,8},{12,16},{20,24},{8,4},{16,12},{24,20},{5,9},{13,17},{21,25},... | collective-permute-start | bytes 589832 | tf_op jit(solution)/shard_map/ppermute | solution.py:439
  24.3 10.5 %collective-permute-start.2 = (f32[384,128]{1,0:T(8,128)S(1)}, f32[384,128]{1,0:T(8,128)S(1)}, u32[]{:S(2)}, u32[]{:S(2)}) collective-permute-start(f32[384,128]{1,0:T(8,128)S(1)} %get-tuple-element.25.own_ref.refs_0_), channel_id=1, source_target_pairs={{0,4},{8,12},{16,20},{24,28},{4,0},{12,8},{20,16},{28,24},{1,5},{9... | collective-permute-start | bytes 589832 | tf_op jit(solution)/shard_map/ppermute | solution.py:439
  26.9 3.4 %collective-permute-start.7 = (f32[2,4,32,128]{3,2,1,0:T(8,128)S(1)}, f32[2,4,32,128]{3,2,1,0:T(8,128)S(1)}, u32[]{:S(2)}, u32[]{:S(2)}) collective-permute-start(f32[2,4,32,128]{3,2,1,0:T(8,128)S(1)} %pad_maximum_fusion.1.refs_0_), channel_id=1, source_target_pairs={{0,1},{1,0},{2,3},{3,2},{4,5},{5,4},{6,7},{7,6},{8,9},{9,8},{10,11... | collective-permute-start | bytes 393224 | tf_op jit(solution)/shard_map/ppermute | solution.py:430
  34.9 7.8 %copy-start = (s32[4,8192]{1,0:T(4,128)S(1)}, s32[4,8192]{1,0:T(4,128)}, u32[]{:S(2)}) copy-start(s32[4,8192]{1,0:T(4,128)} %cell_ref.7) | copy-start | bytes 393220
  34.9 7.8 %copy-start.2 = (f32[8192]{0:T(1024)S(1)}, f32[8192]{0:T(1024)}, u32[]{:S(2)}) copy-start(f32[8192]{0:T(1024)} %param.7) | copy-start | bytes 98308
  34.9 7.8 %copy-start.3 = (f32[8192]{0:T(1024)S(1)}, f32[8192]{0:T(1024)}, u32[]{:S(2)}) copy-start(f32[8192]{0:T(1024)} %param.8) | copy-start | bytes 98308
  37.2 8.6 %collective-permute-start.9 = (f32[160,128]{1,0:T(8,128)S(1)}, f32[160,128]{1,0:T(8,128)S(1)}, u32[]{:S(2)}, u32[]{:S(2)}) collective-permute-start(f32[160,128]{1,0:T(8,128)S(1)} %relax.1.refs_3_), channel_id=1, source_target_pairs={{4,8},{12,16},{20,24},{8,4},{16,12},{24,20},{5,9},{13,17},{21,25},... | collective-permute-start | bytes 245768 | tf_op jit(solution)/shard_map/ppermute | solution.py:439
  38.1 7.7 %collective-permute-start.8 = (f32[160,128]{1,0:T(8,128)S(1)}, f32[160,128]{1,0:T(8,128)S(1)}, u32[]{:S(2)}, u32[]{:S(2)}) collective-permute-start(f32[160,128]{1,0:T(8,128)S(1)} %relax.1.refs_3_), channel_id=1, source_target_pairs={{0,4},{8,12},{16,20},{24,28},{4,0},{12,8},{20,16},{28,24},{1,5},{9... | collective-permute-start | bytes 245768 | tf_op jit(solution)/shard_map/ppermute | solution.py:439
  46.9 3.7 %collective-permute-start.10 = (f32[1,224,128]{2,1,0:T(8,128)S(1)}, f32[1,224,128]{2,1,0:T(8,128)S(1)}, u32[]{:S(2)}, u32[]{:S(2)}) collective-permute-start(f32[1,224,128]{2,1,0:T(8,128)S(1)} %bitcast.6), channel_id=1, source_target_pairs={{0,2},{1,3},{2,0},{3,1},{4,6},{5,7},{6,4},{7,5},{8,10},{9,11},{10,... | collective-permute-start | bytes 344072 | tf_op jit(solution)/shard_map/ppermute | solution.py:430
  50.7 5.7 %copy-start.1 = (f32[3,8192]{1,0:T(4,128)S(1)}, f32[3,8192]{1,0:T(4,128)}, u32[]{:S(2)}) copy-start(f32[3,8192]{1,0:T(4,128)} %velocity_ref.1) | copy-start | bytes 294916
  50.7 5.7 %collective-permute-start.11 = (f32[2,224,128]{2,1,0:T(8,128)S(1)}, f32[2,224,128]{2,1,0:T(8,128)S(1)}, u32[]{:S(2)}, u32[]{:S(2)}) collective-permute-start(f32[2,224,128]{2,1,0:T(8,128)S(1)} %pad_maximum_fusion.held_ref.refs_1_), channel_id=1, source_target_pairs={{0,1},{1,0},{2,3},{3,2},{4,5},{5,4},{6,7},{7,6},{8,9},{9,8},{10,11... | collective-permute-start | bytes 688136 | tf_op jit(solution)/shard_map/ppermute | solution.py:430

commit v2 on v1

--- a/solution.py
+++ b/solution.py
@@ -496,22 +496,8 @@
         swapped(distance, matching, coefs[distance - 1])
         for distance, matching in swap_plan(DEPTH)
     ]
+    stack[-1], solid = lax.optimization_barrier((stack[-1], solid))
     solids = nearly_all(solid)
-    solids = [solids, over_quad(last, solids)]
-    stack, solids = lax.optimization_barrier((stack, solids))
-    factor = pl.pallas_call(
-        functools.partial(factor_kernel, quads, min(grains, 512)),
-        out_shape=cells(1, grains),
-        in_specs=[SMEM, SMEM] + [VMEM] * 5,
-        out_specs=VMEM,
-        scratch_shapes=[pltpu.VMEM((quads,) + solid.shape, jnp.float32)],
-        compiler_params=LIMIT,
-        cost_estimate=pl.CostEstimate(
-            flops=4 * CB * CH * across * grains, bytes_accessed=2**20, transcendentals=0
-        ),
-        name="factor",
-    )(place, grain_count, grain_cell, weight, volume, *solids)
-
     frame = cells(packed_rows(across, 1, SUBLANES, own) + 2 * tall, LANES)
     layers = CH * len(stack)
     two_rounds = FIRST < ITERS
@@ -526,6 +512,21 @@
         compiler_params=LIMIT,
         name="relax",
     )(level, *stack)
+    centre, solids = lax.optimization_barrier((centre, solids))
+    solids = [solids, over_quad(last, solids)]
+    factor = pl.pallas_call(
+        functools.partial(factor_kernel, quads, min(grains, 512)),
+        out_shape=cells(1, grains),
+        in_specs=[SMEM, SMEM] + [VMEM] * 5,
+        out_specs=VMEM,
+        scratch_shapes=[pltpu.VMEM((quads,) + solid.shape, jnp.float32)],
+        compiler_params=LIMIT,
+        cost_estimate=pl.CostEstimate(
+            flops=4 * CB * CH * across * grains, bytes_accessed=2**20, transcendentals=0
+        ),
+        name="factor",
+    )(place, grain_count, grain_cell, weight, volume, *solids)
+
     mine = centre
     if two_rounds:
         pressures = [centre] + [swapped(*swap, centre) for swap in swap_plan(1)]

time: 61.4 us -> 59.7 us (0.972)
  the two profiles are of different devices: /device:TPU:1 before, /device:TPU:9 now
where the time goes in v2:
time: 59.7 us; the launch traced here: 59.1 us
  Pallas kernels  23.2 us (39%)
  starting transfers between devices  20.1 us (34%)
  waiting for transfers between devices  14.3 us (24%)
  between operations  1.46 us (2%)
    ppermute x6, starting transfers between devices, swapped(): lax.ppermute(value, 'slab', pairs + [(high, low) for low, high in pairs])  12.8 us
    ppermute x6, starting transfers between devices, over_quad(): return lax.ppermute(value, 'quad', pairs)  7.27 us
    ppermute x6, waiting for transfers between devices, over_quad(): return lax.ppermute(value, 'quad', pairs)  7.15 us
    ppermute x6, waiting for transfers between devices, swapped(): lax.ppermute(value, 'slab', pairs + [(high, low) for low, high in pairs])  7.11 us
    pallas_call x1, Pallas kernels, body(): pl.pallas_call(functools.partial(deposit_kernel, quads, min(grains, 2048)...  6.8 us
    pallas_call x1, Pallas kernels, body(): pl.pallas_call(functools.partial(drag_kernel, quads, grain_chunk), out_sh...  4.88 us
    pallas_call x2, Pallas kernels, sampled_from(): pl.pallas_call(functools.partial(sampled_kernel, quads, grain_chunk, plac...  4.38 us
    pallas_call x1, Pallas kernels, body(): pl.pallas_call(functools.partial(factor_kernel, quads, min(grains, 512)),...  3.11 us
  transfers between devices with their start and end apart: 12, of which 6 were waited for; matrix products, arithmetic and copies ran while one was open for 0% of the time, Pallas kernels for 17%

profile of v2, /device:TPU:9, one launch (start us, length us, event | category | flops | bytes accessed | tf_op | source)
XLA Modules:
  0.0 59.1 jit_solution(6537857335316322709)
XLA Ops:
  1.3 6.8 %deposit.1 = (f32[2,384,128]{2,1,0:T(8,128)S(1)}, f32[2,384,128]{2,1,0:T(8,128)S(1)}) custom-call(s32[1]{0:T(128)} %bitcast.place_ref, s32[1]{0:T(128)S(6)} %copy.7.count_ref, s32[4,8192]{1,0:T(4,128)} %cell_ref.7, f32[1,8192]{1,0:T(1,128)} %bitcast.9, f32[1,8192]{1,0:T(1,128)} %bitcast.16, f32[3,8192]{1,0:T(4,128)} %velocity_ref.1), custom_call_target="tpu_custom_call" | custom-call | tf_op jit(solution)/shard_map/deposit/pallas_call | solution.py:452
  8.1 0.7 %collective-permute-start = (f32[2,384,128]{2,1,0:T(8,128)S(1)}, f32[2,384,128]{2,1,0:T(8,128)S(1)}, u32[]{:S(2)}, u32[]{:S(2)}) collective-permute-start(f32[2,384,128]{2,1,0:T(8,128)S(1)} %get-tuple-element.18), channel_id=1, source_target_pairs={{0,1},{1,0},{2,3},{3,2},{4,5},{5,4},{6,7},{7,6},{8,9},{9,8},{10,11... | collective-permute-start | bytes 1179656 | tf_op jit(solution)/shard_map/ppermute | solution.py:430
  8.8 1.3 %collective-permute-done = f32[2,384,128]{2,1,0:T(8,128)S(1)} collective-permute-done((f32[2,384,128]{2,1,0:T(8,128)S(1)}, f32[2,384,128]{2,1,0:T(8,128)S(1)}, u32[]{:S(2)}, u32[]{:S(2)}) %collective-permute-start) | collective-permute-done | bytes 393248 | tf_op jit(solution)/shard_map/ppermute | solution.py:430
  10.3 1.3 %collective-permute-start.1 = (f32[1,384,128]{2,1,0:T(8,128)S(1)}, f32[1,384,128]{2,1,0:T(8,128)S(1)}, u32[]{:S(2)}, u32[]{:S(2)}) collective-permute-start(f32[1,384,128]{2,1,0:T(8,128)S(1)} %get-tuple-element.32), channel_id=1, source_target_pairs={{0,2},{1,3},{2,0},{3,1},{4,6},{5,7},{6,4},{7,5},{8,10},{9,11},{10,... | collective-permute-start | bytes 589832 | tf_op jit(solution)/shard_map/ppermute | solution.py:430
  11.5 4.9 %collective-permute-done.1.got_ref = f32[1,384,128]{2,1,0:T(8,128)S(1)} collective-permute-done((f32[1,384,128]{2,1,0:T(8,128)S(1)}, f32[1,384,128]{2,1,0:T(8,128)S(1)}, u32[]{:S(2)}, u32[]{:S(2)}) %collective-permute-start.1) | collective-permute-done | bytes 196640 | tf_op jit(solution)/shard_map/ppermute | solution.py:430
  16.4 0.5 coefficients.1
  17.0 3.2 %collective-permute-start.5 = (f32[320,128]{1,0:T(8,128)S(1)}, f32[320,128]{1,0:T(8,128)S(1)}, u32[]{:S(2)}, u32[]{:S(2)}) collective-permute-start(f32[320,128]{1,0:T(8,128)S(1)} %get-tuple-element.20), channel_id=1, source_target_pairs={{8,16},{12,20},{16,8},{20,12},{9,17},{13,21},{17,9},{21,13},{10,18... | collective-permute-start | bytes 491528 | tf_op jit(solution)/shard_map/ppermute | solution.py:439
  20.2 1.9 %collective-permute-start.3 = (f32[384,128]{1,0:T(8,128)S(1)}, f32[384,128]{1,0:T(8,128)S(1)}, u32[]{:S(2)}, u32[]{:S(2)}) collective-permute-start(f32[384,128]{1,0:T(8,128)S(1)} %get-tuple-element.19.own_ref.refs_0_), channel_id=1, source_target_pairs={{4,8},{12,16},{20,24},{8,4},{16,12},{24,20},{5,9},{13,17},{21,25},... | collective-permute-start | bytes 589832 | tf_op jit(solution)/shard_map/ppermute | solution.py:439
  22.1 1.4 %collective-permute-start.2 = (f32[384,128]{1,0:T(8,128)S(1)}, f32[384,128]{1,0:T(8,128)S(1)}, u32[]{:S(2)}, u32[]{:S(2)}) collective-permute-start(f32[384,128]{1,0:T(8,128)S(1)} %get-tuple-element.19.own_ref.refs_0_), channel_id=1, source_target_pairs={{0,4},{8,12},{16,20},{24,28},{4,0},{12,8},{20,16},{28,24},{1,5},{9... | collective-permute-start | bytes 589832 | tf_op jit(solution)/shard_map/ppermute | solution.py:439
  23.5 1.3 %collective-permute-start.4 = (f32[320,128]{1,0:T(8,128)S(1)}, f32[320,128]{1,0:T(8,128)S(1)}, u32[]{:S(2)}, u32[]{:S(2)}) collective-permute-start(f32[320,128]{1,0:T(8,128)S(1)} %get-tuple-element.20), channel_id=1, source_target_pairs={{0,8},{4,12},{16,24},{20,28},{8,0},{12,4},{24,16},{28,20},{1,9},{5... | collective-permute-start | bytes 491528 | tf_op jit(solution)/shard_map/ppermute | solution.py:439
  24.8 0.0 collective-permute-done.5.refs_3_
  24.8 1.2 %collective-permute-start.6 = (f32[1,4,32,128]{3,2,1,0:T(8,128)S(1)}, f32[1,4,32,128]{3,2,1,0:T(8,128)S(1)}, u32[]{:S(2)}, u32[]{:S(2)}) collective-permute-start(f32[1,4,32,128]{3,2,1,0:T(8,128)S(1)} %bitcast.14), channel_id=1, source_target_pairs={{0,2},{1,3},{2,0},{3,1},{4,6},{5,7},{6,4},{7,5},{8,10},{9,11},{10,... | collective-permute-start | bytes 196616 | tf_op jit(solution)/shard_map/ppermute | solution.py:430
  26.1 2.8 %collective-permute-done.4.refs_2_ = f32[320,128]{1,0:T(8,128)S(1)} collective-permute-done((f32[320,128]{1,0:T(8,128)S(1)}, f32[320,128]{1,0:T(8,128)S(1)}, u32[]{:S(2)}, u32[]{:S(2)}) %collective-permute-start.4) | collective-permute-done | bytes 163872 | tf_op jit(solution)/shard_map/ppermute | solution.py:439
  28.9 0.0 collective-permute-done.3.refs_1_.refs_2_
  28.9 3.5 %collective-permute-done.2.refs_0_.refs_1_ = f32[384,128]{1,0:T(8,128)S(1)} collective-permute-done((f32[384,128]{1,0:T(8,128)S(1)}, f32[384,128]{1,0:T(8,128)S(1)}, u32[]{:S(2)}, u32[]{:S(2)}) %collective-permute-start.2) | collective-permute-done | bytes 196640 | tf_op jit(solution)/shard_map/ppermute | solution.py:439
  32.4 2.4 %relax.1.refs_3_ = f32[160,128]{1,0:T(8,128)S(1)} custom-call(s32[1]{0:T(128)} %bitcast.2.slab_ref, f32[384,128]{1,0:T(8,128)S(1)} %get-tuple-element.19.own_ref.refs_0_, f32[384,128]{1,0:T(8,128)S(1)} %collective-permute-done.2.refs_0_.refs_1_, f32[384,128]{1,0:T(8,128)S(1)} %collective-permute-done.3.refs_1_.refs_2_, ...), custom_call_target="tpu_custom_call" | custom-call | tf_op jit(solution)/shard_map/relax/pallas_call | solution.py:504
  34.7 0.0 copy-start
  34.8 0.0 copy-start.2
  34.8 0.0 copy-start.3
  34.8 0.0 collective-permute-done.6
  34.8 1.4 %collective-permute-start.9 = (f32[2,4,32,128]{3,2,1,0:T(8,128)S(1)}, f32[2,4,32,128]{3,2,1,0:T(8,128)S(1)}, u32[]{:S(2)}, u32[]{:S(2)}) collective-permute-start(f32[2,4,32,128]{3,2,1,0:T(8,128)S(1)} %pad_maximum_fusion.1.refs_0_), channel_id=1, source_target_pairs={{0,1},{1,0},{2,3},{3,2},{4,5},{5,4},{6,7},{7,6},{8,9},{9,8},{10,11... | collective-permute-start | bytes 393224 | tf_op jit(solution)/shard_map/ppermute | solution.py:430
  36.2 2.9 %collective-permute-start.8 = (f32[160,128]{1,0:T(8,128)S(1)}, f32[160,128]{1,0:T(8,128)S(1)}, u32[]{:S(2)}, u32[]{:S(2)}) collective-permute-start(f32[160,128]{1,0:T(8,128)S(1)} %relax.1.refs_3_), channel_id=1, source_target_pairs={{4,8},{12,16},{20,24},{8,4},{16,12},{24,20},{5,9},{13,17},{21,25},... | collective-permute-start | bytes 245768 | tf_op jit(solution)/shard_map/ppermute | solution.py:439
  39.1 2.1 %collective-permute-start.7 = (f32[160,128]{1,0:T(8,128)S(1)}, f32[160,128]{1,0:T(8,128)S(1)}, u32[]{:S(2)}, u32[]{:S(2)}) collective-permute-start(f32[160,128]{1,0:T(8,128)S(1)} %relax.1.refs_3_), channel_id=1, source_target_pairs={{0,4},{8,12},{16,20},{24,28},{4,0},{12,8},{20,16},{28,24},{1,5},{9... | collective-permute-start | bytes 245768 | tf_op jit(solution)/shard_map/ppermute | solution.py:439
  41.3 0.0 collective-permute-done.9.refs_1_
  41.3 0.0 copy-done
  41.3 0.0 copy-done.2
  41.3 0.0 copy-done.3
  41.3 3.1 %factor.1.factor_ref = f32[1,8192]{1,0:T(1,128)S(1)} custom-call(s32[1]{0:T(128)} %bitcast.place_ref, s32[1]{0:T(128)S(6)} %copy.7.count_ref, s32[4,8192]{1,0:T(4,128)S(1)} %copy-done, f32[1,8192]{1,0:T(1,128)S(1)} %bitcast.10, f32[1,8192]{1,0:T(1,128)S(1)} %bitcast.17, f32[2,4,32,128]{3,2,1,0:T(8,128)S(1)} %pad_maximum_fusion.1.refs_0_, ...), custom_call_target="tpu_custom_call" | custom-call | flops 2147483648 | bytes 1048576 | tf_op jit(solution)/shard_map/factor/pallas_call | solution.py:517
  44.4 0.0 collective-permute-done.8.refs_5_
  44.4 0.8 %collective-permute-done.7.refs_4_ = f32[160,128]{1,0:T(8,128)S(1)} collective-permute-done((f32[160,128]{1,0:T(8,128)S(1)}, f32[160,128]{1,0:T(8,128)S(1)}, u32[]{:S(2)}, u32[]{:S(2)}) %collective-permute-start.7) | collective-permute-done | bytes 81952 | tf_op jit(solution)/shard_map/ppermute | solution.py:439
  45.2 1.1 %finish.1 = f32[224,128]{1,0:T(8,128)S(1)} custom-call(s32[1]{0:T(128)} %bitcast.2.slab_ref, f32[384,128]{1,0:T(8,128)S(1)} %get-tuple-element.19.own_ref.refs_0_, f32[384,128]{1,0:T(8,128)S(1)} %collective-permute-done.2.refs_0_.refs_1_, f32[384,128]{1,0:T(8,128)S(1)} %collective-permute-done.3.refs_1_.refs_2_, f32[160,128]{1,0:T(8,128)S(1)} %relax.1.refs_3_, ...), custom_call_target="tpu_custom_call" | custom-call | tf_op jit(solution)/shard_map/finish/pallas_call | solution.py:534
  46.3 1.3 %collective-permute-start.10 = (f32[1,224,128]{2,1,0:T(8,128)S(1)}, f32[1,224,128]{2,1,0:T(8,128)S(1)}, u32[]{:S(2)}, u32[]{:S(2)}) collective-permute-start(f32[1,224,128]{2,1,0:T(8,128)S(1)} %bitcast.6), channel_id=1, source_target_pairs={{0,2},{1,3},{2,0},{3,1},{4,6},{5,7},{6,4},{7,5},{8,10},{9,11},{10,... | collective-permute-start | bytes 344072 | tf_op jit(solution)/shard_map/ppermute | solution.py:430
  47.6 2.2 %sampled.2.refs_0_ = f32[3,8192]{1,0:T(4,128)S(1)} custom-call(s32[1]{0:T(128)} %bitcast.place_ref, s32[4,8192]{1,0:T(4,128)S(1)} %copy-done, f32[1,8192]{1,0:T(1,128)S(1)} %bitcast.11, f32[1,224,128]{2,1,0:T(8,128)S(1)} %bitcast.7), custom_call_target="tpu_custom_call" | custom-call | flops 1610612736 | bytes 1048576 | tf_op jit(solution)/shard_map/sampled/pallas_call | solution.py:547
  49.8 0.9 %collective-permute-done.10 = f32[1,224,128]{2,1,0:T(8,128)S(1)} collective-permute-done((f32[1,224,128]{2,1,0:T(8,128)S(1)}, f32[1,224,128]{2,1,0:T(8,128)S(1)}, u32[]{:S(2)}, u32[]{:S(2)}) %collective-permute-start.10) | collective-permute-done | bytes 114720 | tf_op jit(solution)/shard_map/ppermute | solution.py:430
  50.7 0.0 copy-start.1
  50.7 1.3 %collective-permute-start.11 = (f32[2,224,128]{2,1,0:T(8,128)S(1)}, f32[2,224,128]{2,1,0:T(8,128)S(1)}, u32[]{:S(2)}, u32[]{:S(2)}) collective-permute-start(f32[2,224,128]{2,1,0:T(8,128)S(1)} %pad_maximum_fusion.held_ref.refs_1_), channel_id=1, source_target_pairs={{0,1},{1,0},{2,3},{3,2},{4,5},{5,4},{6,7},{7,6},{8,9},{9,8},{10,11... | collective-permute-start | bytes 688136 | tf_op jit(solution)/shard_map/ppermute | solution.py:430
  52.0 2.2 %sampled.3.refs_0_ = f32[3,8192]{1,0:T(4,128)S(1)} custom-call(s32[1]{0:T(128)} %bitcast.place_ref, s32[4,8192]{1,0:T(4,128)S(1)} %copy-done, f32[1,8192]{1,0:T(1,128)S(1)} %bitcast.12, f32[2,224,128]{2,1,0:T(8,128)S(1)} %pad_maximum_fusion.held_ref.refs_1_, f32[3,8192]{1,0:T(4,128)S(1)} %sampled.2.refs_0_), custom_call_target="tpu_custom_call" | custom-call | flops 1610612736 | bytes 1048576 | tf_op jit(solution)/shard_map/sampled/pallas_call | solution.py:547
  54.2 0.0 collective-permute-done.11.refs_2_
  54.3 0.0 copy-done.1
  54.3 4.9 %drag.1 = (f32[4,16,256]{2,1,0:T(8,128)}, f32[3,8192]{1,0:T(4,128)}) custom-call(s32[1]{0:T(128)} %bitcast.place_ref, s32[4,8192]{1,0:T(4,128)S(1)} %copy-done, f32[1,8192]{1,0:T(1,128)S(1)} %bitcast.13, f32[3,8192]{1,0:T(4,128)S(1)} %copy-done.1, f32[1,8192]{1,0:T(1,128)S(1)} %factor.1.factor_ref, f32[3,8192]{1,0:T(4,128)S(1)} %sampled.3.refs_0_, ...), custom_call_target="tpu_custom_call" | custom-call | tf_op jit(solution)/shard_map/drag/pallas_call | solution.py:570
  (4 shorter events, 0.1 us)
Async XLA Ops:
  8.1 2.1 %collective-permute-start = (f32[2,384,128]{2,1,0:T(8,128)S(1)}, f32[2,384,128]{2,1,0:T(8,128)S(1)}, u32[]{:S(2)}, u32[]{:S(2)}) collective-permute-start(f32[2,384,128]{2,1,0:T(8,128)S(1)} %get-tuple-element.18), channel_id=1, source_target_pairs={{0,1},{1,0},{2,3},{3,2},{4,5},{5,4},{6,7},{7,6},{8,9},{9,8},{10,11... | collective-permute-start | bytes 1179656 | tf_op jit(solution)/shard_map/ppermute | solution.py:430
  10.3 6.2 %collective-permute-start.1 = (f32[1,384,128]{2,1,0:T(8,128)S(1)}, f32[1,384,128]{2,1,0:T(8,128)S(1)}, u32[]{:S(2)}, u32[]{:S(2)}) collective-permute-start(f32[1,384,128]{2,1,0:T(8,128)S(1)} %get-tuple-element.32), channel_id=1, source_target_pairs={{0,2},{1,3},{2,0},{3,1},{4,6},{5,7},{6,4},{7,5},{8,10},{9,11},{10,... | collective-permute-start | bytes 589832 | tf_op jit(solution)/shard_map/ppermute | solution.py:430
  17.0 7.8 %collective-permute-start.5 = (f32[320,128]{1,0:T(8,128)S(1)}, f32[320,128]{1,0:T(8,128)S(1)}, u32[]{:S(2)}, u32[]{:S(2)}) collective-permute-start(f32[320,128]{1,0:T(8,128)S(1)} %get-tuple-element.20), channel_id=1, source_target_pairs={{8,16},{12,20},{16,8},{20,12},{9,17},{13,21},{17,9},{21,13},{10,18... | collective-permute-start | bytes 491528 | tf_op jit(solution)/shard_map/ppermute | solution.py:439
  20.2 8.7 %collective-permute-start.3 = (f32[384,128]{1,0:T(8,128)S(1)}, f32[384,128]{1,0:T(8,128)S(1)}, u32[]{:S(2)}, u32[]{:S(2)}) collective-permute-start(f32[384,128]{1,0:T(8,128)S(1)} %get-tuple-element.19.own_ref.refs_0_), channel_id=1, source_target_pairs={{4,8},{12,16},{20,24},{8,4},{16,12},{24,20},{5,9},{13,17},{21,25},... | collective-permute-start | bytes 589832 | tf_op jit(solution)/shard_map/ppermute | solution.py:439
  22.1 10.2 %collective-permute-start.2 = (f32[384,128]{1,0:T(8,128)S(1)}, f32[384,128]{1,0:T(8,128)S(1)}, u32[]{:S(2)}, u32[]{:S(2)}) collective-permute-start(f32[384,128]{1,0:T(8,128)S(1)} %get-tuple-element.19.own_ref.refs_0_), channel_id=1, source_target_pairs={{0,4},{8,12},{16,20},{24,28},{4,0},{12,8},{20,16},{28,24},{1,5},{9... | collective-permute-start | bytes 589832 | tf_op jit(solution)/shard_map/ppermute | solution.py:439
  23.5 5.3 %collective-permute-start.4 = (f32[320,128]{1,0:T(8,128)S(1)}, f32[320,128]{1,0:T(8,128)S(1)}, u32[]{:S(2)}, u32[]{:S(2)}) collective-permute-start(f32[320,128]{1,0:T(8,128)S(1)} %get-tuple-element.20), channel_id=1, source_target_pairs={{0,8},{4,12},{16,24},{20,28},{8,0},{12,4},{24,16},{28,20},{1,9},{5... | collective-permute-start | bytes 491528 | tf_op jit(solution)/shard_map/ppermute | solution.py:439
  24.8 9.9 %collective-permute-start.6 = (f32[1,4,32,128]{3,2,1,0:T(8,128)S(1)}, f32[1,4,32,128]{3,2,1,0:T(8,128)S(1)}, u32[]{:S(2)}, u32[]{:S(2)}) collective-permute-start(f32[1,4,32,128]{3,2,1,0:T(8,128)S(1)} %bitcast.14), channel_id=1, source_target_pairs={{0,2},{1,3},{2,0},{3,1},{4,6},{5,7},{6,4},{7,5},{8,10},{9,11},{10,... | collective-permute-start | bytes 196616 | tf_op jit(solution)/shard_map/ppermute | solution.py:430
  34.7 6.5 %copy-start = (s32[4,8192]{1,0:T(4,128)S(1)}, s32[4,8192]{1,0:T(4,128)}, u32[]{:S(2)}) copy-start(s32[4,8192]{1,0:T(4,128)} %cell_ref.7) | copy-start | bytes 393220
  34.8 6.5 %copy-start.2 = (f32[8192]{0:T(1024)S(1)}, f32[8192]{0:T(1024)}, u32[]{:S(2)}) copy-start(f32[8192]{0:T(1024)} %param.7) | copy-start | bytes 98308
  34.8 6.5 %copy-start.3 = (f32[8192]{0:T(1024)S(1)}, f32[8192]{0:T(1024)}, u32[]{:S(2)}) copy-start(f32[8192]{0:T(1024)} %param.8) | copy-start | bytes 98308
  34.8 6.5 %collective-permute-start.9 = (f32[2,4,32,128]{3,2,1,0:T(8,128)S(1)}, f32[2,4,32,128]{3,2,1,0:T(8,128)S(1)}, u32[]{:S(2)}, u32[]{:S(2)}) collective-permute-start(f32[2,4,32,128]{3,2,1,0:T(8,128)S(1)} %pad_maximum_fusion.1.refs_0_), channel_id=1, source_target_pairs={{0,1},{1,0},{2,3},{3,2},{4,5},{5,4},{6,7},{7,6},{8,9},{9,8},{10,11... | collective-permute-start | bytes 393224 | tf_op jit(solution)/shard_map/ppermute | solution.py:430
  36.2 8.2 %collective-permute-start.8 = (f32[160,128]{1,0:T(8,128)S(1)}, f32[160,128]{1,0:T(8,128)S(1)}, u32[]{:S(2)}, u32[]{:S(2)}) collective-permute-start(f32[160,128]{1,0:T(8,128)S(1)} %relax.1.refs_3_), channel_id=1, source_target_pairs={{4,8},{12,16},{20,24},{8,4},{16,12},{24,20},{5,9},{13,17},{21,25},... | collective-permute-start | bytes 245768 | tf_op jit(solution)/shard_map/ppermute | solution.py:439
  39.1 6.1 %collective-permute-start.7 = (f32[160,128]{1,0:T(8,128)S(1)}, f32[160,128]{1,0:T(8,128)S(1)}, u32[]{:S(2)}, u32[]{:S(2)}) collective-permute-start(f32[160,128]{1,0:T(8,128)S(1)} %relax.1.refs_3_), channel_id=1, source_target_pairs={{0,4},{8,12},{16,20},{24,28},{4,0},{12,8},{20,16},{28,24},{1,5},{9... | collective-permute-start | bytes 245768 | tf_op jit(solution)/shard_map/ppermute | solution.py:439
  46.3 4.3 %collective-permute-start.10 = (f32[1,224,128]{2,1,0:T(8,128)S(1)}, f32[1,224,128]{2,1,0:T(8,128)S(1)}, u32[]{:S(2)}, u32[]{:S(2)}) collective-permute-start(f32[1,224,128]{2,1,0:T(8,128)S(1)} %bitcast.6), channel_id=1, source_target_pairs={{0,2},{1,3},{2,0},{3,1},{4,6},{5,7},{6,4},{7,5},{8,10},{9,11},{10,... | collective-permute-start | bytes 344072 | tf_op jit(solution)/shard_map/ppermute | solution.py:430
  50.7 3.6 %copy-start.1 = (f32[3,8192]{1,0:T(4,128)S(1)}, f32[3,8192]{1,0:T(4,128)}, u32[]{:S(2)}) copy-start(f32[3,8192]{1,0:T(4,128)} %velocity_ref.1) | copy-start | bytes 294916
  50.7 3.5 %collective-permute-start.11 = (f32[2,224,128]{2,1,0:T(8,128)S(1)}, f32[2,224,128]{2,1,0:T(8,128)S(1)}, u32[]{:S(2)}, u32[]{:S(2)}) collective-permute-start(f32[2,224,128]{2,1,0:T(8,128)S(1)} %pad_maximum_fusion.held_ref.refs_1_), channel_id=1, source_target_pairs={{0,1},{1,0},{2,3},{3,2},{4,5},{5,4},{6,7},{7,6},{8,9},{9,8},{10,11... | collective-permute-start | bytes 688136 | tf_op jit(solution)/shard_map/ppermute | solution.py:430

commit v3 on v2

--- a/solution.py
+++ b/solution.py
@@ -193,7 +193,7 @@
     outs, solid_ref = refs[:-1], refs[-1]
     across, own = quads * CA, CB // quads
     total = kept_ref[0] + got_ref[0]
-    solid_ref[...] = total[: solid_ref.shape[0] * solid_ref.shape[1]].reshape(solid_ref.shape)
+    solid_ref[...] = total[: solid_ref.shape[0]]
     solid, moment = unpack(total, 2, across, reach(0), own)
     lane = lanes_of(solid.shape)
     column = jnp.where(lane < (LANES + own) // 2, lane, lane - LANES) + place_ref[0] * own
@@ -257,15 +257,22 @@
         out_ref[...] = framed(last, DEPTH * CH, own)
 
 
-def finish_kernel(quads, slab_ref, *refs):
-    *parts, out_ref, offset_ref, gain_ref, even_ref, odd_ref = refs
+def finish_kernel(quads, slab_ref, offset_ref, gain_ref, *refs):
+    *parts, out_ref, even_ref, odd_ref = refs
     across, own = quads * CA, CB // quads
     slots = [1] + [1 + slot_of(slab_ref[0], *swap) for swap in swap_plan(1)]
-    for slot, coef, pressure in zip(slots, parts[:3], parts[3:]):
-        span = pl.ds(slot * CH, CH)
-        offset_ref[span], gain_ref[span] = unpack(coef[...], 2, across, reach(1), own)
-        (even_ref[span],) = unpack(pressure[...], 1, across, SUBLANES, own)
-    last = sweep_over(ITERS - FIRST, 3 * CH, across, even_ref, odd_ref, offset_ref, gain_ref)
+    for slot, pressure in zip(slots, parts):
+        (even_ref[pl.ds(slot * CH, CH)],) = unpack(pressure[...], 1, across, SUBLANES, own)
+    near = pl.ds((DEPTH - 1) * CH, 3 * CH)
+    last = sweep_over(
+        ITERS - FIRST,
+        3 * CH,
+        across,
+        even_ref,
+        odd_ref,
+        offset_ref.at[near],
+        gain_ref.at[near],
+    )
     out_ref[...] = framed(last, CH, own)
 
 
@@ -313,22 +320,9 @@
     return jnp.sum(picked[field * size : (field + 1) * size] * blend, axis=0, keepdims=True)
 
 
-def factor_kernel(quads, chunk, place_ref, count_ref, cell_ref, weight_ref, volume_ref, *refs):
-    *halfs, factor_ref, gathered = refs
-    across = quads * CA
-    rows = CH * across
-    parts = [half[index] for half in halfs for index in range(quads // 2)]
-    solid = whole_table(quads, place_ref, parts, gathered)
-    pieces = jnp.concatenate(halves(solid.reshape(rows, CB).T), axis=1)
-    row_iota = short_iota((rows, chunk))
-    col_iota = lax.broadcasted_iota(jnp.int32, (CB, chunk), 0)
-    for first in range(0, weight_ref.shape[1], chunk):
-        span = pl.ds(first, chunk)
-        mass = mass_of(count_ref, volume_ref, first, span)
-        hot = one_hot(row_iota, row_of(cell_ref, span, across))
-        blend = blend_of(col_iota, cell_ref[3:4, span], weight_ref[0:1, span])
-        sampled = blended(picked_by(pieces, hot), blend, 0)
-        factor_ref[0:1, span] = mass * (1.0 + sampled) ** 2
+def solid_table(value, across, own):
+    window = unpack_own(value.reshape(CH, across * own // LANES, LANES), own)
+    return jnp.concatenate(halves(window.reshape(CH * across, LANES).T[:own]), axis=1)
 
 
 def velocity_table(value, across, own):
@@ -350,54 +344,91 @@
     return jnp.concatenate(halves(jnp.concatenate(columns, axis=0)), axis=1)
 
 
-def velocity_chunk(quads, place_ref, tables, offsets, cell_ref, weight_ref, row_iota, span):
+def chunk_sums(quads, place_ref, table, offsets, fields, cell_ref, weight_ref, row_iota, span):
     across, own = quads * CA, CB // quads
     hot = one_hot(row_iota, row_of(cell_ref, span, across))
     lower = weight_ref[0:1, span]
-    picked = picked_by(tables, hot)
+    picked = picked_by(table, hot)
     col_iota = lax.broadcasted_iota(jnp.int32, (own, picked.shape[1]), 0)
-    sums = [0.0] * 3
+    sums = [0.0] * fields
     for index, offset in enumerate(offsets):
         at = cell_ref[3:4, span] - (place_ref[0] ^ offset) * own
         blend = blend_of(col_iota, at, lower)
-        for component in range(3):
-            sums[component] += blended(picked, blend, 3 * index + component)
+        for field in range(fields):
+            sums[field] += blended(picked, blend, fields * index + field)
     return sums
+
+
+def store_sums(chunk, table, offsets, fields, quads, place_ref, cell_ref, weight_ref, earlier, out_ref):
+    row_iota = short_iota((CH * quads * CA, chunk))
+    for first in range(0, weight_ref.shape[1], chunk):
+        span = pl.ds(first, chunk)
+        sums = chunk_sums(
+            quads, place_ref, table, offsets, fields, cell_ref, weight_ref, row_iota, span
+        )
+        for field, value in enumerate(sums):
+            one = pl.ds(field, 1)
+            for partial in earlier:
+                value = value + partial[one, span]
+            out_ref[one, span] = value
+
+
+def solid_kernel(quads, chunk, place_ref, cell_ref, weight_ref, held_ref, out_ref):
+    across, own = quads * CA, CB // quads
+    half = quads // 2
+    tables = [solid_table(held_ref[index], across, own) for index in range(half)]
+    store_sums(
+        chunk,
+        jnp.concatenate(tables, axis=0),
+        place_offsets(quads)[:half],
+        1,
+        quads,
+        place_ref,
+        cell_ref,
+        weight_ref,
+        [],
+        out_ref,
+    )
 
 
 def sampled_kernel(quads, chunk, offset, index, place_ref, cell_ref, weight_ref, held_ref, *refs):
     *earlier, out_ref = refs
+    table = velocity_table(held_ref[index], quads * CA, CB // quads)
+    store_sums(
+        chunk, table, [offset], 3, quads, place_ref, cell_ref, weight_ref, earlier, out_ref
+    )
+
+
+def drag_kernel(quads, chunk, place_ref, count_ref, cell_ref, weight_ref, volume_ref, *refs):
+    velocity_ref, solid_ref, sampled_ref, held_ref, got_ref = refs[:5]
+    pressure_ref, drag_ref, gathered = refs[5:]
     across, own = quads * CA, CB // quads
-    table = velocity_table(held_ref[index], across, own)
+    half = quads // 2
+    frame = held_ref.shape[1]
+    tables = []
+    for index in range(half):
+        got = got_ref[index]
+        tables += [velocity_table(got[:frame], across, own), solid_table(got[frame:], across, own)]
+    table = jnp.concatenate(tables, axis=0)
     row_iota = short_iota((CH * across, chunk))
     for first in range(0, weight_ref.shape[1], chunk):
         span = pl.ds(first, chunk)
-        sums = velocity_chunk(
-            quads, place_ref, table, [offset], cell_ref, weight_ref, row_iota, span
+        *sums, solid = chunk_sums(
+            quads,
+            place_ref,
+            table,
+            place_offsets(quads)[half:],
+            4,
+            cell_ref,
+            weight_ref,
+            row_iota,
+            span,
         )
+        factor = mass_of(count_ref, volume_ref, first, span)
+        factor = factor * (1.0 + (solid + solid_ref[0:1, span])) ** 2
         for component, value in enumerate(sums):
             one = pl.ds(component, 1)
-            for partial in earlier:
-                value = value + partial[one, span]
-            out_ref[one, span] = value
-
-
-def drag_kernel(quads, chunk, place_ref, cell_ref, weight_ref, velocity_ref, factor_ref, *refs):
-    sampled_ref, held_ref, got_ref, pressure_ref, drag_ref, gathered = refs
-    across, own = quads * CA, CB // quads
-    half = quads // 2
-    offsets = place_offsets(quads)[half:]
-    tables = [velocity_table(got_ref[index], across, own) for index in range(half)]
-    tables = jnp.concatenate(tables, axis=0)
-    row_iota = short_iota((CH * across, chunk))
-    for first in range(0, weight_ref.shape[1], chunk):
-        span = pl.ds(first, chunk)
-        sums = velocity_chunk(
-            quads, place_ref, tables, offsets, cell_ref, weight_ref, row_iota, span
-        )
-        for component, value in enumerate(sums):
-            one = pl.ds(component, 1)
-            drag_ref[one, span] = factor_ref[0:1, span] * (
+            drag_ref[one, span] = factor * (
                 value + sampled_ref[one, span] - velocity_ref[one, span]
             )
     shape = gathered.shape[1:]
@@ -421,6 +452,8 @@
     level = lax.axis_index("slab").astype(jnp.int32).reshape(1)
     weight = grain_weight.reshape(1, grains)
     volume = grain_volume.reshape(1, grains)
+
+    grain_chunk = min(grains, 512)
 
     def cells(*shape):
         return jax.ShapeDtypeStruct(shape, jnp.float32)
@@ -485,7 +518,7 @@
             cells(packed_rows(across, 2, reach(distance), own), LANES)
             for distance in range(1, DEPTH + 1)
         ]
-        + [cells(CH, tall, LANES)],
+        + [cells(CH * tall, LANES)],
         in_specs=[SMEM] + [VMEM] * 2,
         out_specs=[VMEM] * (DEPTH + 1),
         compiler_params=LIMIT,
@@ -501,47 +534,46 @@
     frame = cells(packed_rows(across, 1, SUBLANES, own) + 2 * tall, LANES)
     layers = CH * len(stack)
     two_rounds = FIRST < ITERS
-    centre = pl.pallas_call(
+    window = cells(layers, across, LANES)
+    centre, offset, gain = pl.pallas_call(
         functools.partial(relax_kernel, quads),
-        out_shape=cells(packed_rows(across, 1, SUBLANES, own), LANES)
-        if two_rounds
-        else frame,
+        out_shape=[
+            cells(packed_rows(across, 1, SUBLANES, own), LANES) if two_rounds else frame,
+            window,
+            window,
+        ],
         in_specs=[SMEM] + [VMEM] * len(stack),
-        out_specs=VMEM,
-        scratch_shapes=[pltpu.VMEM((layers, across, LANES), jnp.float32)] * 4,
+        out_specs=[VMEM] * 3,
+        scratch_shapes=[pltpu.VMEM(window.shape, window.dtype)] * 2,
         compiler_params=LIMIT,
         name="relax",
     )(level, *stack)
     centre, solids = lax.optimization_barrier((centre, solids))
-    solids = [solids, over_quad(last, solids)]
-    factor = pl.pallas_call(
-        functools.partial(factor_kernel, quads, min(grains, 512)),
+    solid_sampled = pl.pallas_call(
+        functools.partial(solid_kernel, quads, grain_chunk),
         out_shape=cells(1, grains),
-        in_specs=[SMEM, SMEM] + [VMEM] * 5,
+        in_specs=[SMEM] + [VMEM] * 3,
         out_specs=VMEM,
-        scratch_shapes=[pltpu.VMEM((quads,) + solid.shape, jnp.float32)],
         compiler_params=LIMIT,
         cost_estimate=pl.CostEstimate(
-            flops=4 * CB * CH * across * grains, bytes_accessed=2**20, transcendentals=0
+            flops=8 * own * CH * across * grains, bytes_accessed=2**20, transcendentals=0
         ),
-        name="factor",
-    )(place, grain_count, grain_cell, weight, volume, *solids)
+        name="solid",
+    )(place, grain_cell, weight, solids)
 
     mine = centre
     if two_rounds:
         pressures = [centre] + [swapped(*swap, centre) for swap in swap_plan(1)]
-        pressures, factor = lax.optimization_barrier((pressures, factor))
+        pressures, solid_sampled = lax.optimization_barrier((pressures, solid_sampled))
         mine = pl.pallas_call(
             functools.partial(finish_kernel, quads),
             out_shape=frame,
-            in_specs=[SMEM] + [VMEM] * 6,
+            in_specs=[SMEM] + [VMEM] * 5,
             out_specs=VMEM,
-            scratch_shapes=[pltpu.VMEM((3 * CH, across, LANES), jnp.float32)] * 4,
+            scratch_shapes=[pltpu.VMEM((3 * CH, across, LANES), jnp.float32)] * 2,
             compiler_params=LIMIT,
             name="finish",
-        )(level, *stack[:3], *pressures)
-
-    grain_chunk = min(grains, 512)
+        )(level, offset, gain, *pressures)
 
     def sampled_from(held, index, *earlier):
         return pl.pallas_call(
@@ -566,16 +598,27 @@
         held, partial = lax.optimization_barrier((held, partial))
         for index in range(known, held.shape[0]):
             partial = sampled_from(held, index, partial)
-    got = over_quad(last, held)
+    got = over_quad(last, jnp.concatenate([held, solids], axis=1))
     pressure, drag = pl.pallas_call(
         functools.partial(drag_kernel, quads, grain_chunk),
         out_shape=[cells(CH, CA, CB), cells(3, grains)],
-        in_specs=[SMEM] + [VMEM] * 7,
+        in_specs=[SMEM] * 2 + [VMEM] * 8,
         out_specs=[VMEM] * 2,
         scratch_shapes=[pltpu.VMEM((quads, CH, tall, LANES), jnp.float32)],
         compiler_params=LIMIT,
         name="drag",
-    )(place, grain_cell, weight, grain_velocity, factor, partial, held, got)
+    )(
+        place,
+        grain_count,
+        grain_cell,
+        weight,
+        volume,
+        grain_velocity,
+        solid_sampled,
+        partial,
+        held,
+        got,
+    )
     return pressure, drag
 
 

time: 59.7 us -> 60 us (level)
  starting transfers between devices: 20.1 us -> 21.7 us
  waiting for transfers between devices: 14.3 us -> 13.3 us
    ppermute x6 -> x5, starting transfers between devices: 7.27 us -> 10 us  [over_quad(): return lax.ppermute(value, 'quad', pairs)]
    ppermute x6, starting transfers between devices: 12.8 us -> 11.7 us  [swapped(): lax.ppermute(value, 'slab', pairs + [(high, low) for low, high in pairs])]
    pallas_call x1, Pallas kernels: 4.88 us -> 5.95 us  [body(): pl.pallas_call(functools.partial(drag_kernel, quads, grain_chunk), out_sh...]
    pallas_call x2, Pallas kernels: 5.47 us -> 4.49 us  [the longest x1 2.58 us: body(): pl.pallas_call(functools.partial(relax_kernel, quads), out_shape=[cells(p...]
    ppermute x6 -> x5, waiting for transfers between devices: 7.15 us -> 6.51 us  [over_quad(): return lax.ppermute(value, 'quad', pairs)]
  transfers between devices with their start and end apart: 12 -> 11, of which waited for: 6 -> 5; matrix products, arithmetic and copies ran while one was open for 0% -> 0% of each run, Pallas kernels for 17% -> 15%
where the time goes in v3:
time: 60 us; the launch traced here: 59.8 us
  Pallas kernels  23.1 us (38%)
  starting transfers between devices  21.7 us (36%)
  waiting for transfers between devices  13.3 us (22%)
  between operations  1.49 us (2%)
    ppermute x6, starting transfers between devices, swapped(): lax.ppermute(value, 'slab', pairs + [(high, low) for low, high in pairs])  11.7 us
    ppermute x5, starting transfers between devices, over_quad(): return lax.ppermute(value, 'quad', pairs)  10 us
    ppermute x6, waiting for transfers between devices, swapped(): lax.ppermute(value, 'slab', pairs + [(high, low) for low, high in pairs])  6.82 us
    pallas_call x1, Pallas kernels, body(): pl.pallas_call(functools.partial(deposit_kernel, quads, min(grains, 2048)...  6.8 us
    ppermute x5, waiting for transfers between devices, over_quad(): return lax.ppermute(value, 'quad', pairs)  6.51 us
    pallas_call x1, Pallas kernels, body(): pl.pallas_call(functools.partial(drag_kernel, quads, grain_chunk), out_sh...  5.95 us
    pallas_call x2, Pallas kernels, sampled_from(): pl.pallas_call(functools.partial(sampled_kernel, quads, grain_chunk, plac...  4.38 us
    pallas_call x1, Pallas kernels, body(): pl.pallas_call(functools.partial(relax_kernel, quads), out_shape=[cells(p...  2.58 us
  transfers between devices with their start and end apart: 11, of which 5 were waited for; matrix products, arithmetic and copies ran while one was open for 0% of the time, Pallas kernels for 15%

profile of v3, /device:TPU:9, one launch (start us, length us, event | category | flops | bytes accessed | tf_op | source)
XLA Modules:
  0.0 59.8 jit_solution(509177510125110139)
XLA Ops:
  1.3 6.8 %deposit.1 = (f32[2,384,128]{2,1,0:T(8,128)S(1)}, f32[2,384,128]{2,1,0:T(8,128)S(1)}) custom-call(s32[1]{0:T(128)} %bitcast.place_ref, s32[1]{0:T(128)S(6)} %copy.7.count_ref, s32[4,8192]{1,0:T(4,128)} %cell_ref.7, f32[1,8192]{1,0:T(1,128)} %bitcast.9, f32[1,8192]{1,0:T(1,128)} %bitcast.14, f32[3,8192]{1,0:T(4,128)} %refs_0_.3), custom_call_target="tpu_custom_call" | custom-call | tf_op jit(solution)/shard_map/deposit/pallas_call | solution.py:485
  8.1 0.7 %collective-permute-start = (f32[2,384,128]{2,1,0:T(8,128)S(1)}, f32[2,384,128]{2,1,0:T(8,128)S(1)}, u32[]{:S(2)}, u32[]{:S(2)}) collective-permute-start(f32[2,384,128]{2,1,0:T(8,128)S(1)} %get-tuple-element.21), channel_id=1, source_target_pairs={{0,1},{1,0},{2,3},{3,2},{4,5},{5,4},{6,7},{7,6},{8,9},{9,8},{10,11... | collective-permute-start | bytes 1179656 | tf_op jit(solution)/shard_map/ppermute | solution.py:463
  8.8 1.3 %collective-permute-done = f32[2,384,128]{2,1,0:T(8,128)S(1)} collective-permute-done((f32[2,384,128]{2,1,0:T(8,128)S(1)}, f32[2,384,128]{2,1,0:T(8,128)S(1)}, u32[]{:S(2)}, u32[]{:S(2)}) %collective-permute-start) | collective-permute-done | bytes 393248 | tf_op jit(solution)/shard_map/ppermute | solution.py:463
  10.3 1.3 %collective-permute-start.1 = (f32[1,384,128]{2,1,0:T(8,128)S(1)}, f32[1,384,128]{2,1,0:T(8,128)S(1)}, u32[]{:S(2)}, u32[]{:S(2)}) collective-permute-start(f32[1,384,128]{2,1,0:T(8,128)S(1)} %get-tuple-element.38), channel_id=1, source_target_pairs={{0,2},{1,3},{2,0},{3,1},{4,6},{5,7},{6,4},{7,5},{8,10},{9,11},{10,... | collective-permute-start | bytes 589832 | tf_op jit(solution)/shard_map/ppermute | solution.py:463
  11.5 4.9 %collective-permute-done.1.got_ref = f32[1,384,128]{2,1,0:T(8,128)S(1)} collective-permute-done((f32[1,384,128]{2,1,0:T(8,128)S(1)}, f32[1,384,128]{2,1,0:T(8,128)S(1)}, u32[]{:S(2)}, u32[]{:S(2)}) %collective-permute-start.1) | collective-permute-done | bytes 196640 | tf_op jit(solution)/shard_map/ppermute | solution.py:463
  16.4 0.5 coefficients.1
  17.0 3.2 %collective-permute-start.5 = (f32[320,128]{1,0:T(8,128)S(1)}, f32[320,128]{1,0:T(8,128)S(1)}, u32[]{:S(2)}, u32[]{:S(2)}) collective-permute-start(f32[320,128]{1,0:T(8,128)S(1)} %get-tuple-element.23), channel_id=1, source_target_pairs={{8,16},{12,20},{16,8},{20,12},{9,17},{13,21},{17,9},{21,13},{10,18... | collective-permute-start | bytes 491528 | tf_op jit(solution)/shard_map/ppermute | solution.py:472
  20.2 1.3 %collective-permute-start.2 = (f32[384,128]{1,0:T(8,128)S(1)}, f32[384,128]{1,0:T(8,128)S(1)}, u32[]{:S(2)}, u32[]{:S(2)}) collective-permute-start(f32[384,128]{1,0:T(8,128)S(1)} %get-tuple-element.22.own_ref), channel_id=1, source_target_pairs={{0,4},{8,12},{16,20},{24,28},{4,0},{12,8},{20,16},{28,24},{1,5},{9... | collective-permute-start | bytes 589832 | tf_op jit(solution)/shard_map/ppermute | solution.py:472
  21.5 1.9 %collective-permute-start.3 = (f32[384,128]{1,0:T(8,128)S(1)}, f32[384,128]{1,0:T(8,128)S(1)}, u32[]{:S(2)}, u32[]{:S(2)}) collective-permute-start(f32[384,128]{1,0:T(8,128)S(1)} %get-tuple-element.22.own_ref), channel_id=1, source_target_pairs={{4,8},{12,16},{20,24},{8,4},{16,12},{24,20},{5,9},{13,17},{21,25},... | collective-permute-start | bytes 589832 | tf_op jit(solution)/shard_map/ppermute | solution.py:472
  23.4 0.1 collective-permute-start.4
  23.5 0.0 collective-permute-done.5.refs_3_
  23.5 1.3 %collective-permute-start.6 = (f32[1,128,128]{2,1,0:T(8,128)S(1)}, f32[1,128,128]{2,1,0:T(8,128)S(1)}, u32[]{:S(2)}, u32[]{:S(2)}) collective-permute-start(f32[1,128,128]{2,1,0:T(8,128)S(1)} %bitcast.16), channel_id=1, source_target_pairs={{0,2},{1,3},{2,0},{3,1},{4,6},{5,7},{6,4},{7,5},{8,10},{9,11},{10,... | collective-permute-start | bytes 196616 | tf_op jit(solution)/shard_map/ppermute | solution.py:463
  24.8 4.8 %collective-permute-done.4.refs_2_ = f32[320,128]{1,0:T(8,128)S(1)} collective-permute-done((f32[320,128]{1,0:T(8,128)S(1)}, f32[320,128]{1,0:T(8,128)S(1)}, u32[]{:S(2)}, u32[]{:S(2)}) %collective-permute-start.4) | collective-permute-done | bytes 163872 | tf_op jit(solution)/shard_map/ppermute | solution.py:472
  29.6 0.0 collective-permute-done.2.refs_0_
  29.6 0.0 collective-permute-done.3.refs_1_
  29.6 2.6 %relax.1 = (f32[160,128]{1,0:T(8,128)S(1)}, f32[20,64,128]{2,1,0:T(8,128)S(1)}, f32[20,64,128]{2,1,0:T(8,128)S(1)}) custom-call(s32[1]{0:T(128)} %bitcast.3.slab_ref, f32[384,128]{1,0:T(8,128)S(1)} %get-tuple-element.22.own_ref, f32[384,128]{1,0:T(8,128)S(1)} %collective-permute-done.2.refs_0_, f32[384,128]{1,0:T(8,128)S(1)} %collective-permute-done.3.refs_1_, ...), custom_call_target="tpu_custom_call" | custom-call | tf_op jit(solution)/shard_map/relax/pallas_call | solution.py:538
  32.2 0.0 copy-start
  32.2 0.0 copy-start.2
  32.2 0.0 collective-permute-done.6
  32.3 3.1 %collective-permute-start.7 = (f32[160,128]{1,0:T(8,128)S(1)}, f32[160,128]{1,0:T(8,128)S(1)}, u32[]{:S(2)}, u32[]{:S(2)}) collective-permute-start(f32[160,128]{1,0:T(8,128)S(1)} %get-tuple-element.33.refs_0_), channel_id=1, source_target_pairs={{0,4},{8,12},{16,20},{24,28},{4,0},{12,8},{20,16},{28,24},{1,5},{9... | collective-permute-start | bytes 245768 | tf_op jit(solution)/shard_map/ppermute | solution.py:472
  35.4 2.1 %collective-permute-start.8 = (f32[160,128]{1,0:T(8,128)S(1)}, f32[160,128]{1,0:T(8,128)S(1)}, u32[]{:S(2)}, u32[]{:S(2)}) collective-permute-start(f32[160,128]{1,0:T(8,128)S(1)} %get-tuple-element.33.refs_0_), channel_id=1, source_target_pairs={{4,8},{12,16},{20,24},{8,4},{16,12},{24,20},{5,9},{13,17},{21,25},... | collective-permute-start | bytes 245768 | tf_op jit(solution)/shard_map/ppermute | solution.py:472
  37.5 0.0 copy-done
  37.5 0.0 copy-done.2
  37.5 1.9 %solid.1.refs_1_ = f32[1,8192]{1,0:T(1,128)S(1)} custom-call(s32[1]{0:T(128)} %bitcast.place_ref, s32[4,8192]{1,0:T(4,128)S(1)} %copy-done, f32[1,8192]{1,0:T(1,128)S(1)} %bitcast.10, f32[2,128,128]{2,1,0:T(8,128)S(1)} %pad_maximum_fusion.2.held_ref), custom_call_target="tpu_custom_call" | custom-call | flops 1073741824 | bytes 1048576 | tf_op jit(solution)/shard_map/solid/pallas_call | solution.py:552
  39.5 0.0 collective-permute-done.7.refs_1_
  39.5 2.0 %collective-permute-done.8.refs_2_ = f32[160,128]{1,0:T(8,128)S(1)} collective-permute-done((f32[160,128]{1,0:T(8,128)S(1)}, f32[160,128]{1,0:T(8,128)S(1)}, u32[]{:S(2)}, u32[]{:S(2)}) %collective-permute-start.8) | collective-permute-done | bytes 81952 | tf_op jit(solution)/shard_map/ppermute | solution.py:472
  41.4 0.9 %finish.1 = f32[224,128]{1,0:T(8,128)S(1)} custom-call(s32[1]{0:T(128)} %bitcast.3.slab_ref, f32[20,64,128]{2,1,0:T(8,128)S(1)} %get-tuple-element.31.offset_ref, f32[20,64,128]{2,1,0:T(8,128)S(1)} %get-tuple-element.32.gain_ref, f32[160,128]{1,0:T(8,128)S(1)} %get-tuple-element.33.refs_0_, f32[160,128]{1,0:T(8,128)S(1)} %collective-permute-done.7.refs_1_, ...), custom_call_target="tpu_custom_call" | custom-call | tf_op jit(solution)/shard_map/finish/pallas_call | solution.py:568
  42.4 1.3 %collective-permute-start.9 = (f32[1,224,128]{2,1,0:T(8,128)S(1)}, f32[1,224,128]{2,1,0:T(8,128)S(1)}, u32[]{:S(2)}, u32[]{:S(2)}) collective-permute-start(f32[1,224,128]{2,1,0:T(8,128)S(1)} %bitcast.6), channel_id=1, source_target_pairs={{0,2},{1,3},{2,0},{3,1},{4,6},{5,7},{6,4},{7,5},{8,10},{9,11},{10,... | collective-permute-start | bytes 344072 | tf_op jit(solution)/shard_map/ppermute | solution.py:463
  43.6 2.2 %sampled.2.refs_0_ = f32[3,8192]{1,0:T(4,128)S(1)} custom-call(s32[1]{0:T(128)} %bitcast.place_ref, s32[4,8192]{1,0:T(4,128)S(1)} %copy-done, f32[1,8192]{1,0:T(1,128)S(1)} %bitcast.11, f32[1,224,128]{2,1,0:T(8,128)S(1)} %bitcast.7), custom_call_target="tpu_custom_call" | custom-call | flops 1610612736 | bytes 1048576 | tf_op jit(solution)/shard_map/sampled/pallas_call | solution.py:579
  45.8 0.2 collective-permute-done.9
  46.1 0.0 copy-start.1
  46.1 0.0 copy-start.3
  46.1 5.4 %collective-permute-start.10 = (f32[2,352,128]{2,1,0:T(8,128)S(1)}, f32[2,352,128]{2,1,0:T(8,128)S(1)}, u32[]{:S(2)}, u32[]{:S(2)}) collective-permute-start(f32[2,352,128]{2,1,0:T(8,128)S(1)} %pad_maximum_fusion), channel_id=1, source_target_pairs={{0,1},{1,0},{2,3},{3,2},{4,5},{5,4},{6,7},{7,6},{8,9},{9,8},{10,11... | collective-permute-start | bytes 1081352 | tf_op jit(solution)/shard_map/ppermute | solution.py:463
  51.6 2.2 %sampled.3.refs_2_ = f32[3,8192]{1,0:T(4,128)S(1)} custom-call(s32[1]{0:T(128)} %bitcast.place_ref, s32[4,8192]{1,0:T(4,128)S(1)} %copy-done, f32[1,8192]{1,0:T(1,128)S(1)} %bitcast.12, f32[2,224,128]{2,1,0:T(8,128)S(1)} %pad_maximum_fusion.1.held_ref.refs_3_, f32[3,8192]{1,0:T(4,128)S(1)} %sampled.2.refs_0_), custom_call_target="tpu_custom_call" | custom-call | flops 1610612736 | bytes 1048576 | tf_op jit(solution)/shard_map/sampled/pallas_call | solution.py:579
  53.8 0.0 collective-permute-done.10.refs_4_
  53.8 0.0 copy-done.1
  53.8 0.0 copy-done.3
  53.8 5.9 %drag.1 = (f32[4,16,256]{2,1,0:T(8,128)}, f32[3,8192]{1,0:T(4,128)}) custom-call(s32[1]{0:T(128)} %bitcast.place_ref, s32[1]{0:T(128)S(6)} %copy.7.count_ref, s32[4,8192]{1,0:T(4,128)S(1)} %copy-done, f32[1,8192]{1,0:T(1,128)S(1)} %bitcast.13, f32[1,8192]{1,0:T(1,128)S(1)} %bitcast.15, f32[3,8192]{1,0:T(4,128)S(1)} %copy-done.1, ...), custom_call_target="tpu_custom_call" | custom-call | tf_op jit(solution)/shard_map/drag/pallas_call | solution.py:602
  (5 shorter events, 0.1 us)
Async XLA Ops:
  8.1 2.1 %collective-permute-start = (f32[2,384,128]{2,1,0:T(8,128)S(1)}, f32[2,384,128]{2,1,0:T(8,128)S(1)}, u32[]{:S(2)}, u32[]{:S(2)}) collective-permute-start(f32[2,384,128]{2,1,0:T(8,128)S(1)} %get-tuple-element.21), channel_id=1, source_target_pairs={{0,1},{1,0},{2,3},{3,2},{4,5},{5,4},{6,7},{7,6},{8,9},{9,8},{10,11... | collective-permute-start | bytes 1179656 | tf_op jit(solution)/shard_map/ppermute | solution.py:463
  10.3 6.2 %collective-permute-start.1 = (f32[1,384,128]{2,1,0:T(8,128)S(1)}, f32[1,384,128]{2,1,0:T(8,128)S(1)}, u32[]{:S(2)}, u32[]{:S(2)}) collective-permute-start(f32[1,384,128]{2,1,0:T(8,128)S(1)} %get-tuple-element.38), channel_id=1, source_target_pairs={{0,2},{1,3},{2,0},{3,1},{4,6},{5,7},{6,4},{7,5},{8,10},{9,11},{10,... | collective-permute-start | bytes 589832 | tf_op jit(solution)/shard_map/ppermute | solution.py:463
  17.0 6.5 %collective-permute-start.5 = (f32[320,128]{1,0:T(8,128)S(1)}, f32[320,128]{1,0:T(8,128)S(1)}, u32[]{:S(2)}, u32[]{:S(2)}) collective-permute-start(f32[320,128]{1,0:T(8,128)S(1)} %get-tuple-element.23), channel_id=1, source_target_pairs={{8,16},{12,20},{16,8},{20,12},{9,17},{13,21},{17,9},{21,13},{10,18... | collective-permute-start | bytes 491528 | tf_op jit(solution)/shard_map/ppermute | solution.py:472
  20.2 9.4 %collective-permute-start.2 = (f32[384,128]{1,0:T(8,128)S(1)}, f32[384,128]{1,0:T(8,128)S(1)}, u32[]{:S(2)}, u32[]{:S(2)}) collective-permute-start(f32[384,128]{1,0:T(8,128)S(1)} %get-tuple-element.22.own_ref), channel_id=1, source_target_pairs={{0,4},{8,12},{16,20},{24,28},{4,0},{12,8},{20,16},{28,24},{1,5},{9... | collective-permute-start | bytes 589832 | tf_op jit(solution)/shard_map/ppermute | solution.py:472
  21.5 8.1 %collective-permute-start.3 = (f32[384,128]{1,0:T(8,128)S(1)}, f32[384,128]{1,0:T(8,128)S(1)}, u32[]{:S(2)}, u32[]{:S(2)}) collective-permute-start(f32[384,128]{1,0:T(8,128)S(1)} %get-tuple-element.22.own_ref), channel_id=1, source_target_pairs={{4,8},{12,16},{20,24},{8,4},{16,12},{24,20},{5,9},{13,17},{21,25},... | collective-permute-start | bytes 589832 | tf_op jit(solution)/shard_map/ppermute | solution.py:472
  23.4 6.2 %collective-permute-start.4 = (f32[320,128]{1,0:T(8,128)S(1)}, f32[320,128]{1,0:T(8,128)S(1)}, u32[]{:S(2)}, u32[]{:S(2)}) collective-permute-start(f32[320,128]{1,0:T(8,128)S(1)} %get-tuple-element.23), channel_id=1, source_target_pairs={{0,8},{4,12},{16,24},{20,28},{8,0},{12,4},{24,16},{28,20},{1,9},{5... | collective-permute-start | bytes 491528 | tf_op jit(solution)/shard_map/ppermute | solution.py:472
  23.5 8.7 %collective-permute-start.6 = (f32[1,128,128]{2,1,0:T(8,128)S(1)}, f32[1,128,128]{2,1,0:T(8,128)S(1)}, u32[]{:S(2)}, u32[]{:S(2)}) collective-permute-start(f32[1,128,128]{2,1,0:T(8,128)S(1)} %bitcast.16), channel_id=1, source_target_pairs={{0,2},{1,3},{2,0},{3,1},{4,6},{5,7},{6,4},{7,5},{8,10},{9,11},{10,... | collective-permute-start | bytes 196616 | tf_op jit(solution)/shard_map/ppermute | solution.py:463
  32.2 5.3 %copy-start = (s32[4,8192]{1,0:T(4,128)S(1)}, s32[4,8192]{1,0:T(4,128)}, u32[]{:S(2)}) copy-start(s32[4,8192]{1,0:T(4,128)} %cell_ref.7) | copy-start | bytes 393220
  32.2 5.3 %copy-start.2 = (f32[8192]{0:T(1024)S(1)}, f32[8192]{0:T(1024)}, u32[]{:S(2)}) copy-start(f32[8192]{0:T(1024)} %param.7) | copy-start | bytes 98308
  32.3 7.2 %collective-permute-start.7 = (f32[160,128]{1,0:T(8,128)S(1)}, f32[160,128]{1,0:T(8,128)S(1)}, u32[]{:S(2)}, u32[]{:S(2)}) collective-permute-start(f32[160,128]{1,0:T(8,128)S(1)} %get-tuple-element.33.refs_0_), channel_id=1, source_target_pairs={{0,4},{8,12},{16,20},{24,28},{4,0},{12,8},{20,16},{28,24},{1,5},{9... | collective-permute-start | bytes 245768 | tf_op jit(solution)/shard_map/ppermute | solution.py:472
  35.4 6.1 %collective-permute-start.8 = (f32[160,128]{1,0:T(8,128)S(1)}, f32[160,128]{1,0:T(8,128)S(1)}, u32[]{:S(2)}, u32[]{:S(2)}) collective-permute-start(f32[160,128]{1,0:T(8,128)S(1)} %get-tuple-element.33.refs_0_), channel_id=1, source_target_pairs={{4,8},{12,16},{20,24},{8,4},{16,12},{24,20},{5,9},{13,17},{21,25},... | collective-permute-start | bytes 245768 | tf_op jit(solution)/shard_map/ppermute | solution.py:472
  42.4 3.7 %collective-permute-start.9 = (f32[1,224,128]{2,1,0:T(8,128)S(1)}, f32[1,224,128]{2,1,0:T(8,128)S(1)}, u32[]{:S(2)}, u32[]{:S(2)}) collective-permute-start(f32[1,224,128]{2,1,0:T(8,128)S(1)} %bitcast.6), channel_id=1, source_target_pairs={{0,2},{1,3},{2,0},{3,1},{4,6},{5,7},{6,4},{7,5},{8,10},{9,11},{10,... | collective-permute-start | bytes 344072 | tf_op jit(solution)/shard_map/ppermute | solution.py:463
  46.1 7.7 %copy-start.1 = (f32[3,8192]{1,0:T(4,128)S(1)}, f32[3,8192]{1,0:T(4,128)}, u32[]{:S(2)}) copy-start(f32[3,8192]{1,0:T(4,128)} %refs_0_.3) | copy-start | bytes 294916
  46.1 7.7 %copy-start.3 = (f32[8192]{0:T(1024)S(1)}, f32[8192]{0:T(1024)}, u32[]{:S(2)}) copy-start(f32[8192]{0:T(1024)} %param.8) | copy-start | bytes 98308
  46.1 7.7 %collective-permute-start.10 = (f32[2,352,128]{2,1,0:T(8,128)S(1)}, f32[2,352,128]{2,1,0:T(8,128)S(1)}, u32[]{:S(2)}, u32[]{:S(2)}) collective-permute-start(f32[2,352,128]{2,1,0:T(8,128)S(1)} %pad_maximum_fusion), channel_id=1, source_target_pairs={{0,1},{1,0},{2,3},{3,2},{4,5},{5,4},{6,7},{7,6},{8,9},{9,8},{10,11... | collective-permute-start | bytes 1081352 | tf_op jit(solution)/shard_map/ppermute | solution.py:463

commit v4 on v3

--- a/solution.py
+++ b/solution.py
@@ -13,8 +13,7 @@
 ITERS = 12
 LANES = 128
 SUBLANES = 8
-DEPTH = 2
-FIRST = CH * DEPTH + 1
+DEPTH = 3
 
 damping = 0.05
 source_gain = 4.0
@@ -249,31 +248,8 @@
         offset_ref[span] = offset
         even_ref[span] = offset
         gain_ref[span] = gain
-    sweeps = min(FIRST, ITERS) - 1
-    last = sweep_over(sweeps, layers, across, even_ref, odd_ref, offset_ref, gain_ref)
-    if FIRST < ITERS:
-        out_ref[...] = pack([last[DEPTH * CH : (DEPTH + 1) * CH]], SUBLANES, own)
-    else:
-        out_ref[...] = framed(last, DEPTH * CH, own)
-
-
-def finish_kernel(quads, slab_ref, offset_ref, gain_ref, *refs):
-    *parts, out_ref, even_ref, odd_ref = refs
-    across, own = quads * CA, CB // quads
-    slots = [1] + [1 + slot_of(slab_ref[0], *swap) for swap in swap_plan(1)]
-    for slot, pressure in zip(slots, parts):
-        (even_ref[pl.ds(slot * CH, CH)],) = unpack(pressure[...], 1, across, SUBLANES, own)
-    near = pl.ds((DEPTH - 1) * CH, 3 * CH)
-    last = sweep_over(
-        ITERS - FIRST,
-        3 * CH,
-        across,
-        even_ref,
-        odd_ref,
-        offset_ref.at[near],
-        gain_ref.at[near],
-    )
-    out_ref[...] = framed(last, CH, own)
+    last = sweep_over(ITERS - 1, layers, across, even_ref, odd_ref, offset_ref, gain_ref)
+    out_ref[...] = framed(last, DEPTH * CH, own)
 
 
 def halving(quads):
@@ -529,26 +505,7 @@
         swapped(distance, matching, coefs[distance - 1])
         for distance, matching in swap_plan(DEPTH)
     ]
-    stack[-1], solid = lax.optimization_barrier((stack[-1], solid))
     solids = nearly_all(solid)
-    frame = cells(packed_rows(across, 1, SUBLANES, own) + 2 * tall, LANES)
-    layers = CH * len(stack)
-    two_rounds = FIRST < ITERS
-    window = cells(layers, across, LANES)
-    centre, offset, gain = pl.pallas_call(
-        functools.partial(relax_kernel, quads),
-        out_shape=[
-            cells(packed_rows(across, 1, SUBLANES, own), LANES) if two_rounds else frame,
-            window,
-            window,
-        ],
-        in_specs=[SMEM] + [VMEM] * len(stack),
-        out_specs=[VMEM] * 3,
-        scratch_shapes=[pltpu.VMEM(window.shape, window.dtype)] * 2,
-        compiler_params=LIMIT,
-        name="relax",
-    )(level, *stack)
-    centre, solids = lax.optimization_barrier((centre, solids))
     solid_sampled = pl.pallas_call(
         functools.partial(solid_kernel, quads, grain_chunk),
         out_shape=cells(1, grains),
@@ -560,20 +517,18 @@
         ),
         name="solid",
     )(place, grain_cell, weight, solids)
-
-    mine = centre
-    if two_rounds:
-        pressures = [centre] + [swapped(*swap, centre) for swap in swap_plan(1)]
-        pressures, solid_sampled = lax.optimization_barrier((pressures, solid_sampled))
-        mine = pl.pallas_call(
-            functools.partial(finish_kernel, quads),
-            out_shape=frame,
-            in_specs=[SMEM] + [VMEM] * 5,
-            out_specs=VMEM,
-            scratch_shapes=[pltpu.VMEM((3 * CH, across, LANES), jnp.float32)] * 2,
-            compiler_params=LIMIT,
-            name="finish",
-        )(level, offset, gain, *pressures)
+    stack, solid_sampled = lax.optimization_barrier((stack, solid_sampled))
+
+    window = pltpu.VMEM((CH * len(stack), across, LANES), jnp.float32)
+    mine = pl.pallas_call(
+        functools.partial(relax_kernel, quads),
+        out_shape=cells(packed_rows(across, 1, SUBLANES, own) + 2 * tall, LANES),
+        in_specs=[SMEM] + [VMEM] * len(stack),
+        out_specs=VMEM,
+        scratch_shapes=[window] * 4,
+        compiler_params=LIMIT,
+        name="relax",
+    )(level, *stack)
 
     def sampled_from(held, index, *earlier):
         return pl.pallas_call(

time: 60 us -> 60.9 us (1.015)
  starting transfers between devices: 21.7 us -> 19.5 us
  waiting for transfers between devices: 13.3 us -> 14.9 us
  Pallas kernels: 23.1 us -> 24.3 us
    ppermute x5, starting transfers between devices: 10 us -> 6.68 us  [over_quad(): return lax.ppermute(value, 'quad', pairs)]
    ppermute x6, starting transfers between devices: 11.7 us -> 12.8 us  [swapped(): lax.ppermute(value, 'slab', pairs + [(high, low) for low, high in pairs])]
    ppermute x5, waiting for transfers between devices: 6.51 us -> 7.46 us  [over_quad(): return lax.ppermute(value, 'quad', pairs)]
    pallas_call x2 -> x1, Pallas kernels: 3.49 us -> 4.33 us  [body(): pl.pallas_call(functools.partial(relax_kernel, quads), out_shape=cells(pa...]
  transfers between devices with their start and end apart: 11 -> 11, of which waited for: 5 -> 6; matrix products, arithmetic and copies ran while one was open for 0% -> 0% of each run, Pallas kernels for 15% -> 10%
where the time goes in v4:
time: 60.9 us; the launch traced here: 60.3 us
  Pallas kernels  24.3 us (40%)
  starting transfers between devices  19.5 us (32%)
  waiting for transfers between devices  14.9 us (24%)
  between operations  1.49 us (2%)
    ppermute x6, starting transfers between devices, swapped(): lax.ppermute(value, 'slab', pairs + [(high, low) for low, high in pairs])  12.8 us
    ppermute x5, waiting for transfers between devices, over_quad(): return lax.ppermute(value, 'quad', pairs)  7.46 us
    ppermute x6, waiting for transfers between devices, swapped(): lax.ppermute(value, 'slab', pairs + [(high, low) for low, high in pairs])  7.42 us
    pallas_call x1, Pallas kernels, body(): pl.pallas_call(functools.partial(deposit_kernel, quads, min(grains, 2048)...  6.8 us
    ppermute x5, starting transfers between devices, over_quad(): return lax.ppermute(value, 'quad', pairs)  6.68 us
    pallas_call x1, Pallas kernels, body(): pl.pallas_call(functools.partial(drag_kernel, quads, grain_chunk), out_sh...  6.18 us
    pallas_call x2, Pallas kernels, sampled_from(): pl.pallas_call(functools.partial(sampled_kernel, quads, grain_chunk, plac...  4.37 us
    pallas_call x1, Pallas kernels, body(): pl.pallas_call(functools.partial(relax_kernel, quads), out_shape=cells(pa...  4.33 us
  transfers between devices with their start and end apart: 11, of which 6 were waited for; matrix products, arithmetic and copies ran while one was open for 0% of the time, Pallas kernels for 10%

profile of v4, /device:TPU:9, one launch (start us, length us, event | category | flops | bytes accessed | tf_op | source)
XLA Modules:
  0.0 60.3 jit_solution(13462443174943942600)
XLA Ops:
  1.3 6.8 %deposit.1 = (f32[2,384,128]{2,1,0:T(8,128)S(1)}, f32[2,384,128]{2,1,0:T(8,128)S(1)}) custom-call(s32[1]{0:T(128)} %bitcast.place_ref, s32[1]{0:T(128)S(6)} %copy.7.count_ref, s32[4,8192]{1,0:T(4,128)} %cell_ref.7, f32[1,8192]{1,0:T(1,128)} %bitcast.12, f32[1,8192]{1,0:T(1,128)} %bitcast.17, f32[3,8192]{1,0:T(4,128)} %refs_0_.3), custom_call_target="tpu_custom_call" | custom-call | tf_op jit(solution)/shard_map/deposit/pallas_call | solution.py:461
  8.1 0.7 %collective-permute-start = (f32[2,384,128]{2,1,0:T(8,128)S(1)}, f32[2,384,128]{2,1,0:T(8,128)S(1)}, u32[]{:S(2)}, u32[]{:S(2)}) collective-permute-start(f32[2,384,128]{2,1,0:T(8,128)S(1)} %get-tuple-element.19), channel_id=1, source_target_pairs={{0,1},{1,0},{2,3},{3,2},{4,5},{5,4},{6,7},{7,6},{8,9},{9,8},{10,11... | collective-permute-start | bytes 1179656 | tf_op jit(solution)/shard_map/ppermute | solution.py:439
  8.8 1.3 %collective-permute-done = f32[2,384,128]{2,1,0:T(8,128)S(1)} collective-permute-done((f32[2,384,128]{2,1,0:T(8,128)S(1)}, f32[2,384,128]{2,1,0:T(8,128)S(1)}, u32[]{:S(2)}, u32[]{:S(2)}) %collective-permute-start) | collective-permute-done | bytes 393248 | tf_op jit(solution)/shard_map/ppermute | solution.py:439
  10.3 1.3 %collective-permute-start.1 = (f32[1,384,128]{2,1,0:T(8,128)S(1)}, f32[1,384,128]{2,1,0:T(8,128)S(1)}, u32[]{:S(2)}, u32[]{:S(2)}) collective-permute-start(f32[1,384,128]{2,1,0:T(8,128)S(1)} %get-tuple-element.34), channel_id=1, source_target_pairs={{0,2},{1,3},{2,0},{3,1},{4,6},{5,7},{6,4},{7,5},{8,10},{9,11},{10,... | collective-permute-start | bytes 589832 | tf_op jit(solution)/shard_map/ppermute | solution.py:439
  11.5 4.9 %collective-permute-done.1.got_ref = f32[1,384,128]{2,1,0:T(8,128)S(1)} collective-permute-done((f32[1,384,128]{2,1,0:T(8,128)S(1)}, f32[1,384,128]{2,1,0:T(8,128)S(1)}, u32[]{:S(2)}, u32[]{:S(2)}) %collective-permute-start.1) | collective-permute-done | bytes 196640 | tf_op jit(solution)/shard_map/ppermute | solution.py:439
  16.4 0.7 %coefficients.1 = (f32[384,128]{1,0:T(8,128)S(1)}, f32[320,128]{1,0:T(8,128)S(1)}, f32[288,128]{1,0:T(8,128)S(1)}, f32[128,128]{1,0:T(8,128)S(1)}) custom-call(s32[1]{0:T(128)} %bitcast.place_ref, f32[1,384,128]{2,1,0:T(8,128)S(1)} %get-tuple-element.35.kept_ref, f32[1,384,128]{2,1,0:T(8,128)S(1)} %collective-permute-done.1.got_ref), custom_call_target="tpu_custom_call" | custom-call | tf_op jit(solution)/shard_map/coefficients/pallas_call | solution.py:491
  17.1 0.7 %collective-permute-start.7 = (f32[288,128]{1,0:T(8,128)S(1)}, f32[288,128]{1,0:T(8,128)S(1)}, u32[]{:S(2)}, u32[]{:S(2)}) collective-permute-start(f32[288,128]{1,0:T(8,128)S(1)} %get-tuple-element.22), channel_id=1, source_target_pairs={{12,24},{16,28},{24,12},{28,16},{13,25},{17,29},{25,13},{29,17},{1... | collective-permute-start | bytes 442376 | tf_op jit(solution)/shard_map/ppermute | solution.py:448
  17.8 1.3 %collective-permute-start.8 = (f32[1,128,128]{2,1,0:T(8,128)S(1)}, f32[1,128,128]{2,1,0:T(8,128)S(1)}, u32[]{:S(2)}, u32[]{:S(2)}) collective-permute-start(f32[1,128,128]{2,1,0:T(8,128)S(1)} %bitcast.9), channel_id=1, source_target_pairs={{0,2},{1,3},{2,0},{3,1},{4,6},{5,7},{6,4},{7,5},{8,10},{9,11},{10,... | collective-permute-start | bytes 196616 | tf_op jit(solution)/shard_map/ppermute | solution.py:439
  19.1 4.1 %collective-permute-start.6 = (f32[288,128]{1,0:T(8,128)S(1)}, f32[288,128]{1,0:T(8,128)S(1)}, u32[]{:S(2)}, u32[]{:S(2)}) collective-permute-start(f32[288,128]{1,0:T(8,128)S(1)} %get-tuple-element.22), channel_id=1, source_target_pairs={{0,12},{4,16},{8,20},{12,0},{16,4},{20,8},{1,13},{5,17},{9,21},{13... | collective-permute-start | bytes 442376 | tf_op jit(solution)/shard_map/ppermute | solution.py:448
  23.3 4.5 %collective-permute-start.5 = (f32[320,128]{1,0:T(8,128)S(1)}, f32[320,128]{1,0:T(8,128)S(1)}, u32[]{:S(2)}, u32[]{:S(2)}) collective-permute-start(f32[320,128]{1,0:T(8,128)S(1)} %get-tuple-element.21), channel_id=1, source_target_pairs={{8,16},{12,20},{16,8},{20,12},{9,17},{13,21},{17,9},{21,13},{10,18... | collective-permute-start | bytes 491528 | tf_op jit(solution)/shard_map/ppermute | solution.py:448
  27.7 0.1 collective-permute-start.4
  27.8 0.0 collective-permute-done.8
  27.8 0.0 copy-start
  27.8 0.0 copy-start.2
  27.8 3.3 %collective-permute-start.3 = (f32[384,128]{1,0:T(8,128)S(1)}, f32[384,128]{1,0:T(8,128)S(1)}, u32[]{:S(2)}, u32[]{:S(2)}) collective-permute-start(f32[384,128]{1,0:T(8,128)S(1)} %get-tuple-element.25.own_ref), channel_id=1, source_target_pairs={{4,8},{12,16},{20,24},{8,4},{16,12},{24,20},{5,9},{13,17},{21,25},... | collective-permute-start | bytes 589832 | tf_op jit(solution)/shard_map/ppermute | solution.py:448
  31.1 0.0 collective-permute-done.7.refs_5_
  31.2 0.2 collective-permute-start.2
  31.3 0.0 copy-done
  31.4 0.0 copy-done.2
  31.4 1.9 %solid.1.refs_1_ = f32[1,8192]{1,0:T(1,128)S(1)} custom-call(s32[1]{0:T(128)} %bitcast.place_ref, s32[4,8192]{1,0:T(4,128)S(1)} %copy-done, f32[1,8192]{1,0:T(1,128)S(1)} %bitcast.13, f32[2,128,128]{2,1,0:T(8,128)S(1)} %pad_maximum_fusion.1.held_ref), custom_call_target="tpu_custom_call" | custom-call | flops 1073741824 | bytes 1048576 | tf_op jit(solution)/shard_map/solid/pallas_call | solution.py:509
  33.3 0.0 collective-permute-done.6.refs_4_
  33.3 0.0 collective-permute-done.5.refs_3_
  33.3 0.7 %collective-permute-done.4.refs_2_ = f32[320,128]{1,0:T(8,128)S(1)} collective-permute-done((f32[320,128]{1,0:T(8,128)S(1)}, f32[320,128]{1,0:T(8,128)S(1)}, u32[]{:S(2)}, u32[]{:S(2)}) %collective-permute-start.4) | collective-permute-done | bytes 163872 | tf_op jit(solution)/shard_map/ppermute | solution.py:448
  34.0 3.5 %collective-permute-done.3.refs_1_ = f32[384,128]{1,0:T(8,128)S(1)} collective-permute-done((f32[384,128]{1,0:T(8,128)S(1)}, f32[384,128]{1,0:T(8,128)S(1)}, u32[]{:S(2)}, u32[]{:S(2)}) %collective-permute-start.3) | collective-permute-done | bytes 196640 | tf_op jit(solution)/shard_map/ppermute | solution.py:448
  37.5 3.2 %collective-permute-done.2.refs_0_ = f32[384,128]{1,0:T(8,128)S(1)} collective-permute-done((f32[384,128]{1,0:T(8,128)S(1)}, f32[384,128]{1,0:T(8,128)S(1)}, u32[]{:S(2)}, u32[]{:S(2)}) %collective-permute-start.2) | collective-permute-done | bytes 196640 | tf_op jit(solution)/shard_map/ppermute | solution.py:448
  40.7 4.3 %relax.1 = f32[224,128]{1,0:T(8,128)S(1)} custom-call(s32[1]{0:T(128)} %bitcast.4.slab_ref, f32[384,128]{1,0:T(8,128)S(1)} %get-tuple-element.25.own_ref, f32[384,128]{1,0:T(8,128)S(1)} %collective-permute-done.2.refs_0_, f32[384,128]{1,0:T(8,128)S(1)} %collective-permute-done.3.refs_1_, f32[320,128]{1,0:T(8,128)S(1)} %collective-permute-done.4.refs_2_, ...), custom_call_target="tpu_custom_call" | custom-call | tf_op jit(solution)/shard_map/relax/pallas_call | solution.py:523
  45.0 0.3 collective-permute-start.9
  45.4 2.2 %sampled.2.refs_0_ = f32[3,8192]{1,0:T(4,128)S(1)} custom-call(s32[1]{0:T(128)} %bitcast.place_ref, s32[4,8192]{1,0:T(4,128)S(1)} %copy-done, f32[1,8192]{1,0:T(1,128)S(1)} %bitcast.14, f32[1,224,128]{2,1,0:T(8,128)S(1)} %bitcast.7), custom_call_target="tpu_custom_call" | custom-call | flops 1610612736 | bytes 1048576 | tf_op jit(solution)/shard_map/sampled/pallas_call | solution.py:534
  47.6 1.2 %collective-permute-done.9 = f32[1,224,128]{2,1,0:T(8,128)S(1)} collective-permute-done((f32[1,224,128]{2,1,0:T(8,128)S(1)}, f32[1,224,128]{2,1,0:T(8,128)S(1)}, u32[]{:S(2)}, u32[]{:S(2)}) %collective-permute-start.9) | collective-permute-done | bytes 114720 | tf_op jit(solution)/shard_map/ppermute | solution.py:439
  48.8 0.0 copy-start.1
  48.8 0.0 copy-start.3
  48.8 3.1 %collective-permute-start.10 = (f32[2,352,128]{2,1,0:T(8,128)S(1)}, f32[2,352,128]{2,1,0:T(8,128)S(1)}, u32[]{:S(2)}, u32[]{:S(2)}) collective-permute-start(f32[2,352,128]{2,1,0:T(8,128)S(1)} %maximum_maximum_fusion), channel_id=1, source_target_pairs={{0,1},{1,0},{2,3},{3,2},{4,5},{5,4},{6,7},{7,6},{8,9},{9,8},{10,11... | collective-permute-start | bytes 1081352 | tf_op jit(solution)/shard_map/ppermute | solution.py:439
  51.9 2.2 %sampled.3.refs_2_ = f32[3,8192]{1,0:T(4,128)S(1)} custom-call(s32[1]{0:T(128)} %bitcast.place_ref, s32[4,8192]{1,0:T(4,128)S(1)} %copy-done, f32[1,8192]{1,0:T(1,128)S(1)} %bitcast.15, f32[2,224,128]{2,1,0:T(8,128)S(1)} %pad_maximum_fusion.held_ref.refs_3_, f32[3,8192]{1,0:T(4,128)S(1)} %sampled.2.refs_0_), custom_call_target="tpu_custom_call" | custom-call | flops 1610612736 | bytes 1048576 | tf_op jit(solution)/shard_map/sampled/pallas_call | solution.py:534
  54.1 0.0 collective-permute-done.10.refs_4_
  54.1 0.0 copy-done.1
  54.1 0.0 copy-done.3
  54.1 6.2 %drag.1 = (f32[4,16,256]{2,1,0:T(8,128)}, f32[3,8192]{1,0:T(4,128)}) custom-call(s32[1]{0:T(128)} %bitcast.place_ref, s32[1]{0:T(128)S(6)} %copy.7.count_ref, s32[4,8192]{1,0:T(4,128)S(1)} %copy-done, f32[1,8192]{1,0:T(1,128)S(1)} %bitcast.16, f32[1,8192]{1,0:T(1,128)S(1)} %bitcast.18, f32[3,8192]{1,0:T(4,128)S(1)} %copy-done.1, ...), custom_call_target="tpu_custom_call" | custom-call | tf_op jit(solution)/shard_map/drag/pallas_call | solution.py:557
  (5 shorter events, 0.1 us)
Async XLA Ops:
  8.1 2.1 %collective-permute-start = (f32[2,384,128]{2,1,0:T(8,128)S(1)}, f32[2,384,128]{2,1,0:T(8,128)S(1)}, u32[]{:S(2)}, u32[]{:S(2)}) collective-permute-start(f32[2,384,128]{2,1,0:T(8,128)S(1)} %get-tuple-element.19), channel_id=1, source_target_pairs={{0,1},{1,0},{2,3},{3,2},{4,5},{5,4},{6,7},{7,6},{8,9},{9,8},{10,11... | collective-permute-start | bytes 1179656 | tf_op jit(solution)/shard_map/ppermute | solution.py:439
  10.3 6.2 %collective-permute-start.1 = (f32[1,384,128]{2,1,0:T(8,128)S(1)}, f32[1,384,128]{2,1,0:T(8,128)S(1)}, u32[]{:S(2)}, u32[]{:S(2)}) collective-permute-start(f32[1,384,128]{2,1,0:T(8,128)S(1)} %get-tuple-element.34), channel_id=1, source_target_pairs={{0,2},{1,3},{2,0},{3,1},{4,6},{5,7},{6,4},{7,5},{8,10},{9,11},{10,... | collective-permute-start | bytes 589832 | tf_op jit(solution)/shard_map/ppermute | solution.py:439
  17.1 14.0 %collective-permute-start.7 = (f32[288,128]{1,0:T(8,128)S(1)}, f32[288,128]{1,0:T(8,128)S(1)}, u32[]{:S(2)}, u32[]{:S(2)}) collective-permute-start(f32[288,128]{1,0:T(8,128)S(1)} %get-tuple-element.22), channel_id=1, source_target_pairs={{12,24},{16,28},{24,12},{28,16},{13,25},{17,29},{25,13},{29,17},{1... | collective-permute-start | bytes 442376 | tf_op jit(solution)/shard_map/ppermute | solution.py:448
  17.8 10.0 %collective-permute-start.8 = (f32[1,128,128]{2,1,0:T(8,128)S(1)}, f32[1,128,128]{2,1,0:T(8,128)S(1)}, u32[]{:S(2)}, u32[]{:S(2)}) collective-permute-start(f32[1,128,128]{2,1,0:T(8,128)S(1)} %bitcast.9), channel_id=1, source_target_pairs={{0,2},{1,3},{2,0},{3,1},{4,6},{5,7},{6,4},{7,5},{8,10},{9,11},{10,... | collective-permute-start | bytes 196616 | tf_op jit(solution)/shard_map/ppermute | solution.py:439
  19.1 14.2 %collective-permute-start.6 = (f32[288,128]{1,0:T(8,128)S(1)}, f32[288,128]{1,0:T(8,128)S(1)}, u32[]{:S(2)}, u32[]{:S(2)}) collective-permute-start(f32[288,128]{1,0:T(8,128)S(1)} %get-tuple-element.22), channel_id=1, source_target_pairs={{0,12},{4,16},{8,20},{12,0},{16,4},{20,8},{1,13},{5,17},{9,21},{13... | collective-permute-start | bytes 442376 | tf_op jit(solution)/shard_map/ppermute | solution.py:448
  23.3 10.0 %collective-permute-start.5 = (f32[320,128]{1,0:T(8,128)S(1)}, f32[320,128]{1,0:T(8,128)S(1)}, u32[]{:S(2)}, u32[]{:S(2)}) collective-permute-start(f32[320,128]{1,0:T(8,128)S(1)} %get-tuple-element.21), channel_id=1, source_target_pairs={{8,16},{12,20},{16,8},{20,12},{9,17},{13,21},{17,9},{21,13},{10,18... | collective-permute-start | bytes 491528 | tf_op jit(solution)/shard_map/ppermute | solution.py:448
  27.7 6.3 %collective-permute-start.4 = (f32[320,128]{1,0:T(8,128)S(1)}, f32[320,128]{1,0:T(8,128)S(1)}, u32[]{:S(2)}, u32[]{:S(2)}) collective-permute-start(f32[320,128]{1,0:T(8,128)S(1)} %get-tuple-element.21), channel_id=1, source_target_pairs={{0,8},{4,12},{16,24},{20,28},{8,0},{12,4},{24,16},{28,20},{1,9},{5... | collective-permute-start | bytes 491528 | tf_op jit(solution)/shard_map/ppermute | solution.py:448
  27.8 3.5 %copy-start = (s32[4,8192]{1,0:T(4,128)S(1)}, s32[4,8192]{1,0:T(4,128)}, u32[]{:S(2)}) copy-start(s32[4,8192]{1,0:T(4,128)} %cell_ref.7) | copy-start | bytes 393220
  27.8 3.5 %copy-start.2 = (f32[8192]{0:T(1024)S(1)}, f32[8192]{0:T(1024)}, u32[]{:S(2)}) copy-start(f32[8192]{0:T(1024)} %param.7) | copy-start | bytes 98308
  27.8 9.6 %collective-permute-start.3 = (f32[384,128]{1,0:T(8,128)S(1)}, f32[384,128]{1,0:T(8,128)S(1)}, u32[]{:S(2)}, u32[]{:S(2)}) collective-permute-start(f32[384,128]{1,0:T(8,128)S(1)} %get-tuple-element.25.own_ref), channel_id=1, source_target_pairs={{4,8},{12,16},{20,24},{8,4},{16,12},{24,20},{5,9},{13,17},{21,25},... | collective-permute-start | bytes 589832 | tf_op jit(solution)/shard_map/ppermute | solution.py:448
  31.2 9.6 %collective-permute-start.2 = (f32[384,128]{1,0:T(8,128)S(1)}, f32[384,128]{1,0:T(8,128)S(1)}, u32[]{:S(2)}, u32[]{:S(2)}) collective-permute-start(f32[384,128]{1,0:T(8,128)S(1)} %get-tuple-element.25.own_ref), channel_id=1, source_target_pairs={{0,4},{8,12},{16,20},{24,28},{4,0},{12,8},{20,16},{28,24},{1,5},{9... | collective-permute-start | bytes 589832 | tf_op jit(solution)/shard_map/ppermute | solution.py:448
  45.0 3.7 %collective-permute-start.9 = (f32[1,224,128]{2,1,0:T(8,128)S(1)}, f32[1,224,128]{2,1,0:T(8,128)S(1)}, u32[]{:S(2)}, u32[]{:S(2)}) collective-permute-start(f32[1,224,128]{2,1,0:T(8,128)S(1)} %bitcast.6), channel_id=1, source_target_pairs={{0,2},{1,3},{2,0},{3,1},{4,6},{5,7},{6,4},{7,5},{8,10},{9,11},{10,... | collective-permute-start | bytes 344072 | tf_op jit(solution)/shard_map/ppermute | solution.py:439
  48.8 5.3 %copy-start.1 = (f32[3,8192]{1,0:T(4,128)S(1)}, f32[3,8192]{1,0:T(4,128)}, u32[]{:S(2)}) copy-start(f32[3,8192]{1,0:T(4,128)} %refs_0_.3) | copy-start | bytes 294916
  48.8 5.3 %copy-start.3 = (f32[8192]{0:T(1024)S(1)}, f32[8192]{0:T(1024)}, u32[]{:S(2)}) copy-start(f32[8192]{0:T(1024)} %param.8) | copy-start | bytes 98308
  48.8 5.3 %collective-permute-start.10 = (f32[2,352,128]{2,1,0:T(8,128)S(1)}, f32[2,352,128]{2,1,0:T(8,128)S(1)}, u32[]{:S(2)}, u32[]{:S(2)}) collective-permute-start(f32[2,352,128]{2,1,0:T(8,128)S(1)} %maximum_maximum_fusion), channel_id=1, source_target_pairs={{0,1},{1,0},{2,3},{3,2},{4,5},{5,4},{6,7},{7,6},{8,9},{9,8},{10,11... | collective-permute-start | bytes 1081352 | tf_op jit(solution)/shard_map/ppermute | solution.py:439

commit v5 on v3

--- a/solution.py
+++ b/solution.py
@@ -135,66 +135,81 @@
     return jnp.where(slot < count_ref[0], volume, 0.0)
 
 
-def deposit_kernel(quads, chunk, place_ref, count_ref, *refs):
-    sources, outs = refs[:4], refs[4:6]
-    cell_ref, weight_ref, volume_ref, velocity_ref, sems = refs[6:]
+def grain_kernel(quads, count_ref, *refs):
+    sources, out_ref, targets, sems = refs[:4], refs[4], refs[5:9], refs[9]
     copies = [
         pltpu.make_async_copy(source, target, sems.at[index])
-        for index, (source, target) in enumerate(
-            zip(sources, (cell_ref, weight_ref, volume_ref, velocity_ref))
-        )
+        for index, (source, target) in enumerate(zip(sources, targets))
     ]
     for copy in copies:
         copy.start()
-    across = quads * CA
-    rows = CH * across
-    grains = weight_ref.shape[1]
-    own = CB // quads
-    row_iota = short_iota((rows, chunk))
-    col_iota = short_iota((CB, chunk))
-    total = jnp.zeros((4 * CB, rows), jnp.float32)
     for copy in copies:
         copy.wait()
-    for first in range(0, grains, chunk):
+    cell_ref, weight_ref, volume_ref, velocity_ref = targets
+    span = pl.ds(0, weight_ref.shape[1])
+    mass = mass_of(count_ref, volume_ref, 0, span)
+    flat = row_of(cell_ref, span, quads * CA) * CB + cell_ref[3:4, span]
+    out_ref[0:1, :] = flat.astype(jnp.float32)
+    out_ref[1:2, :] = weight_ref[...]
+    out_ref[2:3, :] = mass
+    out_ref[3:4, :] = mass * velocity_ref[0:1, span]
+
+
+def deposit_into(total, quads, chunk, place_ref, grain_ref):
+    own = CB // quads
+    halo = reach(0)
+    rows = CH * quads * CA
+    size = own + 2 * halo
+    row_iota = short_iota((rows, chunk))
+    iota = lax.broadcasted_iota(jnp.int32, (size, chunk), 0)
+    col_iota = jnp.where(iota < own + halo, iota, iota - size).astype(jnp.int16)
+    for first in range(0, grain_ref.shape[1], chunk):
         span = pl.ds(first, chunk)
-        mass = mass_of(count_ref, volume_ref, first, span)
-        moment = mass * velocity_ref[0:1, span]
-        lower = weight_ref[0:1, span]
+        flat = grain_ref[0:1, span]
+        row = jnp.floor(flat * (1.0 / CB))
+        col = (flat - row * CB).astype(jnp.int32) - place_ref[0] * own
+        lower = grain_ref[1:2, span]
         upper = 1.0 - lower
-        hot = one_hot(row_iota, row_of(cell_ref, span, across))
-        col = cell_ref[3:4, span]
+        hot = one_hot(row_iota, row.astype(jnp.int32))
         at_lower = col_iota == col.astype(jnp.int16)
         at_upper = col_iota == (col + 1).astype(jnp.int16)
         parts = []
-        for amount in (mass, moment):
+        for amount in (grain_ref[2:3, span], grain_ref[3:4, span]):
             for low, high in zip(halves(amount * lower), halves(amount * upper)):
                 parts.append(jnp.where(at_lower, low, jnp.where(at_upper, high, jnp.bfloat16(0))))
-        spread = jnp.concatenate(parts, axis=0)
-        total = total + lax.dot_general(
-            spread, hot, (((1,), (1,)), ((), ())), preferred_element_type=jnp.float32
+        product = lax.dot_general(
+            jnp.concatenate(parts, axis=0),
+            hot,
+            (((1,), (1,)), ((), ())),
+            preferred_element_type=jnp.float32,
         )
-    lane = lanes_of((CH, across, LANES))
-    fields = [
-        (total[base : base + CB] + total[base + CB : base + 2 * CB]).T
-        for base in range(0, 4 * CB, 2 * CB)
-    ]
-    for step in range(quads):
-        target = place_ref[0] ^ step
-        windows = []
-        for field in fields:
-            moved = pltpu.roll(field, lax.rem(CB - target * own, CB), 1)
-            moved = moved.reshape(CH, across, CB)
-            near, past = moved[:, :, :LANES], moved[:, :, CB - LANES :]
-            windows.append(jnp.where(lane < (LANES + own) // 2, near, past))
-        outs[step % 2][step // 2] = pack(windows, reach(0), own)
-
-
-def coefficient_kernel(quads, place_ref, kept_ref, got_ref, *refs):
-    outs, solid_ref = refs[:-1], refs[-1]
+        total = product if total is None else total + product
+    return total
+
+
+def deposit_kernel(quads, chunk, place_ref, grain_ref, *refs):
+    *earlier, out_ref = refs
+    total = earlier[0][...] if earlier else None
+    out_ref[...] = deposit_into(total, quads, chunk, place_ref, grain_ref)
+
+
+def coefficient_kernel(quads, chunk, place_ref, *refs):
+    half = quads // 2
+    grains, total_ref, outs, solid_ref = refs[:half], refs[half], refs[half + 1 : -1], refs[-1]
     across, own = quads * CA, CB // quads
-    total = kept_ref[0] + got_ref[0]
-    solid_ref[...] = total[: solid_ref.shape[0]]
-    solid, moment = unpack(total, 2, across, reach(0), own)
+    total = total_ref[...]
+    for grain_ref in grains:
+        total = deposit_into(total, quads, chunk, place_ref, grain_ref)
+    halo = reach(0)
+    size = own + 2 * halo
+    windows = []
+    for base in range(0, 4 * size, 2 * size):
+        field = total[base : base + size] + total[base + size : base + 2 * size]
+        gap = jnp.zeros((LANES - size, field.shape[1]), jnp.float32)
+        field = jnp.concatenate([field[: own + halo], gap, field[own + halo :]], axis=0)
+        windows.append(field.T.reshape(CH, across, LANES))
+    solid, moment = windows
+    solid_ref[...] = pack_own(solid, own).reshape(solid_ref.shape)
     lane = lanes_of(solid.shape)
     column = jnp.where(lane < (LANES + own) // 2, lane, lane - LANES) + place_ref[0] * own
     inside = (column >= 0) & (column < CB)
@@ -285,25 +300,6 @@
     for bit in halving(quads):
         offsets += [offset ^ bit for offset in offsets]
     return offsets
-
-
-def whole_table(quads, place_ref, parts, gathered):
-    own = CB // quads
-    pieces = LANES // own
-    for offset, part in zip(place_offsets(quads), parts):
-        gathered[place_ref[0] ^ offset] = part
-    lane = lanes_of(gathered.shape[1:])
-    bands = []
-    for piece in range(pieces):
-        columns = []
-        for first in range(0, quads, pieces):
-            block = None
-            for near in range(pieces):
-                part = turned(gathered[first + near], (near - piece) * own)
-                block = part if block is None else jnp.where(lane < near * own, block, part)
-            columns.append(block)
-        bands.append(jnp.concatenate(columns, axis=2))
-    return jnp.concatenate(bands, axis=1)
 
 
 def blend_of(col_iota, at, lower):
@@ -436,9 +432,19 @@
     parts = [
         ref[index][:count].reshape(shape) for ref in (held_ref, got_ref) for index in range(half)
     ]
-    pressure = whole_table(quads, place_ref, parts, gathered)
-    mine = pltpu.roll(pressure, lax.rem(across - place_ref[0] * CA, across), 1)
-    pressure_ref[...] = mine[:, :CA]
+    for offset, part in zip(place_offsets(quads), parts):
+        gathered[place_ref[0] ^ offset] = part
+    bands = shape[1] // CA
+    band = pl.ds(pl.multiple_of(lax.rem(place_ref[0], bands) * CA, SUBLANES), CA)
+    back = lax.rem(LANES - lax.div(place_ref[0], bands) * own, LANES)
+    lane = lanes_of((CH, CA, LANES))
+    pieces = LANES // own
+    for first in range(0, quads, pieces):
+        block = None
+        for near in range(pieces):
+            part = pltpu.roll(gathered[first + near, :, band, :], lax.rem(back + near * own, LANES), 2)
+            block = part if block is None else jnp.where(lane < near * own, block, part)
+        pressure_ref[:, :, first * own : first * own + LANES] = block
 
 
 def body(grain_cell, grain_count, grain_weight, grain_volume, grain_velocity):
@@ -482,11 +488,11 @@
     def pinned(value):
         return pltpu.with_memory_space_constraint(value, pltpu.HBM)
 
-    kept, sent = pl.pallas_call(
-        functools.partial(deposit_kernel, quads, min(grains, 2048)),
-        out_shape=[cells(quads // 2, packed_rows(across, 2, reach(0), own), LANES)] * 2,
-        in_specs=[SMEM, SMEM] + [HBM] * 4,
-        out_specs=[VMEM] * 2,
+    packed_grains = pl.pallas_call(
+        functools.partial(grain_kernel, quads),
+        out_shape=cells(4, grains),
+        in_specs=[SMEM] + [HBM] * 4,
+        out_specs=VMEM,
         scratch_shapes=[
             pltpu.VMEM((4, grains), jnp.int32),
             pltpu.VMEM((1, grains), jnp.float32),
@@ -495,35 +501,44 @@
             pltpu.SemaphoreType.DMA((4,)),
         ],
         compiler_params=LIMIT,
-        name="deposit",
+        name="grains",
     )(
-        place,
         grain_count,
         pinned(grain_cell),
         pinned(weight),
         pinned(volume),
         pinned(grain_velocity),
     )
-
-    bit = 1
-    got = over_quad(bit, sent)
-    while kept.shape[0] > 1:
-        bit *= 2
-        total = kept + got
-        kept, sent = total[0::2], total[1::2]
-        got = over_quad(bit, sent)
+    half = quads // 2
+    others = [over_quad(step, packed_grains) for step in reversed(range(1, quads))][::-1]
+    size = own + 2 * reach(0)
+    deposit_chunk = min(grains, 2048)
+    total = None
+    for arrived in [packed_grains] + others[: half - 1]:
+        earlier = [] if total is None else [total]
+        total = pl.pallas_call(
+            functools.partial(deposit_kernel, quads, deposit_chunk),
+            out_shape=cells(4 * size, CH * across),
+            in_specs=[SMEM] + [VMEM] * (1 + len(earlier)),
+            out_specs=VMEM,
+            compiler_params=LIMIT,
+            cost_estimate=pl.CostEstimate(
+                flops=8 * size * CH * across * grains, bytes_accessed=2**20, transcendentals=0
+            ),
+            name="deposit",
+        )(place, arrived, *earlier)
     *coefs, solid = pl.pallas_call(
-        functools.partial(coefficient_kernel, quads),
+        functools.partial(coefficient_kernel, quads, deposit_chunk),
         out_shape=[
             cells(packed_rows(across, 2, reach(distance), own), LANES)
             for distance in range(1, DEPTH + 1)
         ]
         + [cells(CH * tall, LANES)],
-        in_specs=[SMEM] + [VMEM] * 2,
+        in_specs=[SMEM] + [VMEM] * (half + 1),
         out_specs=[VMEM] * (DEPTH + 1),
         compiler_params=LIMIT,
         name="coefficients",
-    )(place, kept, got)
+    )(place, *others[half - 1 :], total)
 
     stack = [coefs[0]] + [
         swapped(distance, matching, coefs[distance - 1])

time: 60 us -> 57.4 us (0.957)
  waiting for transfers between devices: 13.3 us -> 9.69 us
  Pallas kernels: 23.1 us -> 24.6 us
    ppermute x5 -> x6, waiting for transfers between devices: 6.51 us -> 1.91 us  [over_quad(): return lax.ppermute(value, 'quad', pairs)]
    pallas_call x2 -> x4, Pallas kernels: 7.35 us -> 8.92 us  [the longest x1 4.01 us: body(): pl.pallas_call(functools.partial(coefficient_kernel, quads, deposit_chunk...]
    ppermute x6, waiting for transfers between devices: 6.82 us -> 7.78 us  [swapped(): lax.ppermute(value, 'slab', pairs + [(high, low) for low, high in pairs])]
    ppermute x5 -> x6, starting transfers between devices: 10 us -> 9.34 us  [over_quad(): return lax.ppermute(value, 'quad', pairs)]
  transfers between devices with their start and end apart: 11 -> 12, of which waited for: 5 -> 4; matrix products, arithmetic and copies ran while one was open for 0% -> 0% of each run, Pallas kernels for 15% -> 22%
where the time goes in v5:
time: 57.4 us; the launch traced here: 57.2 us
  Pallas kernels  24.6 us (43%)
  starting transfers between devices  21.4 us (37%)
  waiting for transfers between devices  9.69 us (17%)
  between operations  1.51 us (3%)
    ppermute x6, starting transfers between devices, swapped(): lax.ppermute(value, 'slab', pairs + [(high, low) for low, high in pairs])  12 us
    ppermute x6, starting transfers between devices, over_quad(): return lax.ppermute(value, 'quad', pairs)  9.34 us
    ppermute x6, waiting for transfers between devices, swapped(): lax.ppermute(value, 'slab', pairs + [(high, low) for low, high in pairs])  7.78 us
    pallas_call x1, Pallas kernels, body(): pl.pallas_call(functools.partial(drag_kernel, quads, grain_chunk), out_sh...  5.9 us
    pallas_call x2, Pallas kernels, sampled_from(): pl.pallas_call(functools.partial(sampled_kernel, quads, grain_chunk, plac...  4.37 us
    pallas_call x1, Pallas kernels, body(): pl.pallas_call(functools.partial(coefficient_kernel, quads, deposit_chunk...  4.01 us
    pallas_call x2, Pallas kernels, body(): pl.pallas_call(functools.partial(deposit_kernel, quads, deposit_chunk), o...  3.79 us
    pallas_call x1, Pallas kernels, body(): pl.pallas_call(functools.partial(relax_kernel, quads), out_shape=[cells(p...  2.58 us
  transfers between devices with their start and end apart: 12, of which 4 were waited for; matrix products, arithmetic and copies ran while one was open for 0% of the time, Pallas kernels for 22%

profile of v5, /device:TPU:9, one launch (start us, length us, event | category | flops | bytes accessed | tf_op | source)
XLA Modules:
  0.0 57.2 jit_solution(8988575305313341774)
XLA Ops:
  1.3 1.1 %grains.1.grain_ref = f32[4,8192]{1,0:T(4,128)S(1)} custom-call(s32[1]{0:T(128)S(6)} %copy.7.count_ref, s32[4,8192]{1,0:T(4,128)} %cell_ref.7, f32[1,8192]{1,0:T(1,128)} %bitcast.9, f32[1,8192]{1,0:T(1,128)} %bitcast.14, f32[3,8192]{1,0:T(4,128)} %refs_0_.3), custom_call_target="tpu_custom_call" | custom-call | tf_op jit(solution)/shard_map/grains/pallas_call | solution.py:491
  2.4 1.3 %collective-permute-start = (f32[4,8192]{1,0:T(4,128)S(1)}, f32[4,8192]{1,0:T(4,128)S(1)}, u32[]{:S(2)}, u32[]{:S(2)}) collective-permute-start(f32[4,8192]{1,0:T(4,128)S(1)} %grains.1.grain_ref), channel_id=1, source_target_pairs={{0,2},{1,3},{2,0},{3,1},{4,6},{5,7},{6,4},{7,5},{8,10},{9,11},{10,... | collective-permute-start | bytes 393224 | tf_op jit(solution)/shard_map/ppermute | solution.py:469
  3.7 1.1 %collective-permute-start.1 = (f32[4,8192]{1,0:T(4,128)S(1)}, f32[4,8192]{1,0:T(4,128)S(1)}, u32[]{:S(2)}, u32[]{:S(2)}) collective-permute-start(f32[4,8192]{1,0:T(4,128)S(1)} %grains.1.grain_ref), channel_id=1, source_target_pairs={{0,3},{1,2},{2,1},{3,0},{4,7},{5,6},{6,5},{7,4},{8,11},{9,10},{10,... | collective-permute-start | bytes 393224 | tf_op jit(solution)/shard_map/ppermute | solution.py:469
  4.8 0.0 collective-permute-start.2
  4.8 1.9 %deposit.2.refs_0_ = f32[384,256]{1,0:T(8,128)S(1)} custom-call(s32[1]{0:T(128)} %bitcast.place_ref, f32[4,8192]{1,0:T(4,128)S(1)} %grains.1.grain_ref), custom_call_target="tpu_custom_call" | custom-call | flops 1610612736 | bytes 1048576 | tf_op jit(solution)/shard_map/deposit/pallas_call | solution.py:519
  6.7 0.0 collective-permute-done.2.grain_ref
  6.7 1.9 %deposit.3.refs_2_ = f32[384,256]{1,0:T(8,128)S(1)} custom-call(s32[1]{0:T(128)} %bitcast.place_ref, f32[4,8192]{1,0:T(4,128)S(1)} %collective-permute-done.2.grain_ref, f32[384,256]{1,0:T(8,128)S(1)} %deposit.2.refs_0_), custom_call_target="tpu_custom_call" | custom-call | flops 1610612736 | bytes 1048576 | tf_op jit(solution)/shard_map/deposit/pallas_call | solution.py:519
  8.6 0.0 collective-permute-done.refs_0_
  8.6 1.9 %collective-permute-done.1.refs_1_ = f32[4,8192]{1,0:T(4,128)S(1)} collective-permute-done((f32[4,8192]{1,0:T(4,128)S(1)}, f32[4,8192]{1,0:T(4,128)S(1)}, u32[]{:S(2)}, u32[]{:S(2)}) %collective-permute-start.1) | collective-permute-done | bytes 131104 | tf_op jit(solution)/shard_map/ppermute | solution.py:469
  10.5 4.0 %coefficients.1 = (f32[384,128]{1,0:T(8,128)S(1)}, f32[320,128]{1,0:T(8,128)S(1)}, f32[128,128]{1,0:T(8,128)S(1)}) custom-call(s32[1]{0:T(128)} %bitcast.place_ref, f32[4,8192]{1,0:T(4,128)S(1)} %collective-permute-done.refs_0_, f32[4,8192]{1,0:T(4,128)S(1)} %collective-permute-done.1.refs_1_, f32[384,256]{1,0:T(8,128)S(1)} %deposit.3.refs_2_), custom_call_target="tpu_custom_call" | custom-call | tf_op jit(solution)/shard_map/coefficients/pallas_call | solution.py:530
  14.5 3.2 %collective-permute-start.6 = (f32[320,128]{1,0:T(8,128)S(1)}, f32[320,128]{1,0:T(8,128)S(1)}, u32[]{:S(2)}, u32[]{:S(2)}) collective-permute-start(f32[320,128]{1,0:T(8,128)S(1)} %get-tuple-element.19), channel_id=1, source_target_pairs={{8,16},{12,20},{16,8},{20,12},{9,17},{13,21},{17,9},{21,13},{10,18... | collective-permute-start | bytes 491528 | tf_op jit(solution)/shard_map/ppermute | solution.py:478
  17.7 1.3 %collective-permute-start.3 = (f32[384,128]{1,0:T(8,128)S(1)}, f32[384,128]{1,0:T(8,128)S(1)}, u32[]{:S(2)}, u32[]{:S(2)}) collective-permute-start(f32[384,128]{1,0:T(8,128)S(1)} %get-tuple-element.18.own_ref), channel_id=1, source_target_pairs={{0,4},{8,12},{16,20},{24,28},{4,0},{12,8},{20,16},{28,24},{1,5},{9... | collective-permute-start | bytes 589832 | tf_op jit(solution)/shard_map/ppermute | solution.py:478
  19.0 1.9 %collective-permute-start.4 = (f32[384,128]{1,0:T(8,128)S(1)}, f32[384,128]{1,0:T(8,128)S(1)}, u32[]{:S(2)}, u32[]{:S(2)}) collective-permute-start(f32[384,128]{1,0:T(8,128)S(1)} %get-tuple-element.18.own_ref), channel_id=1, source_target_pairs={{4,8},{12,16},{20,24},{8,4},{16,12},{24,20},{5,9},{13,17},{21,25},... | collective-permute-start | bytes 589832 | tf_op jit(solution)/shard_map/ppermute | solution.py:478
  21.0 0.1 collective-permute-start.5
  21.0 1.3 %collective-permute-done.6.refs_3_ = f32[320,128]{1,0:T(8,128)S(1)} collective-permute-done((f32[320,128]{1,0:T(8,128)S(1)}, f32[320,128]{1,0:T(8,128)S(1)}, u32[]{:S(2)}, u32[]{:S(2)}) %collective-permute-start.6) | collective-permute-done | bytes 163872 | tf_op jit(solution)/shard_map/ppermute | solution.py:478
  22.3 1.5 %collective-permute-start.7 = (f32[1,128,128]{2,1,0:T(8,128)S(1)}, f32[1,128,128]{2,1,0:T(8,128)S(1)}, u32[]{:S(2)}, u32[]{:S(2)}) collective-permute-start(f32[1,128,128]{2,1,0:T(8,128)S(1)} %bitcast.16), channel_id=1, source_target_pairs={{0,2},{1,3},{2,0},{3,1},{4,6},{5,7},{6,4},{7,5},{8,10},{9,11},{10,... | collective-permute-start | bytes 196616 | tf_op jit(solution)/shard_map/ppermute | solution.py:469
  23.9 4.7 %collective-permute-done.5.refs_2_ = f32[320,128]{1,0:T(8,128)S(1)} collective-permute-done((f32[320,128]{1,0:T(8,128)S(1)}, f32[320,128]{1,0:T(8,128)S(1)}, u32[]{:S(2)}, u32[]{:S(2)}) %collective-permute-start.5) | collective-permute-done | bytes 163872 | tf_op jit(solution)/shard_map/ppermute | solution.py:478
  28.6 0.0 collective-permute-done.3.refs_0_
  28.6 0.0 collective-permute-done.4.refs_1_
  28.6 2.6 %relax.1 = (f32[160,128]{1,0:T(8,128)S(1)}, f32[20,64,128]{2,1,0:T(8,128)S(1)}, f32[20,64,128]{2,1,0:T(8,128)S(1)}) custom-call(s32[1]{0:T(128)} %bitcast.3.slab_ref, f32[384,128]{1,0:T(8,128)S(1)} %get-tuple-element.18.own_ref, f32[384,128]{1,0:T(8,128)S(1)} %collective-permute-done.3.refs_0_, f32[384,128]{1,0:T(8,128)S(1)} %collective-permute-done.4.refs_1_, ...), custom_call_target="tpu_custom_call" | custom-call | tf_op jit(solution)/shard_map/relax/pallas_call | solution.py:553
  31.2 0.0 copy-start
  31.2 0.0 copy-start.2
  31.2 0.0 collective-permute-done.7
  31.2 3.2 %collective-permute-start.8 = (f32[160,128]{1,0:T(8,128)S(1)}, f32[160,128]{1,0:T(8,128)S(1)}, u32[]{:S(2)}, u32[]{:S(2)}) collective-permute-start(f32[160,128]{1,0:T(8,128)S(1)} %get-tuple-element.29.refs_0_), channel_id=1, source_target_pairs={{0,4},{8,12},{16,20},{24,28},{4,0},{12,8},{20,16},{28,24},{1,5},{9... | collective-permute-start | bytes 245768 | tf_op jit(solution)/shard_map/ppermute | solution.py:478
  34.4 2.4 %collective-permute-start.9 = (f32[160,128]{1,0:T(8,128)S(1)}, f32[160,128]{1,0:T(8,128)S(1)}, u32[]{:S(2)}, u32[]{:S(2)}) collective-permute-start(f32[160,128]{1,0:T(8,128)S(1)} %get-tuple-element.29.refs_0_), channel_id=1, source_target_pairs={{4,8},{12,16},{20,24},{8,4},{16,12},{24,20},{5,9},{13,17},{21,25},... | collective-permute-start | bytes 245768 | tf_op jit(solution)/shard_map/ppermute | solution.py:478
  36.7 0.0 copy-done
  36.8 0.0 copy-done.2
  36.8 1.9 %solid.1.refs_1_ = f32[1,8192]{1,0:T(1,128)S(1)} custom-call(s32[1]{0:T(128)} %bitcast.place_ref, s32[4,8192]{1,0:T(4,128)S(1)} %copy-done, f32[1,8192]{1,0:T(1,128)S(1)} %bitcast.10, f32[2,128,128]{2,1,0:T(8,128)S(1)} %pad_maximum_fusion.2.held_ref), custom_call_target="tpu_custom_call" | custom-call | flops 1073741824 | bytes 1048576 | tf_op jit(solution)/shard_map/solid/pallas_call | solution.py:567
  38.7 0.0 collective-permute-done.8.refs_1_
  38.7 1.8 %collective-permute-done.9.refs_2_ = f32[160,128]{1,0:T(8,128)S(1)} collective-permute-done((f32[160,128]{1,0:T(8,128)S(1)}, f32[160,128]{1,0:T(8,128)S(1)}, u32[]{:S(2)}, u32[]{:S(2)}) %collective-permute-start.9) | collective-permute-done | bytes 81952 | tf_op jit(solution)/shard_map/ppermute | solution.py:478
  40.4 0.9 %finish.1 = f32[224,128]{1,0:T(8,128)S(1)} custom-call(s32[1]{0:T(128)} %bitcast.3.slab_ref, f32[20,64,128]{2,1,0:T(8,128)S(1)} %get-tuple-element.27.offset_ref, f32[20,64,128]{2,1,0:T(8,128)S(1)} %get-tuple-element.28.gain_ref, f32[160,128]{1,0:T(8,128)S(1)} %get-tuple-element.29.refs_0_, f32[160,128]{1,0:T(8,128)S(1)} %collective-permute-done.8.refs_1_, ...), custom_call_target="tpu_custom_call" | custom-call | tf_op jit(solution)/shard_map/finish/pallas_call | solution.py:583
  41.4 1.7 %collective-permute-start.10 = (f32[1,224,128]{2,1,0:T(8,128)S(1)}, f32[1,224,128]{2,1,0:T(8,128)S(1)}, u32[]{:S(2)}, u32[]{:S(2)}) collective-permute-start(f32[1,224,128]{2,1,0:T(8,128)S(1)} %bitcast.6), channel_id=1, source_target_pairs={{0,2},{1,3},{2,0},{3,1},{4,6},{5,7},{6,4},{7,5},{8,10},{9,11},{10,... | collective-permute-start | bytes 344072 | tf_op jit(solution)/shard_map/ppermute | solution.py:469
  43.1 2.2 %sampled.2.refs_0_ = f32[3,8192]{1,0:T(4,128)S(1)} custom-call(s32[1]{0:T(128)} %bitcast.place_ref, s32[4,8192]{1,0:T(4,128)S(1)} %copy-done, f32[1,8192]{1,0:T(1,128)S(1)} %bitcast.11, f32[1,224,128]{2,1,0:T(8,128)S(1)} %bitcast.7), custom_call_target="tpu_custom_call" | custom-call | flops 1610612736 | bytes 1048576 | tf_op jit(solution)/shard_map/sampled/pallas_call | solution.py:594
  45.3 0.0 collective-permute-done.10
  45.4 0.0 copy-start.1
  45.4 0.0 copy-start.3
  45.4 3.7 %collective-permute-start.11 = (f32[2,352,128]{2,1,0:T(8,128)S(1)}, f32[2,352,128]{2,1,0:T(8,128)S(1)}, u32[]{:S(2)}, u32[]{:S(2)}) collective-permute-start(f32[2,352,128]{2,1,0:T(8,128)S(1)} %pad_maximum_fusion), channel_id=1, source_target_pairs={{0,1},{1,0},{2,3},{3,2},{4,5},{5,4},{6,7},{7,6},{8,9},{9,8},{10,11... | collective-permute-start | bytes 1081352 | tf_op jit(solution)/shard_map/ppermute | solution.py:469
  49.1 2.2 %sampled.3.refs_2_ = f32[3,8192]{1,0:T(4,128)S(1)} custom-call(s32[1]{0:T(128)} %bitcast.place_ref, s32[4,8192]{1,0:T(4,128)S(1)} %copy-done, f32[1,8192]{1,0:T(1,128)S(1)} %bitcast.12, f32[2,224,128]{2,1,0:T(8,128)S(1)} %pad_maximum_fusion.1.held_ref.refs_3_, f32[3,8192]{1,0:T(4,128)S(1)} %sampled.2.refs_0_), custom_call_target="tpu_custom_call" | custom-call | flops 1610612736 | bytes 1048576 | tf_op jit(solution)/shard_map/sampled/pallas_call | solution.py:594
  51.3 0.0 collective-permute-done.11.refs_4_
  51.3 0.0 copy-done.1
  51.3 0.0 copy-done.3
  51.3 5.9 %drag.1 = (f32[4,16,256]{2,1,0:T(8,128)}, f32[3,8192]{1,0:T(4,128)}) custom-call(s32[1]{0:T(128)} %bitcast.place_ref, s32[1]{0:T(128)S(6)} %copy.7.count_ref, s32[4,8192]{1,0:T(4,128)S(1)} %copy-done, f32[1,8192]{1,0:T(1,128)S(1)} %bitcast.13, f32[1,8192]{1,0:T(1,128)S(1)} %bitcast.15, f32[3,8192]{1,0:T(4,128)S(1)} %copy-done.1, ...), custom_call_target="tpu_custom_call" | custom-call | tf_op jit(solution)/shard_map/drag/pallas_call | solution.py:617
  (3 shorter events, 0.1 us)
Async XLA Ops:
  2.4 6.2 %collective-permute-start = (f32[4,8192]{1,0:T(4,128)S(1)}, f32[4,8192]{1,0:T(4,128)S(1)}, u32[]{:S(2)}, u32[]{:S(2)}) collective-permute-start(f32[4,8192]{1,0:T(4,128)S(1)} %grains.1.grain_ref), channel_id=1, source_target_pairs={{0,2},{1,3},{2,0},{3,1},{4,6},{5,7},{6,4},{7,5},{8,10},{9,11},{10,... | collective-permute-start | bytes 393224 | tf_op jit(solution)/shard_map/ppermute | solution.py:469
  3.7 6.8 %collective-permute-start.1 = (f32[4,8192]{1,0:T(4,128)S(1)}, f32[4,8192]{1,0:T(4,128)S(1)}, u32[]{:S(2)}, u32[]{:S(2)}) collective-permute-start(f32[4,8192]{1,0:T(4,128)S(1)} %grains.1.grain_ref), channel_id=1, source_target_pairs={{0,3},{1,2},{2,1},{3,0},{4,7},{5,6},{6,5},{7,4},{8,11},{9,10},{10,... | collective-permute-start | bytes 393224 | tf_op jit(solution)/shard_map/ppermute | solution.py:469
  4.8 1.9 %collective-permute-start.2 = (f32[4,8192]{1,0:T(4,128)S(1)}, f32[4,8192]{1,0:T(4,128)S(1)}, u32[]{:S(2)}, u32[]{:S(2)}) collective-permute-start(f32[4,8192]{1,0:T(4,128)S(1)} %grains.1.grain_ref), channel_id=1, source_target_pairs={{0,1},{1,0},{2,3},{3,2},{4,5},{5,4},{6,7},{7,6},{8,9},{9,8},{10,11... | collective-permute-start | bytes 393224 | tf_op jit(solution)/shard_map/ppermute | solution.py:469
  14.5 7.8 %collective-permute-start.6 = (f32[320,128]{1,0:T(8,128)S(1)}, f32[320,128]{1,0:T(8,128)S(1)}, u32[]{:S(2)}, u32[]{:S(2)}) collective-permute-start(f32[320,128]{1,0:T(8,128)S(1)} %get-tuple-element.19), channel_id=1, source_target_pairs={{8,16},{12,20},{16,8},{20,12},{9,17},{13,21},{17,9},{21,13},{10,18... | collective-permute-start | bytes 491528 | tf_op jit(solution)/shard_map/ppermute | solution.py:478
  17.7 10.8 %collective-permute-start.3 = (f32[384,128]{1,0:T(8,128)S(1)}, f32[384,128]{1,0:T(8,128)S(1)}, u32[]{:S(2)}, u32[]{:S(2)}) collective-permute-start(f32[384,128]{1,0:T(8,128)S(1)} %get-tuple-element.18.own_ref), channel_id=1, source_target_pairs={{0,4},{8,12},{16,20},{24,28},{4,0},{12,8},{20,16},{28,24},{1,5},{9... | collective-permute-start | bytes 589832 | tf_op jit(solution)/shard_map/ppermute | solution.py:478
  19.0 9.5 %collective-permute-start.4 = (f32[384,128]{1,0:T(8,128)S(1)}, f32[384,128]{1,0:T(8,128)S(1)}, u32[]{:S(2)}, u32[]{:S(2)}) collective-permute-start(f32[384,128]{1,0:T(8,128)S(1)} %get-tuple-element.18.own_ref), channel_id=1, source_target_pairs={{4,8},{12,16},{20,24},{8,4},{16,12},{24,20},{5,9},{13,17},{21,25},... | collective-permute-start | bytes 589832 | tf_op jit(solution)/shard_map/ppermute | solution.py:478
  21.0 7.6 %collective-permute-start.5 = (f32[320,128]{1,0:T(8,128)S(1)}, f32[320,128]{1,0:T(8,128)S(1)}, u32[]{:S(2)}, u32[]{:S(2)}) collective-permute-start(f32[320,128]{1,0:T(8,128)S(1)} %get-tuple-element.19), channel_id=1, source_target_pairs={{0,8},{4,12},{16,24},{20,28},{8,0},{12,4},{24,16},{28,20},{1,9},{5... | collective-permute-start | bytes 491528 | tf_op jit(solution)/shard_map/ppermute | solution.py:478
  22.3 8.8 %collective-permute-start.7 = (f32[1,128,128]{2,1,0:T(8,128)S(1)}, f32[1,128,128]{2,1,0:T(8,128)S(1)}, u32[]{:S(2)}, u32[]{:S(2)}) collective-permute-start(f32[1,128,128]{2,1,0:T(8,128)S(1)} %bitcast.16), channel_id=1, source_target_pairs={{0,2},{1,3},{2,0},{3,1},{4,6},{5,7},{6,4},{7,5},{8,10},{9,11},{10,... | collective-permute-start | bytes 196616 | tf_op jit(solution)/shard_map/ppermute | solution.py:469
  31.2 5.6 %copy-start = (s32[4,8192]{1,0:T(4,128)S(1)}, s32[4,8192]{1,0:T(4,128)}, u32[]{:S(2)}) copy-start(s32[4,8192]{1,0:T(4,128)} %cell_ref.7) | copy-start | bytes 393220
  31.2 5.6 %copy-start.2 = (f32[8192]{0:T(1024)S(1)}, f32[8192]{0:T(1024)}, u32[]{:S(2)}) copy-start(f32[8192]{0:T(1024)} %param.7) | copy-start | bytes 98308
  31.2 7.5 %collective-permute-start.8 = (f32[160,128]{1,0:T(8,128)S(1)}, f32[160,128]{1,0:T(8,128)S(1)}, u32[]{:S(2)}, u32[]{:S(2)}) collective-permute-start(f32[160,128]{1,0:T(8,128)S(1)} %get-tuple-element.29.refs_0_), channel_id=1, source_target_pairs={{0,4},{8,12},{16,20},{24,28},{4,0},{12,8},{20,16},{28,24},{1,5},{9... | collective-permute-start | bytes 245768 | tf_op jit(solution)/shard_map/ppermute | solution.py:478
  34.4 6.1 %collective-permute-start.9 = (f32[160,128]{1,0:T(8,128)S(1)}, f32[160,128]{1,0:T(8,128)S(1)}, u32[]{:S(2)}, u32[]{:S(2)}) collective-permute-start(f32[160,128]{1,0:T(8,128)S(1)} %get-tuple-element.29.refs_0_), channel_id=1, source_target_pairs={{4,8},{12,16},{20,24},{8,4},{16,12},{24,20},{5,9},{13,17},{21,25},... | collective-permute-start | bytes 245768 | tf_op jit(solution)/shard_map/ppermute | solution.py:478
  41.4 3.9 %collective-permute-start.10 = (f32[1,224,128]{2,1,0:T(8,128)S(1)}, f32[1,224,128]{2,1,0:T(8,128)S(1)}, u32[]{:S(2)}, u32[]{:S(2)}) collective-permute-start(f32[1,224,128]{2,1,0:T(8,128)S(1)} %bitcast.6), channel_id=1, source_target_pairs={{0,2},{1,3},{2,0},{3,1},{4,6},{5,7},{6,4},{7,5},{8,10},{9,11},{10,... | collective-permute-start | bytes 344072 | tf_op jit(solution)/shard_map/ppermute | solution.py:469
  45.4 6.0 %copy-start.1 = (f32[3,8192]{1,0:T(4,128)S(1)}, f32[3,8192]{1,0:T(4,128)}, u32[]{:S(2)}) copy-start(f32[3,8192]{1,0:T(4,128)} %refs_0_.3) | copy-start | bytes 294916
  45.4 6.0 %copy-start.3 = (f32[8192]{0:T(1024)S(1)}, f32[8192]{0:T(1024)}, u32[]{:S(2)}) copy-start(f32[8192]{0:T(1024)} %param.8) | copy-start | bytes 98308
  45.4 5.9 %collective-permute-start.11 = (f32[2,352,128]{2,1,0:T(8,128)S(1)}, f32[2,352,128]{2,1,0:T(8,128)S(1)}, u32[]{:S(2)}, u32[]{:S(2)}) collective-permute-start(f32[2,352,128]{2,1,0:T(8,128)S(1)} %pad_maximum_fusion), channel_id=1, source_target_pairs={{0,1},{1,0},{2,3},{3,2},{4,5},{5,4},{6,7},{7,6},{8,9},{9,8},{10,11... | collective-permute-start | bytes 1081352 | tf_op jit(solution)/shard_map/ppermute | solution.py:469

commit v6 on v5

--- a/solution.py
+++ b/solution.py
@@ -194,12 +194,9 @@
 
 
 def coefficient_kernel(quads, chunk, place_ref, *refs):
-    half = quads // 2
-    grains, total_ref, outs, solid_ref = refs[:half], refs[half], refs[half + 1 : -1], refs[-1]
+    grain_ref, total_ref, *outs, solid_ref = refs
     across, own = quads * CA, CB // quads
-    total = total_ref[...]
-    for grain_ref in grains:
-        total = deposit_into(total, quads, chunk, place_ref, grain_ref)
+    total = deposit_into(total_ref[...], quads, chunk, place_ref, grain_ref)
     halo = reach(0)
     size = own + 2 * halo
     windows = []
@@ -221,7 +218,7 @@
         out[...] = pack((offset, gain), reach(distance + 1), own)
 
 
-def sweep_over(sweeps, layers, across, old, new, offset_ref, gain_ref):
+def sweep_over(sweeps, layers, across, old, new, spare, offset_ref, gain_ref):
     row = lax.broadcasted_iota(jnp.int32, (across, LANES), 0)
     for sweep in range(1, sweeps + 1):
         for layer in range(sweep, layers - sweep):
@@ -231,7 +228,7 @@
             total = total + jnp.where(row == 0, 0.0, pltpu.roll(centre, 1, 0))
             total = total + jnp.where(row == across - 1, 0.0, pltpu.roll(centre, across - 1, 0))
             new[layer] = offset_ref[layer] + gain_ref[layer] * total
-        old, new = new, old
+        old, new, spare = new, spare, new
     return old
 
 
@@ -262,14 +259,11 @@
         span = pl.ds(slot * CH, CH)
         offset, gain = unpack(part[...], 2, across, reach(distance), own)
         offset_ref[span] = offset
-        even_ref[span] = offset
         gain_ref[span] = gain
-    sweeps = min(FIRST, ITERS) - 1
-    last = sweep_over(sweeps, layers, across, even_ref, odd_ref, offset_ref, gain_ref)
-    if FIRST < ITERS:
-        out_ref[...] = pack([last[DEPTH * CH : (DEPTH + 1) * CH]], SUBLANES, own)
-    else:
-        out_ref[...] = framed(last, DEPTH * CH, own)
+    last = sweep_over(
+        FIRST - 1, layers, across, offset_ref, even_ref, odd_ref, offset_ref, gain_ref
+    )
+    out_ref[...] = pack([last[DEPTH * CH : (DEPTH + 1) * CH]], SUBLANES, own)
 
 
 def finish_kernel(quads, slab_ref, offset_ref, gain_ref, *refs):
@@ -285,6 +279,7 @@
         across,
         even_ref,
         odd_ref,
+        even_ref,
         offset_ref.at[near],
         gain_ref.at[near],
     )
@@ -509,12 +504,15 @@
         pinned(volume),
         pinned(grain_velocity),
     )
+    packs = [packed_grains]
+    for bit in halving(quads):
+        packs += [over_quad(bit, pack) for pack in packs]
     half = quads // 2
-    others = [over_quad(step, packed_grains) for step in reversed(range(1, quads))][::-1]
+    packs = [packs[half * (index % 2) + index // 2] for index in range(quads)]
     size = own + 2 * reach(0)
     deposit_chunk = min(grains, 2048)
     total = None
-    for arrived in [packed_grains] + others[: half - 1]:
+    for arrived in packs[:-1]:
         earlier = [] if total is None else [total]
         total = pl.pallas_call(
             functools.partial(deposit_kernel, quads, deposit_chunk),
@@ -534,11 +532,11 @@
             for distance in range(1, DEPTH + 1)
         ]
         + [cells(CH * tall, LANES)],
-        in_specs=[SMEM] + [VMEM] * (half + 1),
+        in_specs=[SMEM] + [VMEM] * 2,
         out_specs=[VMEM] * (DEPTH + 1),
         compiler_params=LIMIT,
         name="coefficients",
-    )(place, *others[half - 1 :], total)
+    )(place, packs[-1], total)
 
     stack = [coefs[0]] + [
         swapped(distance, matching, coefs[distance - 1])
@@ -548,12 +546,11 @@
     solids = nearly_all(solid)
     frame = cells(packed_rows(across, 1, SUBLANES, own) + 2 * tall, LANES)
     layers = CH * len(stack)
-    two_rounds = FIRST < ITERS
     window = cells(layers, across, LANES)
     centre, offset, gain = pl.pallas_call(
         functools.partial(relax_kernel, quads),
         out_shape=[
-            cells(packed_rows(across, 1, SUBLANES, own), LANES) if two_rounds else frame,
+            cells(packed_rows(across, 1, SUBLANES, own), LANES),
             window,
             window,
         ],
@@ -576,19 +573,17 @@
         name="solid",
     )(place, grain_cell, weight, solids)
 
-    mine = centre
-    if two_rounds:
-        pressures = [centre] + [swapped(*swap, centre) for swap in swap_plan(1)]
-        pressures, solid_sampled = lax.optimization_barrier((pressures, solid_sampled))
-        mine = pl.pallas_call(
-            functools.partial(finish_kernel, quads),
-            out_shape=frame,
-            in_specs=[SMEM] + [VMEM] * 5,
-            out_specs=VMEM,
-            scratch_shapes=[pltpu.VMEM((3 * CH, across, LANES), jnp.float32)] * 2,
-            compiler_params=LIMIT,
-            name="finish",
-        )(level, offset, gain, *pressures)
+    pressures = [centre] + [swapped(*swap, centre) for swap in swap_plan(1)]
+    pressures, solid_sampled = lax.optimization_barrier((pressures, solid_sampled))
+    mine = pl.pallas_call(
+        functools.partial(finish_kernel, quads),
+        out_shape=frame,
+        in_specs=[SMEM] + [VMEM] * 5,
+        out_specs=VMEM,
+        scratch_shapes=[pltpu.VMEM((3 * CH, across, LANES), jnp.float32)] * 2,
+        compiler_params=LIMIT,
+        name="finish",
+    )(level, offset, gain, *pressures)
 
     def sampled_from(held, index, *earlier):
         return pl.pallas_call(

time: 57.4 us -> 57.3 us (level)
  waiting for transfers between devices: 9.69 us -> 8.55 us
  starting transfers between devices: 21.4 us -> 22.3 us
    pallas_call x2 -> x3, Pallas kernels: 3.79 us -> 5.68 us  [body(): pl.pallas_call(functools.partial(deposit_kernel, quads, deposit_chunk), o...]
    pallas_call x1, Pallas kernels: 4.01 us -> 2.33 us  [body(): pl.pallas_call(functools.partial(coefficient_kernel, quads, deposit_chunk...]
    ppermute x6, waiting for transfers between devices: 1.91 us -> 0.54 us  [over_quad(): return lax.ppermute(value, 'quad', pairs)]
    ppermute x6, starting transfers between devices: 9.34 us -> 10.3 us  [over_quad(): return lax.ppermute(value, 'quad', pairs)]
  transfers between devices with their start and end apart: 12 -> 12, of which waited for: 4 -> 5; matrix products, arithmetic and copies ran while one was open for 0% -> 0% of each run, Pallas kernels for 22% -> 25%
where the time goes in v6:
time: 57.3 us; the launch traced here: 57.1 us
  Pallas kernels  24.6 us (43%)
  starting transfers between devices  22.3 us (39%)
  waiting for transfers between devices  8.55 us (15%)
  between operations  1.5 us (3%)
    ppermute x6, starting transfers between devices, swapped(): lax.ppermute(value, 'slab', pairs + [(high, low) for low, high in pairs])  12 us
    ppermute x6, starting transfers between devices, over_quad(): return lax.ppermute(value, 'quad', pairs)  10.3 us
    ppermute x6, waiting for transfers between devices, swapped(): lax.ppermute(value, 'slab', pairs + [(high, low) for low, high in pairs])  8 us
    pallas_call x1, Pallas kernels, body(): pl.pallas_call(functools.partial(drag_kernel, quads, grain_chunk), out_sh...  5.89 us
    pallas_call x3, Pallas kernels, body(): pl.pallas_call(functools.partial(deposit_kernel, quads, deposit_chunk), o...  5.68 us
    pallas_call x2, Pallas kernels, sampled_from(): pl.pallas_call(functools.partial(sampled_kernel, quads, grain_chunk, plac...  4.37 us
    pallas_call x1, Pallas kernels, body(): pl.pallas_call(functools.partial(relax_kernel, quads), out_shape=[cells(p...  2.43 us
    pallas_call x1, Pallas kernels, body(): pl.pallas_call(functools.partial(coefficient_kernel, quads, deposit_chunk...  2.33 us
  transfers between devices with their start and end apart: 12, of which 5 were waited for; matrix products, arithmetic and copies ran while one was open for 0% of the time, Pallas kernels for 25%

profile of v6, /device:TPU:9, one launch (start us, length us, event | category | flops | bytes accessed | tf_op | source)
XLA Modules:
  0.0 57.1 jit_solution(6999870335808239939)
XLA Ops:
  1.3 1.1 %grains.1.grain_ref = f32[4,8192]{1,0:T(4,128)S(1)} custom-call(s32[1]{0:T(128)S(6)} %copy.7.count_ref, s32[4,8192]{1,0:T(4,128)} %cell_ref.7, f32[1,8192]{1,0:T(1,128)} %bitcast.9, f32[1,8192]{1,0:T(1,128)} %bitcast.14, f32[3,8192]{1,0:T(4,128)} %refs_0_.3), custom_call_target="tpu_custom_call" | custom-call | tf_op jit(solution)/shard_map/grains/pallas_call | solution.py:486
  2.4 1.3 %collective-permute-start = (f32[4,8192]{1,0:T(4,128)S(1)}, f32[4,8192]{1,0:T(4,128)S(1)}, u32[]{:S(2)}, u32[]{:S(2)}) collective-permute-start(f32[4,8192]{1,0:T(4,128)S(1)} %grains.1.grain_ref), channel_id=1, source_target_pairs={{0,2},{1,3},{2,0},{3,1},{4,6},{5,7},{6,4},{7,5},{8,10},{9,11},{10,... | collective-permute-start | bytes 393224 | tf_op jit(solution)/shard_map/ppermute | solution.py:464
  3.7 1.0 %collective-permute-start.2 = (f32[4,8192]{1,0:T(4,128)S(1)}, f32[4,8192]{1,0:T(4,128)S(1)}, u32[]{:S(2)}, u32[]{:S(2)}) collective-permute-start(f32[4,8192]{1,0:T(4,128)S(1)} %grains.1.grain_ref), channel_id=1, source_target_pairs={{0,1},{1,0},{2,3},{3,2},{4,5},{5,4},{6,7},{7,6},{8,9},{9,8},{10,11... | collective-permute-start | bytes 393224 | tf_op jit(solution)/shard_map/ppermute | solution.py:464
  4.6 1.9 %deposit.3.refs_0_ = f32[384,256]{1,0:T(8,128)S(1)} custom-call(s32[1]{0:T(128)} %bitcast.place_ref, f32[4,8192]{1,0:T(4,128)S(1)} %grains.1.grain_ref), custom_call_target="tpu_custom_call" | custom-call | flops 1610612736 | bytes 1048576 | tf_op jit(solution)/shard_map/deposit/pallas_call | solution.py:517
  6.5 0.3 collective-permute-done.grain_ref
  6.8 1.5 %collective-permute-start.1 = (f32[4,8192]{1,0:T(4,128)S(1)}, f32[4,8192]{1,0:T(4,128)S(1)}, u32[]{:S(2)}, u32[]{:S(2)}) collective-permute-start(f32[4,8192]{1,0:T(4,128)S(1)} %collective-permute-done.grain_ref), channel_id=1, source_target_pairs={{0,1},{1,0},{2,3},{3,2},{4,5},{5,4},{6,7},{7,6},{8,9},{9,8},{10,11... | collective-permute-start | bytes 393224 | tf_op jit(solution)/shard_map/ppermute | solution.py:464
  8.4 0.0 collective-permute-done.2.grain_ref
  8.4 1.9 %deposit.4.refs_0_ = f32[384,256]{1,0:T(8,128)S(1)} custom-call(s32[1]{0:T(128)} %bitcast.place_ref, f32[4,8192]{1,0:T(4,128)S(1)} %collective-permute-done.2.grain_ref, f32[384,256]{1,0:T(8,128)S(1)} %deposit.3.refs_0_), custom_call_target="tpu_custom_call" | custom-call | flops 1610612736 | bytes 1048576 | tf_op jit(solution)/shard_map/deposit/pallas_call | solution.py:517
  10.3 1.9 %deposit.5.refs_1_ = f32[384,256]{1,0:T(8,128)S(1)} custom-call(s32[1]{0:T(128)} %bitcast.place_ref, f32[4,8192]{1,0:T(4,128)S(1)} %collective-permute-done.grain_ref, f32[384,256]{1,0:T(8,128)S(1)} %deposit.4.refs_0_), custom_call_target="tpu_custom_call" | custom-call | flops 1610612736 | bytes 1048576 | tf_op jit(solution)/shard_map/deposit/pallas_call | solution.py:517
  12.2 0.0 collective-permute-done.1.refs_0_
  12.2 2.3 %coefficients.1 = (f32[384,128]{1,0:T(8,128)S(1)}, f32[320,128]{1,0:T(8,128)S(1)}, f32[128,128]{1,0:T(8,128)S(1)}) custom-call(s32[1]{0:T(128)} %bitcast.place_ref, f32[4,8192]{1,0:T(4,128)S(1)} %collective-permute-done.1.refs_0_, f32[384,256]{1,0:T(8,128)S(1)} %deposit.5.refs_1_), custom_call_target="tpu_custom_call" | custom-call | tf_op jit(solution)/shard_map/coefficients/pallas_call | solution.py:528
  14.5 3.2 %collective-permute-start.6 = (f32[320,128]{1,0:T(8,128)S(1)}, f32[320,128]{1,0:T(8,128)S(1)}, u32[]{:S(2)}, u32[]{:S(2)}) collective-permute-start(f32[320,128]{1,0:T(8,128)S(1)} %get-tuple-element.19), channel_id=1, source_target_pairs={{8,16},{12,20},{16,8},{20,12},{9,17},{13,21},{17,9},{21,13},{10,18... | collective-permute-start | bytes 491528 | tf_op jit(solution)/shard_map/ppermute | solution.py:473
  17.8 1.3 %collective-permute-start.3 = (f32[384,128]{1,0:T(8,128)S(1)}, f32[384,128]{1,0:T(8,128)S(1)}, u32[]{:S(2)}, u32[]{:S(2)}) collective-permute-start(f32[384,128]{1,0:T(8,128)S(1)} %get-tuple-element.18.own_ref), channel_id=1, source_target_pairs={{0,4},{8,12},{16,20},{24,28},{4,0},{12,8},{20,16},{28,24},{1,5},{9... | collective-permute-start | bytes 589832 | tf_op jit(solution)/shard_map/ppermute | solution.py:473
  19.1 1.9 %collective-permute-start.4 = (f32[384,128]{1,0:T(8,128)S(1)}, f32[384,128]{1,0:T(8,128)S(1)}, u32[]{:S(2)}, u32[]{:S(2)}) collective-permute-start(f32[384,128]{1,0:T(8,128)S(1)} %get-tuple-element.18.own_ref), channel_id=1, source_target_pairs={{4,8},{12,16},{20,24},{8,4},{16,12},{24,20},{5,9},{13,17},{21,25},... | collective-permute-start | bytes 589832 | tf_op jit(solution)/shard_map/ppermute | solution.py:473
  21.0 0.1 collective-permute-start.5
  21.1 1.2 %collective-permute-done.6.refs_3_ = f32[320,128]{1,0:T(8,128)S(1)} collective-permute-done((f32[320,128]{1,0:T(8,128)S(1)}, f32[320,128]{1,0:T(8,128)S(1)}, u32[]{:S(2)}, u32[]{:S(2)}) %collective-permute-start.6) | collective-permute-done | bytes 163872 | tf_op jit(solution)/shard_map/ppermute | solution.py:473
  22.3 1.2 %collective-permute-start.7 = (f32[1,128,128]{2,1,0:T(8,128)S(1)}, f32[1,128,128]{2,1,0:T(8,128)S(1)}, u32[]{:S(2)}, u32[]{:S(2)}) collective-permute-start(f32[1,128,128]{2,1,0:T(8,128)S(1)} %bitcast.16), channel_id=1, source_target_pairs={{0,2},{1,3},{2,0},{3,1},{4,6},{5,7},{6,4},{7,5},{8,10},{9,11},{10,... | collective-permute-start | bytes 196616 | tf_op jit(solution)/shard_map/ppermute | solution.py:464
  23.5 5.0 %collective-permute-done.5.refs_2_ = f32[320,128]{1,0:T(8,128)S(1)} collective-permute-done((f32[320,128]{1,0:T(8,128)S(1)}, f32[320,128]{1,0:T(8,128)S(1)}, u32[]{:S(2)}, u32[]{:S(2)}) %collective-permute-start.5) | collective-permute-done | bytes 163872 | tf_op jit(solution)/shard_map/ppermute | solution.py:473
  28.5 0.0 collective-permute-done.3.refs_0_
  28.5 0.0 collective-permute-done.4.refs_1_
  28.5 2.4 %relax.1 = (f32[160,128]{1,0:T(8,128)S(1)}, f32[20,64,128]{2,1,0:T(8,128)S(1)}, f32[20,64,128]{2,1,0:T(8,128)S(1)}) custom-call(s32[1]{0:T(128)} %bitcast.3.slab_ref, f32[384,128]{1,0:T(8,128)S(1)} %get-tuple-element.18.own_ref, f32[384,128]{1,0:T(8,128)S(1)} %collective-permute-done.3.refs_0_, f32[384,128]{1,0:T(8,128)S(1)} %collective-permute-done.4.refs_1_, ...), custom_call_target="tpu_custom_call" | custom-call | tf_op jit(solution)/shard_map/relax/pallas_call | solution.py:550
  30.9 0.0 copy-start
  30.9 0.0 copy-start.2
  30.9 0.0 collective-permute-done.7
  31.0 3.2 %collective-permute-start.8 = (f32[160,128]{1,0:T(8,128)S(1)}, f32[160,128]{1,0:T(8,128)S(1)}, u32[]{:S(2)}, u32[]{:S(2)}) collective-permute-start(f32[160,128]{1,0:T(8,128)S(1)} %get-tuple-element.29.refs_0_), channel_id=1, source_target_pairs={{0,4},{8,12},{16,20},{24,28},{4,0},{12,8},{20,16},{28,24},{1,5},{9... | collective-permute-start | bytes 245768 | tf_op jit(solution)/shard_map/ppermute | solution.py:473
  34.2 2.3 %collective-permute-start.9 = (f32[160,128]{1,0:T(8,128)S(1)}, f32[160,128]{1,0:T(8,128)S(1)}, u32[]{:S(2)}, u32[]{:S(2)}) collective-permute-start(f32[160,128]{1,0:T(8,128)S(1)} %get-tuple-element.29.refs_0_), channel_id=1, source_target_pairs={{4,8},{12,16},{20,24},{8,4},{16,12},{24,20},{5,9},{13,17},{21,25},... | collective-permute-start | bytes 245768 | tf_op jit(solution)/shard_map/ppermute | solution.py:473
  36.5 0.0 copy-done
  36.5 0.0 copy-done.2
  36.5 1.9 %solid.1.refs_1_ = f32[1,8192]{1,0:T(1,128)S(1)} custom-call(s32[1]{0:T(128)} %bitcast.place_ref, s32[4,8192]{1,0:T(4,128)S(1)} %copy-done, f32[1,8192]{1,0:T(1,128)S(1)} %bitcast.10, f32[2,128,128]{2,1,0:T(8,128)S(1)} %pad_maximum_fusion.2.held_ref), custom_call_target="tpu_custom_call" | custom-call | flops 1073741824 | bytes 1048576 | tf_op jit(solution)/shard_map/solid/pallas_call | solution.py:564
  38.4 0.0 collective-permute-done.8.refs_1_
  38.4 1.8 %collective-permute-done.9.refs_2_ = f32[160,128]{1,0:T(8,128)S(1)} collective-permute-done((f32[160,128]{1,0:T(8,128)S(1)}, f32[160,128]{1,0:T(8,128)S(1)}, u32[]{:S(2)}, u32[]{:S(2)}) %collective-permute-start.9) | collective-permute-done | bytes 81952 | tf_op jit(solution)/shard_map/ppermute | solution.py:473
  40.2 0.9 %finish.1 = f32[224,128]{1,0:T(8,128)S(1)} custom-call(s32[1]{0:T(128)} %bitcast.3.slab_ref, f32[20,64,128]{2,1,0:T(8,128)S(1)} %get-tuple-element.27.offset_ref, f32[20,64,128]{2,1,0:T(8,128)S(1)} %get-tuple-element.28.gain_ref, f32[160,128]{1,0:T(8,128)S(1)} %get-tuple-element.29.refs_0_, f32[160,128]{1,0:T(8,128)S(1)} %collective-permute-done.8.refs_1_, ...), custom_call_target="tpu_custom_call" | custom-call | tf_op jit(solution)/shard_map/finish/pallas_call | solution.py:578
  41.2 1.3 %collective-permute-start.10 = (f32[1,224,128]{2,1,0:T(8,128)S(1)}, f32[1,224,128]{2,1,0:T(8,128)S(1)}, u32[]{:S(2)}, u32[]{:S(2)}) collective-permute-start(f32[1,224,128]{2,1,0:T(8,128)S(1)} %bitcast.6), channel_id=1, source_target_pairs={{0,2},{1,3},{2,0},{3,1},{4,6},{5,7},{6,4},{7,5},{8,10},{9,11},{10,... | collective-permute-start | bytes 344072 | tf_op jit(solution)/shard_map/ppermute | solution.py:464
  42.5 2.2 %sampled.2.refs_0_ = f32[3,8192]{1,0:T(4,128)S(1)} custom-call(s32[1]{0:T(128)} %bitcast.place_ref, s32[4,8192]{1,0:T(4,128)S(1)} %copy-done, f32[1,8192]{1,0:T(1,128)S(1)} %bitcast.11, f32[1,224,128]{2,1,0:T(8,128)S(1)} %bitcast.7), custom_call_target="tpu_custom_call" | custom-call | flops 1610612736 | bytes 1048576 | tf_op jit(solution)/shard_map/sampled/pallas_call | solution.py:589
  44.6 0.2 collective-permute-done.10
  44.9 0.0 copy-start.1
  44.9 0.0 copy-start.3
  45.0 4.0 %collective-permute-start.11 = (f32[2,352,128]{2,1,0:T(8,128)S(1)}, f32[2,352,128]{2,1,0:T(8,128)S(1)}, u32[]{:S(2)}, u32[]{:S(2)}) collective-permute-start(f32[2,352,128]{2,1,0:T(8,128)S(1)} %pad_maximum_fusion), channel_id=1, source_target_pairs={{0,1},{1,0},{2,3},{3,2},{4,5},{5,4},{6,7},{7,6},{8,9},{9,8},{10,11... | collective-permute-start | bytes 1081352 | tf_op jit(solution)/shard_map/ppermute | solution.py:464
  49.0 2.2 %sampled.3.refs_2_ = f32[3,8192]{1,0:T(4,128)S(1)} custom-call(s32[1]{0:T(128)} %bitcast.place_ref, s32[4,8192]{1,0:T(4,128)S(1)} %copy-done, f32[1,8192]{1,0:T(1,128)S(1)} %bitcast.12, f32[2,224,128]{2,1,0:T(8,128)S(1)} %pad_maximum_fusion.1.held_ref.refs_3_, f32[3,8192]{1,0:T(4,128)S(1)} %sampled.2.refs_0_), custom_call_target="tpu_custom_call" | custom-call | flops 1610612736 | bytes 1048576 | tf_op jit(solution)/shard_map/sampled/pallas_call | solution.py:589
  51.2 0.0 collective-permute-done.11.refs_4_
  51.2 0.0 copy-done.1
  51.2 0.0 copy-done.3
  51.2 5.9 %drag.1 = (f32[4,16,256]{2,1,0:T(8,128)}, f32[3,8192]{1,0:T(4,128)}) custom-call(s32[1]{0:T(128)} %bitcast.place_ref, s32[1]{0:T(128)S(6)} %copy.7.count_ref, s32[4,8192]{1,0:T(4,128)S(1)} %copy-done, f32[1,8192]{1,0:T(1,128)S(1)} %bitcast.13, f32[1,8192]{1,0:T(1,128)S(1)} %bitcast.15, f32[3,8192]{1,0:T(4,128)S(1)} %copy-done.1, ...), custom_call_target="tpu_custom_call" | custom-call | tf_op jit(solution)/shard_map/drag/pallas_call | solution.py:612
  (3 shorter events, 0.1 us)
Async XLA Ops:
  2.4 4.4 %collective-permute-start = (f32[4,8192]{1,0:T(4,128)S(1)}, f32[4,8192]{1,0:T(4,128)S(1)}, u32[]{:S(2)}, u32[]{:S(2)}) collective-permute-start(f32[4,8192]{1,0:T(4,128)S(1)} %grains.1.grain_ref), channel_id=1, source_target_pairs={{0,2},{1,3},{2,0},{3,1},{4,6},{5,7},{6,4},{7,5},{8,10},{9,11},{10,... | collective-permute-start | bytes 393224 | tf_op jit(solution)/shard_map/ppermute | solution.py:464
  3.7 4.7 %collective-permute-start.2 = (f32[4,8192]{1,0:T(4,128)S(1)}, f32[4,8192]{1,0:T(4,128)S(1)}, u32[]{:S(2)}, u32[]{:S(2)}) collective-permute-start(f32[4,8192]{1,0:T(4,128)S(1)} %grains.1.grain_ref), channel_id=1, source_target_pairs={{0,1},{1,0},{2,3},{3,2},{4,5},{5,4},{6,7},{7,6},{8,9},{9,8},{10,11... | collective-permute-start | bytes 393224 | tf_op jit(solution)/shard_map/ppermute | solution.py:464
  6.8 5.4 %collective-permute-start.1 = (f32[4,8192]{1,0:T(4,128)S(1)}, f32[4,8192]{1,0:T(4,128)S(1)}, u32[]{:S(2)}, u32[]{:S(2)}) collective-permute-start(f32[4,8192]{1,0:T(4,128)S(1)} %collective-permute-done.grain_ref), channel_id=1, source_target_pairs={{0,1},{1,0},{2,3},{3,2},{4,5},{5,4},{6,7},{7,6},{8,9},{9,8},{10,11... | collective-permute-start | bytes 393224 | tf_op jit(solution)/shard_map/ppermute | solution.py:464
  14.5 7.7 %collective-permute-start.6 = (f32[320,128]{1,0:T(8,128)S(1)}, f32[320,128]{1,0:T(8,128)S(1)}, u32[]{:S(2)}, u32[]{:S(2)}) collective-permute-start(f32[320,128]{1,0:T(8,128)S(1)} %get-tuple-element.19), channel_id=1, source_target_pairs={{8,16},{12,20},{16,8},{20,12},{9,17},{13,21},{17,9},{21,13},{10,18... | collective-permute-start | bytes 491528 | tf_op jit(solution)/shard_map/ppermute | solution.py:473
  17.8 10.7 %collective-permute-start.3 = (f32[384,128]{1,0:T(8,128)S(1)}, f32[384,128]{1,0:T(8,128)S(1)}, u32[]{:S(2)}, u32[]{:S(2)}) collective-permute-start(f32[384,128]{1,0:T(8,128)S(1)} %get-tuple-element.18.own_ref), channel_id=1, source_target_pairs={{0,4},{8,12},{16,20},{24,28},{4,0},{12,8},{20,16},{28,24},{1,5},{9... | collective-permute-start | bytes 589832 | tf_op jit(solution)/shard_map/ppermute | solution.py:473
  19.1 9.4 %collective-permute-start.4 = (f32[384,128]{1,0:T(8,128)S(1)}, f32[384,128]{1,0:T(8,128)S(1)}, u32[]{:S(2)}, u32[]{:S(2)}) collective-permute-start(f32[384,128]{1,0:T(8,128)S(1)} %get-tuple-element.18.own_ref), channel_id=1, source_target_pairs={{4,8},{12,16},{20,24},{8,4},{16,12},{24,20},{5,9},{13,17},{21,25},... | collective-permute-start | bytes 589832 | tf_op jit(solution)/shard_map/ppermute | solution.py:473
  21.0 7.5 %collective-permute-start.5 = (f32[320,128]{1,0:T(8,128)S(1)}, f32[320,128]{1,0:T(8,128)S(1)}, u32[]{:S(2)}, u32[]{:S(2)}) collective-permute-start(f32[320,128]{1,0:T(8,128)S(1)} %get-tuple-element.19), channel_id=1, source_target_pairs={{0,8},{4,12},{16,24},{20,28},{8,0},{12,4},{24,16},{28,20},{1,9},{5... | collective-permute-start | bytes 491528 | tf_op jit(solution)/shard_map/ppermute | solution.py:473
  22.3 8.7 %collective-permute-start.7 = (f32[1,128,128]{2,1,0:T(8,128)S(1)}, f32[1,128,128]{2,1,0:T(8,128)S(1)}, u32[]{:S(2)}, u32[]{:S(2)}) collective-permute-start(f32[1,128,128]{2,1,0:T(8,128)S(1)} %bitcast.16), channel_id=1, source_target_pairs={{0,2},{1,3},{2,0},{3,1},{4,6},{5,7},{6,4},{7,5},{8,10},{9,11},{10,... | collective-permute-start | bytes 196616 | tf_op jit(solution)/shard_map/ppermute | solution.py:464
  30.9 5.6 %copy-start = (s32[4,8192]{1,0:T(4,128)S(1)}, s32[4,8192]{1,0:T(4,128)}, u32[]{:S(2)}) copy-start(s32[4,8192]{1,0:T(4,128)} %cell_ref.7) | copy-start | bytes 393220
  30.9 5.6 %copy-start.2 = (f32[8192]{0:T(1024)S(1)}, f32[8192]{0:T(1024)}, u32[]{:S(2)}) copy-start(f32[8192]{0:T(1024)} %param.7) | copy-start | bytes 98308
  31.0 7.5 %collective-permute-start.8 = (f32[160,128]{1,0:T(8,128)S(1)}, f32[160,128]{1,0:T(8,128)S(1)}, u32[]{:S(2)}, u32[]{:S(2)}) collective-permute-start(f32[160,128]{1,0:T(8,128)S(1)} %get-tuple-element.29.refs_0_), channel_id=1, source_target_pairs={{0,4},{8,12},{16,20},{24,28},{4,0},{12,8},{20,16},{28,24},{1,5},{9... | collective-permute-start | bytes 245768 | tf_op jit(solution)/shard_map/ppermute | solution.py:473
  34.2 6.1 %collective-permute-start.9 = (f32[160,128]{1,0:T(8,128)S(1)}, f32[160,128]{1,0:T(8,128)S(1)}, u32[]{:S(2)}, u32[]{:S(2)}) collective-permute-start(f32[160,128]{1,0:T(8,128)S(1)} %get-tuple-element.29.refs_0_), channel_id=1, source_target_pairs={{4,8},{12,16},{20,24},{8,4},{16,12},{24,20},{5,9},{13,17},{21,25},... | collective-permute-start | bytes 245768 | tf_op jit(solution)/shard_map/ppermute | solution.py:473
  41.2 3.7 %collective-permute-start.10 = (f32[1,224,128]{2,1,0:T(8,128)S(1)}, f32[1,224,128]{2,1,0:T(8,128)S(1)}, u32[]{:S(2)}, u32[]{:S(2)}) collective-permute-start(f32[1,224,128]{2,1,0:T(8,128)S(1)} %bitcast.6), channel_id=1, source_target_pairs={{0,2},{1,3},{2,0},{3,1},{4,6},{5,7},{6,4},{7,5},{8,10},{9,11},{10,... | collective-permute-start | bytes 344072 | tf_op jit(solution)/shard_map/ppermute | solution.py:464
  44.9 6.3 %copy-start.1 = (f32[3,8192]{1,0:T(4,128)S(1)}, f32[3,8192]{1,0:T(4,128)}, u32[]{:S(2)}) copy-start(f32[3,8192]{1,0:T(4,128)} %refs_0_.3) | copy-start | bytes 294916
  44.9 6.3 %copy-start.3 = (f32[8192]{0:T(1024)S(1)}, f32[8192]{0:T(1024)}, u32[]{:S(2)}) copy-start(f32[8192]{0:T(1024)} %param.8) | copy-start | bytes 98308
  45.0 6.2 %collective-permute-start.11 = (f32[2,352,128]{2,1,0:T(8,128)S(1)}, f32[2,352,128]{2,1,0:T(8,128)S(1)}, u32[]{:S(2)}, u32[]{:S(2)}) collective-permute-start(f32[2,352,128]{2,1,0:T(8,128)S(1)} %pad_maximum_fusion), channel_id=1, source_target_pairs={{0,1},{1,0},{2,3},{3,2},{4,5},{5,4},{6,7},{7,6},{8,9},{9,8},{10,11... | collective-permute-start | bytes 1081352 | tf_op jit(solution)/shard_map/ppermute | solution.py:464

commit v7 on v6

--- a/solution.py
+++ b/solution.py
@@ -269,7 +269,7 @@
 def finish_kernel(quads, slab_ref, offset_ref, gain_ref, *refs):
     *parts, out_ref, even_ref, odd_ref = refs
     across, own = quads * CA, CB // quads
-    slots = [1] + [1 + slot_of(slab_ref[0], *swap) for swap in swap_plan(1)]
+    slots = [1] + [1 + slot_of(slab_ref[0], *swap) for swap in swap_plan(1)[::-1]]
     for slot, pressure in zip(slots, parts):
         (even_ref[pl.ds(slot * CH, CH)],) = unpack(pressure[...], 1, across, SUBLANES, own)
     near = pl.ds((DEPTH - 1) * CH, 3 * CH)
@@ -505,16 +505,15 @@
         pinned(grain_velocity),
     )
     packs = [packed_grains]
-    for bit in halving(quads):
+    for bit in early:
         packs += [over_quad(bit, pack) for pack in packs]
-    half = quads // 2
-    packs = [packs[half * (index % 2) + index // 2] for index in range(quads)]
     size = own + 2 * reach(0)
     deposit_chunk = min(grains, 2048)
     total = None
-    for arrived in packs[:-1]:
+
+    def deposited(total, arrived):
         earlier = [] if total is None else [total]
-        total = pl.pallas_call(
+        return pl.pallas_call(
             functools.partial(deposit_kernel, quads, deposit_chunk),
             out_shape=cells(4 * size, CH * across),
             in_specs=[SMEM] + [VMEM] * (1 + len(earlier)),
@@ -525,6 +524,14 @@
             ),
             name="deposit",
         )(place, arrived, *earlier)
+
+    for index, pack in enumerate(packs):
+        if index:
+            pack, total = lax.optimization_barrier((pack, total))
+        arriving = over_quad(last, pack)
+        total = deposited(total, pack)
+        if index < len(packs) - 1:
+            total = deposited(total, arriving)
     *coefs, solid = pl.pallas_call(
         functools.partial(coefficient_kernel, quads, deposit_chunk),
         out_shape=[
@@ -536,7 +543,7 @@
         out_specs=[VMEM] * (DEPTH + 1),
         compiler_params=LIMIT,
         name="coefficients",
-    )(place, packs[-1], total)
+    )(place, arriving, total)
 
     stack = [coefs[0]] + [
         swapped(distance, matching, coefs[distance - 1])
@@ -573,7 +580,7 @@
         name="solid",
     )(place, grain_cell, weight, solids)
 
-    pressures = [centre] + [swapped(*swap, centre) for swap in swap_plan(1)]
+    pressures = [centre] + [swapped(*swap, centre) for swap in swap_plan(1)[::-1]]
     pressures, solid_sampled = lax.optimization_barrier((pressures, solid_sampled))
     mine = pl.pallas_call(
         functools.partial(finish_kernel, quads),

time: 57.3 us -> 54.9 us (0.958); the launches traced: 57.1 us -> 53.8 us
  waiting for transfers between devices: 8.55 us -> 5.62 us
    ppermute x6, waiting for transfers between devices: 8 us -> 5.6 us  [swapped(): lax.ppermute(value, 'slab', pairs + [(high, low) for low, high in pairs])]
  transfers between devices with their start and end apart: 12 -> 12, of which waited for: 5 -> 3; matrix products, arithmetic and copies ran while one was open for 0% -> 0% of each run, Pallas kernels for 25% -> 27%
where the time goes in v7:
time: 54.9 us; the launch traced here: 53.8 us
  Pallas kernels  24.7 us (45%)
  starting transfers between devices  21.9 us (40%)
  waiting for transfers between devices  5.62 us (10%)
  between operations  1.52 us (3%)
    ppermute x6, starting transfers between devices, swapped(): lax.ppermute(value, 'slab', pairs + [(high, low) for low, high in pairs])  12 us
    ppermute x6, starting transfers between devices, over_quad(): return lax.ppermute(value, 'quad', pairs)  9.88 us
    pallas_call x1, Pallas kernels, body(): pl.pallas_call(functools.partial(drag_kernel, quads, grain_chunk), out_sh...  5.9 us
    pallas_call x3, Pallas kernels, deposited(): pl.pallas_call(functools.partial(deposit_kernel, quads, deposit_chunk), o...  5.68 us
    ppermute x6, waiting for transfers between devices, swapped(): lax.ppermute(value, 'slab', pairs + [(high, low) for low, high in pairs])  5.6 us
    pallas_call x2, Pallas kernels, sampled_from(): pl.pallas_call(functools.partial(sampled_kernel, quads, grain_chunk, plac...  4.37 us
    pallas_call x1, Pallas kernels, body(): pl.pallas_call(functools.partial(relax_kernel, quads), out_shape=[cells(p...  2.43 us
    pallas_call x1, Pallas kernels, body(): pl.pallas_call(functools.partial(coefficient_kernel, quads, deposit_chunk...  2.33 us
  transfers between devices with their start and end apart: 12, of which 3 were waited for; matrix products, arithmetic and copies ran while one was open for 0% of the time, Pallas kernels for 27%

profile of v7, /device:TPU:9, one launch (start us, length us, event | category | flops | bytes accessed | tf_op | source)
XLA Modules:
  0.0 53.8 jit_solution(11994984682223476114)
XLA Ops:
  1.3 1.1 %grains.1.grain_ref = f32[4,8192]{1,0:T(4,128)S(1)} custom-call(s32[1]{0:T(128)S(6)} %copy.7.count_ref, s32[4,8192]{1,0:T(4,128)} %cell_ref.7, f32[1,8192]{1,0:T(1,128)} %bitcast.9, f32[1,8192]{1,0:T(1,128)} %bitcast.14, f32[3,8192]{1,0:T(4,128)} %refs_0_.3), custom_call_target="tpu_custom_call" | custom-call | tf_op jit(solution)/shard_map/grains/pallas_call | solution.py:486
  2.4 1.3 %collective-permute-start = (f32[4,8192]{1,0:T(4,128)S(1)}, f32[4,8192]{1,0:T(4,128)S(1)}, u32[]{:S(2)}, u32[]{:S(2)}) collective-permute-start(f32[4,8192]{1,0:T(4,128)S(1)} %grains.1.grain_ref), channel_id=1, source_target_pairs={{0,2},{1,3},{2,0},{3,1},{4,6},{5,7},{6,4},{7,5},{8,10},{9,11},{10,... | collective-permute-start | bytes 393224 | tf_op jit(solution)/shard_map/ppermute | solution.py:464
  3.7 1.0 %collective-permute-start.1 = (f32[4,8192]{1,0:T(4,128)S(1)}, f32[4,8192]{1,0:T(4,128)S(1)}, u32[]{:S(2)}, u32[]{:S(2)}) collective-permute-start(f32[4,8192]{1,0:T(4,128)S(1)} %grains.1.grain_ref), channel_id=1, source_target_pairs={{0,1},{1,0},{2,3},{3,2},{4,5},{5,4},{6,7},{7,6},{8,9},{9,8},{10,11... | collective-permute-start | bytes 393224 | tf_op jit(solution)/shard_map/ppermute | solution.py:464
  4.6 1.9 %deposit.3.refs_0_ = f32[384,256]{1,0:T(8,128)S(1)} custom-call(s32[1]{0:T(128)} %bitcast.place_ref, f32[4,8192]{1,0:T(4,128)S(1)} %grains.1.grain_ref), custom_call_target="tpu_custom_call" | custom-call | flops 1610612736 | bytes 1048576 | tf_op jit(solution)/shard_map/deposit/pallas_call | solution.py:516
  6.5 0.0 collective-permute-done.1.grain_ref
  6.5 1.9 %deposit.4.refs_0_ = f32[384,256]{1,0:T(8,128)S(1)} custom-call(s32[1]{0:T(128)} %bitcast.place_ref, f32[4,8192]{1,0:T(4,128)S(1)} %collective-permute-done.1.grain_ref, f32[384,256]{1,0:T(8,128)S(1)} %deposit.3.refs_0_), custom_call_target="tpu_custom_call" | custom-call | flops 1610612736 | bytes 1048576 | tf_op jit(solution)/shard_map/deposit/pallas_call | solution.py:516
  8.5 0.0 collective-permute-done.grain_ref
  8.5 0.1 collective-permute-start.2
  8.5 1.9 %deposit.5.refs_1_ = f32[384,256]{1,0:T(8,128)S(1)} custom-call(s32[1]{0:T(128)} %bitcast.place_ref, f32[4,8192]{1,0:T(4,128)S(1)} %collective-permute-done.grain_ref, f32[384,256]{1,0:T(8,128)S(1)} %deposit.4.refs_0_), custom_call_target="tpu_custom_call" | custom-call | flops 1610612736 | bytes 1048576 | tf_op jit(solution)/shard_map/deposit/pallas_call | solution.py:516
  10.4 0.0 collective-permute-done.2.refs_0_
  10.5 2.3 %coefficients.1 = (f32[384,128]{1,0:T(8,128)S(1)}, f32[320,128]{1,0:T(8,128)S(1)}, f32[128,128]{1,0:T(8,128)S(1)}) custom-call(s32[1]{0:T(128)} %bitcast.place_ref, f32[4,8192]{1,0:T(4,128)S(1)} %collective-permute-done.2.refs_0_, f32[384,256]{1,0:T(8,128)S(1)} %deposit.5.refs_1_), custom_call_target="tpu_custom_call" | custom-call | tf_op jit(solution)/shard_map/coefficients/pallas_call | solution.py:535
  12.8 3.2 %collective-permute-start.6 = (f32[320,128]{1,0:T(8,128)S(1)}, f32[320,128]{1,0:T(8,128)S(1)}, u32[]{:S(2)}, u32[]{:S(2)}) collective-permute-start(f32[320,128]{1,0:T(8,128)S(1)} %get-tuple-element.23), channel_id=1, source_target_pairs={{8,16},{12,20},{16,8},{20,12},{9,17},{13,21},{17,9},{21,13},{10,18... | collective-permute-start | bytes 491528 | tf_op jit(solution)/shard_map/ppermute | solution.py:473
  16.0 1.3 %collective-permute-start.3 = (f32[384,128]{1,0:T(8,128)S(1)}, f32[384,128]{1,0:T(8,128)S(1)}, u32[]{:S(2)}, u32[]{:S(2)}) collective-permute-start(f32[384,128]{1,0:T(8,128)S(1)} %get-tuple-element.22.own_ref), channel_id=1, source_target_pairs={{0,4},{8,12},{16,20},{24,28},{4,0},{12,8},{20,16},{28,24},{1,5},{9... | collective-permute-start | bytes 589832 | tf_op jit(solution)/shard_map/ppermute | solution.py:473
  17.3 1.9 %collective-permute-start.4 = (f32[384,128]{1,0:T(8,128)S(1)}, f32[384,128]{1,0:T(8,128)S(1)}, u32[]{:S(2)}, u32[]{:S(2)}) collective-permute-start(f32[384,128]{1,0:T(8,128)S(1)} %get-tuple-element.22.own_ref), channel_id=1, source_target_pairs={{4,8},{12,16},{20,24},{8,4},{16,12},{24,20},{5,9},{13,17},{21,25},... | collective-permute-start | bytes 589832 | tf_op jit(solution)/shard_map/ppermute | solution.py:473
  19.2 0.1 collective-permute-start.5
  19.3 0.7 %collective-permute-done.6.refs_3_ = f32[320,128]{1,0:T(8,128)S(1)} collective-permute-done((f32[320,128]{1,0:T(8,128)S(1)}, f32[320,128]{1,0:T(8,128)S(1)}, u32[]{:S(2)}, u32[]{:S(2)}) %collective-permute-start.6) | collective-permute-done | bytes 163872 | tf_op jit(solution)/shard_map/ppermute | solution.py:473
  20.0 1.6 %collective-permute-start.7 = (f32[1,128,128]{2,1,0:T(8,128)S(1)}, f32[1,128,128]{2,1,0:T(8,128)S(1)}, u32[]{:S(2)}, u32[]{:S(2)}) collective-permute-start(f32[1,128,128]{2,1,0:T(8,128)S(1)} %bitcast.16), channel_id=1, source_target_pairs={{0,2},{1,3},{2,0},{3,1},{4,6},{5,7},{6,4},{7,5},{8,10},{9,11},{10,... | collective-permute-start | bytes 196616 | tf_op jit(solution)/shard_map/ppermute | solution.py:464
  21.6 4.6 %collective-permute-done.5.refs_2_ = f32[320,128]{1,0:T(8,128)S(1)} collective-permute-done((f32[320,128]{1,0:T(8,128)S(1)}, f32[320,128]{1,0:T(8,128)S(1)}, u32[]{:S(2)}, u32[]{:S(2)}) %collective-permute-start.5) | collective-permute-done | bytes 163872 | tf_op jit(solution)/shard_map/ppermute | solution.py:473
  26.2 0.0 collective-permute-done.3.refs_0_
  26.2 0.0 collective-permute-done.4.refs_1_
  26.2 2.4 %relax.1 = (f32[160,128]{1,0:T(8,128)S(1)}, f32[20,64,128]{2,1,0:T(8,128)S(1)}, f32[20,64,128]{2,1,0:T(8,128)S(1)}) custom-call(s32[1]{0:T(128)} %bitcast.3.slab_ref, f32[384,128]{1,0:T(8,128)S(1)} %get-tuple-element.22.own_ref, f32[384,128]{1,0:T(8,128)S(1)} %collective-permute-done.3.refs_0_, f32[384,128]{1,0:T(8,128)S(1)} %collective-permute-done.4.refs_1_, ...), custom_call_target="tpu_custom_call" | custom-call | tf_op jit(solution)/shard_map/relax/pallas_call | solution.py:557
  28.6 0.0 copy-start
  28.6 0.0 copy-start.2
  28.6 0.0 collective-permute-done.7
  28.7 4.3 %collective-permute-start.8 = (f32[160,128]{1,0:T(8,128)S(1)}, f32[160,128]{1,0:T(8,128)S(1)}, u32[]{:S(2)}, u32[]{:S(2)}) collective-permute-start(f32[160,128]{1,0:T(8,128)S(1)} %get-tuple-element.33.refs_0_), channel_id=1, source_target_pairs={{4,8},{12,16},{20,24},{8,4},{16,12},{24,20},{5,9},{13,17},{21,25},... | collective-permute-start | bytes 245768 | tf_op jit(solution)/shard_map/ppermute | solution.py:473
  33.0 1.2 %collective-permute-start.9 = (f32[160,128]{1,0:T(8,128)S(1)}, f32[160,128]{1,0:T(8,128)S(1)}, u32[]{:S(2)}, u32[]{:S(2)}) collective-permute-start(f32[160,128]{1,0:T(8,128)S(1)} %get-tuple-element.33.refs_0_), channel_id=1, source_target_pairs={{0,4},{8,12},{16,20},{24,28},{4,0},{12,8},{20,16},{28,24},{1,5},{9... | collective-permute-start | bytes 245768 | tf_op jit(solution)/shard_map/ppermute | solution.py:473
  34.2 0.0 copy-done
  34.2 0.0 copy-done.2
  34.2 1.9 %solid.1.refs_1_ = f32[1,8192]{1,0:T(1,128)S(1)} custom-call(s32[1]{0:T(128)} %bitcast.place_ref, s32[4,8192]{1,0:T(4,128)S(1)} %copy-done, f32[1,8192]{1,0:T(1,128)S(1)} %bitcast.10, f32[2,128,128]{2,1,0:T(8,128)S(1)} %pad_maximum_fusion.2.held_ref), custom_call_target="tpu_custom_call" | custom-call | flops 1073741824 | bytes 1048576 | tf_op jit(solution)/shard_map/solid/pallas_call | solution.py:571
  36.1 0.0 collective-permute-done.8.refs_1_
  36.2 0.3 collective-permute-done.9.refs_2_
  36.5 0.9 %finish.1 = f32[224,128]{1,0:T(8,128)S(1)} custom-call(s32[1]{0:T(128)} %bitcast.3.slab_ref, f32[20,64,128]{2,1,0:T(8,128)S(1)} %get-tuple-element.31.offset_ref, f32[20,64,128]{2,1,0:T(8,128)S(1)} %get-tuple-element.32.gain_ref, f32[160,128]{1,0:T(8,128)S(1)} %get-tuple-element.33.refs_0_, f32[160,128]{1,0:T(8,128)S(1)} %collective-permute-done.8.refs_1_, ...), custom_call_target="tpu_custom_call" | custom-call | tf_op jit(solution)/shard_map/finish/pallas_call | solution.py:585
  37.4 2.5 %collective-permute-start.10 = (f32[1,224,128]{2,1,0:T(8,128)S(1)}, f32[1,224,128]{2,1,0:T(8,128)S(1)}, u32[]{:S(2)}, u32[]{:S(2)}) collective-permute-start(f32[1,224,128]{2,1,0:T(8,128)S(1)} %bitcast.6), channel_id=1, source_target_pairs={{0,2},{1,3},{2,0},{3,1},{4,6},{5,7},{6,4},{7,5},{8,10},{9,11},{10,... | collective-permute-start | bytes 344072 | tf_op jit(solution)/shard_map/ppermute | solution.py:464
  39.9 2.2 %sampled.2.refs_0_ = f32[3,8192]{1,0:T(4,128)S(1)} custom-call(s32[1]{0:T(128)} %bitcast.place_ref, s32[4,8192]{1,0:T(4,128)S(1)} %copy-done, f32[1,8192]{1,0:T(1,128)S(1)} %bitcast.11, f32[1,224,128]{2,1,0:T(8,128)S(1)} %bitcast.7), custom_call_target="tpu_custom_call" | custom-call | flops 1610612736 | bytes 1048576 | tf_op jit(solution)/shard_map/sampled/pallas_call | solution.py:596
  42.1 0.0 collective-permute-done.10
  42.2 0.0 copy-start.1
  42.2 0.0 copy-start.3
  42.2 3.5 %collective-permute-start.11 = (f32[2,352,128]{2,1,0:T(8,128)S(1)}, f32[2,352,128]{2,1,0:T(8,128)S(1)}, u32[]{:S(2)}, u32[]{:S(2)}) collective-permute-start(f32[2,352,128]{2,1,0:T(8,128)S(1)} %pad_maximum_fusion), channel_id=1, source_target_pairs={{0,1},{1,0},{2,3},{3,2},{4,5},{5,4},{6,7},{7,6},{8,9},{9,8},{10,11... | collective-permute-start | bytes 1081352 | tf_op jit(solution)/shard_map/ppermute | solution.py:464
  45.7 2.2 %sampled.3.refs_2_ = f32[3,8192]{1,0:T(4,128)S(1)} custom-call(s32[1]{0:T(128)} %bitcast.place_ref, s32[4,8192]{1,0:T(4,128)S(1)} %copy-done, f32[1,8192]{1,0:T(1,128)S(1)} %bitcast.12, f32[2,224,128]{2,1,0:T(8,128)S(1)} %pad_maximum_fusion.1.held_ref.refs_3_, f32[3,8192]{1,0:T(4,128)S(1)} %sampled.2.refs_0_), custom_call_target="tpu_custom_call" | custom-call | flops 1610612736 | bytes 1048576 | tf_op jit(solution)/shard_map/sampled/pallas_call | solution.py:596
  47.9 0.0 collective-permute-done.11.refs_4_
  47.9 0.0 copy-done.1
  47.9 0.0 copy-done.3
  47.9 5.9 %drag.1 = (f32[4,16,256]{2,1,0:T(8,128)}, f32[3,8192]{1,0:T(4,128)}) custom-call(s32[1]{0:T(128)} %bitcast.place_ref, s32[1]{0:T(128)S(6)} %copy.7.count_ref, s32[4,8192]{1,0:T(4,128)S(1)} %copy-done, f32[1,8192]{1,0:T(1,128)S(1)} %bitcast.13, f32[1,8192]{1,0:T(1,128)S(1)} %bitcast.15, f32[3,8192]{1,0:T(4,128)S(1)} %copy-done.1, ...), custom_call_target="tpu_custom_call" | custom-call | tf_op jit(solution)/shard_map/drag/pallas_call | solution.py:619
  (3 shorter events, 0.1 us)
Async XLA Ops:
  2.4 6.0 %collective-permute-start = (f32[4,8192]{1,0:T(4,128)S(1)}, f32[4,8192]{1,0:T(4,128)S(1)}, u32[]{:S(2)}, u32[]{:S(2)}) collective-permute-start(f32[4,8192]{1,0:T(4,128)S(1)} %grains.1.grain_ref), channel_id=1, source_target_pairs={{0,2},{1,3},{2,0},{3,1},{4,6},{5,7},{6,4},{7,5},{8,10},{9,11},{10,... | collective-permute-start | bytes 393224 | tf_op jit(solution)/shard_map/ppermute | solution.py:464
  3.7 2.9 %collective-permute-start.1 = (f32[4,8192]{1,0:T(4,128)S(1)}, f32[4,8192]{1,0:T(4,128)S(1)}, u32[]{:S(2)}, u32[]{:S(2)}) collective-permute-start(f32[4,8192]{1,0:T(4,128)S(1)} %grains.1.grain_ref), channel_id=1, source_target_pairs={{0,1},{1,0},{2,3},{3,2},{4,5},{5,4},{6,7},{7,6},{8,9},{9,8},{10,11... | collective-permute-start | bytes 393224 | tf_op jit(solution)/shard_map/ppermute | solution.py:464
  8.5 2.0 %collective-permute-start.2 = (f32[4,8192]{1,0:T(4,128)S(1)}, f32[4,8192]{1,0:T(4,128)S(1)}, u32[]{:S(2)}, u32[]{:S(2)}) collective-permute-start(f32[4,8192]{1,0:T(4,128)S(1)} %collective-permute-done.grain_ref), channel_id=1, source_target_pairs={{0,1},{1,0},{2,3},{3,2},{4,5},{5,4},{6,7},{7,6},{8,9},{9,8},{10,11... | collective-permute-start | bytes 393224 | tf_op jit(solution)/shard_map/ppermute | solution.py:464
  12.8 7.2 %collective-permute-start.6 = (f32[320,128]{1,0:T(8,128)S(1)}, f32[320,128]{1,0:T(8,128)S(1)}, u32[]{:S(2)}, u32[]{:S(2)}) collective-permute-start(f32[320,128]{1,0:T(8,128)S(1)} %get-tuple-element.23), channel_id=1, source_target_pairs={{8,16},{12,20},{16,8},{20,12},{9,17},{13,21},{17,9},{21,13},{10,18... | collective-permute-start | bytes 491528 | tf_op jit(solution)/shard_map/ppermute | solution.py:473
  16.0 10.2 %collective-permute-start.3 = (f32[384,128]{1,0:T(8,128)S(1)}, f32[384,128]{1,0:T(8,128)S(1)}, u32[]{:S(2)}, u32[]{:S(2)}) collective-permute-start(f32[384,128]{1,0:T(8,128)S(1)} %get-tuple-element.22.own_ref), channel_id=1, source_target_pairs={{0,4},{8,12},{16,20},{24,28},{4,0},{12,8},{20,16},{28,24},{1,5},{9... | collective-permute-start | bytes 589832 | tf_op jit(solution)/shard_map/ppermute | solution.py:473
  17.3 8.9 %collective-permute-start.4 = (f32[384,128]{1,0:T(8,128)S(1)}, f32[384,128]{1,0:T(8,128)S(1)}, u32[]{:S(2)}, u32[]{:S(2)}) collective-permute-start(f32[384,128]{1,0:T(8,128)S(1)} %get-tuple-element.22.own_ref), channel_id=1, source_target_pairs={{4,8},{12,16},{20,24},{8,4},{16,12},{24,20},{5,9},{13,17},{21,25},... | collective-permute-start | bytes 589832 | tf_op jit(solution)/shard_map/ppermute | solution.py:473
  19.2 6.9 %collective-permute-start.5 = (f32[320,128]{1,0:T(8,128)S(1)}, f32[320,128]{1,0:T(8,128)S(1)}, u32[]{:S(2)}, u32[]{:S(2)}) collective-permute-start(f32[320,128]{1,0:T(8,128)S(1)} %get-tuple-element.23), channel_id=1, source_target_pairs={{0,8},{4,12},{16,24},{20,28},{8,0},{12,4},{24,16},{28,20},{1,9},{5... | collective-permute-start | bytes 491528 | tf_op jit(solution)/shard_map/ppermute | solution.py:473
  20.0 8.7 %collective-permute-start.7 = (f32[1,128,128]{2,1,0:T(8,128)S(1)}, f32[1,128,128]{2,1,0:T(8,128)S(1)}, u32[]{:S(2)}, u32[]{:S(2)}) collective-permute-start(f32[1,128,128]{2,1,0:T(8,128)S(1)} %bitcast.16), channel_id=1, source_target_pairs={{0,2},{1,3},{2,0},{3,1},{4,6},{5,7},{6,4},{7,5},{8,10},{9,11},{10,... | collective-permute-start | bytes 196616 | tf_op jit(solution)/shard_map/ppermute | solution.py:464
  28.6 5.6 %copy-start = (s32[4,8192]{1,0:T(4,128)S(1)}, s32[4,8192]{1,0:T(4,128)}, u32[]{:S(2)}) copy-start(s32[4,8192]{1,0:T(4,128)} %cell_ref.7) | copy-start | bytes 393220
  28.6 5.6 %copy-start.2 = (f32[8192]{0:T(1024)S(1)}, f32[8192]{0:T(1024)}, u32[]{:S(2)}) copy-start(f32[8192]{0:T(1024)} %param.7) | copy-start | bytes 98308
  28.7 7.5 %collective-permute-start.8 = (f32[160,128]{1,0:T(8,128)S(1)}, f32[160,128]{1,0:T(8,128)S(1)}, u32[]{:S(2)}, u32[]{:S(2)}) collective-permute-start(f32[160,128]{1,0:T(8,128)S(1)} %get-tuple-element.33.refs_0_), channel_id=1, source_target_pairs={{4,8},{12,16},{20,24},{8,4},{16,12},{24,20},{5,9},{13,17},{21,25},... | collective-permute-start | bytes 245768 | tf_op jit(solution)/shard_map/ppermute | solution.py:473
  33.0 3.5 %collective-permute-start.9 = (f32[160,128]{1,0:T(8,128)S(1)}, f32[160,128]{1,0:T(8,128)S(1)}, u32[]{:S(2)}, u32[]{:S(2)}) collective-permute-start(f32[160,128]{1,0:T(8,128)S(1)} %get-tuple-element.33.refs_0_), channel_id=1, source_target_pairs={{0,4},{8,12},{16,20},{24,28},{4,0},{12,8},{20,16},{28,24},{1,5},{9... | collective-permute-start | bytes 245768 | tf_op jit(solution)/shard_map/ppermute | solution.py:473
  37.4 4.7 %collective-permute-start.10 = (f32[1,224,128]{2,1,0:T(8,128)S(1)}, f32[1,224,128]{2,1,0:T(8,128)S(1)}, u32[]{:S(2)}, u32[]{:S(2)}) collective-permute-start(f32[1,224,128]{2,1,0:T(8,128)S(1)} %bitcast.6), channel_id=1, source_target_pairs={{0,2},{1,3},{2,0},{3,1},{4,6},{5,7},{6,4},{7,5},{8,10},{9,11},{10,... | collective-permute-start | bytes 344072 | tf_op jit(solution)/shard_map/ppermute | solution.py:464
  42.2 5.7 %copy-start.1 = (f32[3,8192]{1,0:T(4,128)S(1)}, f32[3,8192]{1,0:T(4,128)}, u32[]{:S(2)}) copy-start(f32[3,8192]{1,0:T(4,128)} %refs_0_.3) | copy-start | bytes 294916
  42.2 5.7 %copy-start.3 = (f32[8192]{0:T(1024)S(1)}, f32[8192]{0:T(1024)}, u32[]{:S(2)}) copy-start(f32[8192]{0:T(1024)} %param.8) | copy-start | bytes 98308
  42.2 5.7 %collective-permute-start.11 = (f32[2,352,128]{2,1,0:T(8,128)S(1)}, f32[2,352,128]{2,1,0:T(8,128)S(1)}, u32[]{:S(2)}, u32[]{:S(2)}) collective-permute-start(f32[2,352,128]{2,1,0:T(8,128)S(1)} %pad_maximum_fusion), channel_id=1, source_target_pairs={{0,1},{1,0},{2,3},{3,2},{4,5},{5,4},{6,7},{7,6},{8,9},{9,8},{10,11... | collective-permute-start | bytes 1081352 | tf_op jit(solution)/shard_map/ppermute | solution.py:464

commit v8 on v7

--- a/solution.py
+++ b/solution.py
@@ -238,7 +238,7 @@
 
 
 def swap_plan(depth):
-    return [(distance, matching) for distance in range(1, depth + 1) for matching in range(2)]
+    return [(distance, matching) for distance in range(1, depth + 1) for matching in (1, 0)]
 
 
 def framed(last, first, own):
@@ -269,7 +269,7 @@
 def finish_kernel(quads, slab_ref, offset_ref, gain_ref, *refs):
     *parts, out_ref, even_ref, odd_ref = refs
     across, own = quads * CA, CB // quads
-    slots = [1] + [1 + slot_of(slab_ref[0], *swap) for swap in swap_plan(1)[::-1]]
+    slots = [1] + [1 + slot_of(slab_ref[0], *swap) for swap in swap_plan(1)]
     for slot, pressure in zip(slots, parts):
         (even_ref[pl.ds(slot * CH, CH)],) = unpack(pressure[...], 1, across, SUBLANES, own)
     near = pl.ds((DEPTH - 1) * CH, 3 * CH)
@@ -549,7 +549,7 @@
         swapped(distance, matching, coefs[distance - 1])
         for distance, matching in swap_plan(DEPTH)
     ]
-    stack[-1], solid = lax.optimization_barrier((stack[-1], solid))
+    stack[1], solid = lax.optimization_barrier((stack[1], solid))
     solids = nearly_all(solid)
     frame = cells(packed_rows(across, 1, SUBLANES, own) + 2 * tall, LANES)
     layers = CH * len(stack)
@@ -580,7 +580,7 @@
         name="solid",
     )(place, grain_cell, weight, solids)
 
-    pressures = [centre] + [swapped(*swap, centre) for swap in swap_plan(1)[::-1]]
+    pressures = [centre] + [swapped(*swap, centre) for swap in swap_plan(1)]
     pressures, solid_sampled = lax.optimization_barrier((pressures, solid_sampled))
     mine = pl.pallas_call(
         functools.partial(finish_kernel, quads),

time: 54.9 us -> 53.1 us (0.967); the launches traced: 53.8 us -> 52.9 us
  starting transfers between devices: 21.9 us -> 19.1 us
  waiting for transfers between devices: 5.62 us -> 7.57 us
    ppermute x6, starting transfers between devices: 9.88 us -> 6.62 us  [over_quad(): return lax.ppermute(value, 'quad', pairs)]
    ppermute x6, waiting for transfers between devices: 5.6 us -> 6.77 us  [swapped(): lax.ppermute(value, 'slab', pairs + [(high, low) for low, high in pairs])]
    ppermute x6, waiting for transfers between devices: 0.02 us -> 0.8 us  [over_quad(): return lax.ppermute(value, 'quad', pairs)]
  transfers between devices with their start and end apart: 12 -> 12, of which waited for: 3 -> 5; matrix products, arithmetic and copies ran while one was open for 0% -> 0% of each run, Pallas kernels for 27% -> 27%
where the time goes in v8:
time: 53.1 us; the launch traced here: 52.9 us
  Pallas kernels  24.7 us (47%)
  starting transfers between devices  19.1 us (36%)
  waiting for transfers between devices  7.57 us (14%)
  between operations  1.51 us (3%)
    ppermute x6, starting transfers between devices, swapped(): lax.ppermute(value, 'slab', pairs + [(high, low) for low, high in pairs])  12.5 us
    ppermute x6, waiting for transfers between devices, swapped(): lax.ppermute(value, 'slab', pairs + [(high, low) for low, high in pairs])  6.77 us
    ppermute x6, starting transfers between devices, over_quad(): return lax.ppermute(value, 'quad', pairs)  6.62 us
    pallas_call x1, Pallas kernels, body(): pl.pallas_call(functools.partial(drag_kernel, quads, grain_chunk), out_sh...  5.9 us
    pallas_call x3, Pallas kernels, deposited(): pl.pallas_call(functools.partial(deposit_kernel, quads, deposit_chunk), o...  5.68 us
    pallas_call x2, Pallas kernels, sampled_from(): pl.pallas_call(functools.partial(sampled_kernel, quads, grain_chunk, plac...  4.37 us
    pallas_call x1, Pallas kernels, body(): pl.pallas_call(functools.partial(relax_kernel, quads), out_shape=[cells(p...  2.42 us
    pallas_call x1, Pallas kernels, body(): pl.pallas_call(functools.partial(coefficient_kernel, quads, deposit_chunk...  2.33 us
  transfers between devices with their start and end apart: 12, of which 5 were waited for; matrix products, arithmetic and copies ran while one was open for 0% of the time, Pallas kernels for 27%

profile of v8, /device:TPU:9, one launch (start us, length us, event | category | flops | bytes accessed | tf_op | source)
XLA Modules:
  0.0 52.9 jit_solution(12951549593103857375)
XLA Ops:
  1.3 1.1 %grains.1.grain_ref = f32[4,8192]{1,0:T(4,128)S(1)} custom-call(s32[1]{0:T(128)S(6)} %copy.7.count_ref, s32[4,8192]{1,0:T(4,128)} %cell_ref.7, f32[1,8192]{1,0:T(1,128)} %bitcast.9, f32[1,8192]{1,0:T(1,128)} %bitcast.14, f32[3,8192]{1,0:T(4,128)} %refs_0_.3), custom_call_target="tpu_custom_call" | custom-call | tf_op jit(solution)/shard_map/grains/pallas_call | solution.py:486
  2.4 1.3 %collective-permute-start = (f32[4,8192]{1,0:T(4,128)S(1)}, f32[4,8192]{1,0:T(4,128)S(1)}, u32[]{:S(2)}, u32[]{:S(2)}) collective-permute-start(f32[4,8192]{1,0:T(4,128)S(1)} %grains.1.grain_ref), channel_id=1, source_target_pairs={{0,2},{1,3},{2,0},{3,1},{4,6},{5,7},{6,4},{7,5},{8,10},{9,11},{10,... | collective-permute-start | bytes 393224 | tf_op jit(solution)/shard_map/ppermute | solution.py:464
  3.7 1.0 %collective-permute-start.1 = (f32[4,8192]{1,0:T(4,128)S(1)}, f32[4,8192]{1,0:T(4,128)S(1)}, u32[]{:S(2)}, u32[]{:S(2)}) collective-permute-start(f32[4,8192]{1,0:T(4,128)S(1)} %grains.1.grain_ref), channel_id=1, source_target_pairs={{0,1},{1,0},{2,3},{3,2},{4,5},{5,4},{6,7},{7,6},{8,9},{9,8},{10,11... | collective-permute-start | bytes 393224 | tf_op jit(solution)/shard_map/ppermute | solution.py:464
  4.6 1.9 %deposit.3.refs_0_ = f32[384,256]{1,0:T(8,128)S(1)} custom-call(s32[1]{0:T(128)} %bitcast.place_ref, f32[4,8192]{1,0:T(4,128)S(1)} %grains.1.grain_ref), custom_call_target="tpu_custom_call" | custom-call | flops 1610612736 | bytes 1048576 | tf_op jit(solution)/shard_map/deposit/pallas_call | solution.py:516
  6.5 0.0 collective-permute-done.1.grain_ref
  6.5 1.9 %deposit.4.refs_0_ = f32[384,256]{1,0:T(8,128)S(1)} custom-call(s32[1]{0:T(128)} %bitcast.place_ref, f32[4,8192]{1,0:T(4,128)S(1)} %collective-permute-done.1.grain_ref, f32[384,256]{1,0:T(8,128)S(1)} %deposit.3.refs_0_), custom_call_target="tpu_custom_call" | custom-call | flops 1610612736 | bytes 1048576 | tf_op jit(solution)/shard_map/deposit/pallas_call | solution.py:516
  8.5 0.0 collective-permute-done.grain_ref
  8.5 0.1 collective-permute-start.2
  8.5 1.9 %deposit.5.refs_1_ = f32[384,256]{1,0:T(8,128)S(1)} custom-call(s32[1]{0:T(128)} %bitcast.place_ref, f32[4,8192]{1,0:T(4,128)S(1)} %collective-permute-done.grain_ref, f32[384,256]{1,0:T(8,128)S(1)} %deposit.4.refs_0_), custom_call_target="tpu_custom_call" | custom-call | flops 1610612736 | bytes 1048576 | tf_op jit(solution)/shard_map/deposit/pallas_call | solution.py:516
  10.4 0.0 collective-permute-done.2.refs_0_
  10.5 2.3 %coefficients.1 = (f32[384,128]{1,0:T(8,128)S(1)}, f32[320,128]{1,0:T(8,128)S(1)}, f32[128,128]{1,0:T(8,128)S(1)}) custom-call(s32[1]{0:T(128)} %bitcast.place_ref, f32[4,8192]{1,0:T(4,128)S(1)} %collective-permute-done.2.refs_0_, f32[384,256]{1,0:T(8,128)S(1)} %deposit.5.refs_1_), custom_call_target="tpu_custom_call" | custom-call | tf_op jit(solution)/shard_map/coefficients/pallas_call | solution.py:535
  12.8 3.0 %collective-permute-start.3 = (f32[384,128]{1,0:T(8,128)S(1)}, f32[384,128]{1,0:T(8,128)S(1)}, u32[]{:S(2)}, u32[]{:S(2)}) collective-permute-start(f32[384,128]{1,0:T(8,128)S(1)} %get-tuple-element.22.own_ref), channel_id=1, source_target_pairs={{4,8},{12,16},{20,24},{8,4},{16,12},{24,20},{5,9},{13,17},{21,25},... | collective-permute-start | bytes 589832 | tf_op jit(solution)/shard_map/ppermute | solution.py:473
  15.8 1.4 %collective-permute-start.4 = (f32[384,128]{1,0:T(8,128)S(1)}, f32[384,128]{1,0:T(8,128)S(1)}, u32[]{:S(2)}, u32[]{:S(2)}) collective-permute-start(f32[384,128]{1,0:T(8,128)S(1)} %get-tuple-element.22.own_ref), channel_id=1, source_target_pairs={{0,4},{8,12},{16,20},{24,28},{4,0},{12,8},{20,16},{28,24},{1,5},{9... | collective-permute-start | bytes 589832 | tf_op jit(solution)/shard_map/ppermute | solution.py:473
  17.2 3.2 %collective-permute-start.5 = (f32[320,128]{1,0:T(8,128)S(1)}, f32[320,128]{1,0:T(8,128)S(1)}, u32[]{:S(2)}, u32[]{:S(2)}) collective-permute-start(f32[320,128]{1,0:T(8,128)S(1)} %get-tuple-element.25), channel_id=1, source_target_pairs={{8,16},{12,20},{16,8},{20,12},{9,17},{13,21},{17,9},{21,13},{10,18... | collective-permute-start | bytes 491528 | tf_op jit(solution)/shard_map/ppermute | solution.py:473
  20.5 0.1 collective-permute-start.6
  20.5 1.1 %collective-permute-done.3.refs_0_ = f32[384,128]{1,0:T(8,128)S(1)} collective-permute-done((f32[384,128]{1,0:T(8,128)S(1)}, f32[384,128]{1,0:T(8,128)S(1)}, u32[]{:S(2)}, u32[]{:S(2)}) %collective-permute-start.3) | collective-permute-done | bytes 196640 | tf_op jit(solution)/shard_map/ppermute | solution.py:473
  21.6 1.6 %collective-permute-start.7 = (f32[1,128,128]{2,1,0:T(8,128)S(1)}, f32[1,128,128]{2,1,0:T(8,128)S(1)}, u32[]{:S(2)}, u32[]{:S(2)}) collective-permute-start(f32[1,128,128]{2,1,0:T(8,128)S(1)} %bitcast.16), channel_id=1, source_target_pairs={{0,2},{1,3},{2,0},{3,1},{4,6},{5,7},{6,4},{7,5},{8,10},{9,11},{10,... | collective-permute-start | bytes 196616 | tf_op jit(solution)/shard_map/ppermute | solution.py:464
  23.2 2.1 %collective-permute-done.5.refs_2_ = f32[320,128]{1,0:T(8,128)S(1)} collective-permute-done((f32[320,128]{1,0:T(8,128)S(1)}, f32[320,128]{1,0:T(8,128)S(1)}, u32[]{:S(2)}, u32[]{:S(2)}) %collective-permute-start.5) | collective-permute-done | bytes 163872 | tf_op jit(solution)/shard_map/ppermute | solution.py:473
  25.3 0.0 collective-permute-done.6.refs_3_
  25.3 1.3 %collective-permute-done.4.refs_1_ = f32[384,128]{1,0:T(8,128)S(1)} collective-permute-done((f32[384,128]{1,0:T(8,128)S(1)}, f32[384,128]{1,0:T(8,128)S(1)}, u32[]{:S(2)}, u32[]{:S(2)}) %collective-permute-start.4) | collective-permute-done | bytes 196640 | tf_op jit(solution)/shard_map/ppermute | solution.py:473
  26.6 2.4 %relax.1 = (f32[160,128]{1,0:T(8,128)S(1)}, f32[20,64,128]{2,1,0:T(8,128)S(1)}, f32[20,64,128]{2,1,0:T(8,128)S(1)}) custom-call(s32[1]{0:T(128)} %bitcast.3.slab_ref, f32[384,128]{1,0:T(8,128)S(1)} %get-tuple-element.22.own_ref, f32[384,128]{1,0:T(8,128)S(1)} %collective-permute-done.3.refs_0_, f32[384,128]{1,0:T(8,128)S(1)} %collective-permute-done.4.refs_1_, ...), custom_call_target="tpu_custom_call" | custom-call | tf_op jit(solution)/shard_map/relax/pallas_call | solution.py:557
  29.1 0.0 copy-start
  29.1 0.0 copy-start.2
  29.1 0.0 collective-permute-done.7
  29.1 3.3 %collective-permute-start.8 = (f32[160,128]{1,0:T(8,128)S(1)}, f32[160,128]{1,0:T(8,128)S(1)}, u32[]{:S(2)}, u32[]{:S(2)}) collective-permute-start(f32[160,128]{1,0:T(8,128)S(1)} %get-tuple-element.33.refs_0_), channel_id=1, source_target_pairs={{4,8},{12,16},{20,24},{8,4},{16,12},{24,20},{5,9},{13,17},{21,25},... | collective-permute-start | bytes 245768 | tf_op jit(solution)/shard_map/ppermute | solution.py:473
  32.5 1.4 %collective-permute-start.9 = (f32[160,128]{1,0:T(8,128)S(1)}, f32[160,128]{1,0:T(8,128)S(1)}, u32[]{:S(2)}, u32[]{:S(2)}) collective-permute-start(f32[160,128]{1,0:T(8,128)S(1)} %get-tuple-element.33.refs_0_), channel_id=1, source_target_pairs={{0,4},{8,12},{16,20},{24,28},{4,0},{12,8},{20,16},{28,24},{1,5},{9... | collective-permute-start | bytes 245768 | tf_op jit(solution)/shard_map/ppermute | solution.py:473
  33.9 0.0 copy-done
  33.9 0.0 copy-done.2
  33.9 1.9 %solid.1.refs_1_ = f32[1,8192]{1,0:T(1,128)S(1)} custom-call(s32[1]{0:T(128)} %bitcast.place_ref, s32[4,8192]{1,0:T(4,128)S(1)} %copy-done, f32[1,8192]{1,0:T(1,128)S(1)} %bitcast.10, f32[2,128,128]{2,1,0:T(8,128)S(1)} %pad_maximum_fusion.2.held_ref), custom_call_target="tpu_custom_call" | custom-call | flops 1073741824 | bytes 1048576 | tf_op jit(solution)/shard_map/solid/pallas_call | solution.py:571
  35.8 0.0 collective-permute-done.8.refs_1_
  35.8 2.3 %collective-permute-done.9.refs_2_ = f32[160,128]{1,0:T(8,128)S(1)} collective-permute-done((f32[160,128]{1,0:T(8,128)S(1)}, f32[160,128]{1,0:T(8,128)S(1)}, u32[]{:S(2)}, u32[]{:S(2)}) %collective-permute-start.9) | collective-permute-done | bytes 81952 | tf_op jit(solution)/shard_map/ppermute | solution.py:473
  38.1 0.9 %finish.1 = f32[224,128]{1,0:T(8,128)S(1)} custom-call(s32[1]{0:T(128)} %bitcast.3.slab_ref, f32[20,64,128]{2,1,0:T(8,128)S(1)} %get-tuple-element.31.offset_ref, f32[20,64,128]{2,1,0:T(8,128)S(1)} %get-tuple-element.32.gain_ref, f32[160,128]{1,0:T(8,128)S(1)} %get-tuple-element.33.refs_0_, f32[160,128]{1,0:T(8,128)S(1)} %collective-permute-done.8.refs_1_, ...), custom_call_target="tpu_custom_call" | custom-call | tf_op jit(solution)/shard_map/finish/pallas_call | solution.py:585
  39.0 1.2 %collective-permute-start.10 = (f32[1,224,128]{2,1,0:T(8,128)S(1)}, f32[1,224,128]{2,1,0:T(8,128)S(1)}, u32[]{:S(2)}, u32[]{:S(2)}) collective-permute-start(f32[1,224,128]{2,1,0:T(8,128)S(1)} %bitcast.6), channel_id=1, source_target_pairs={{0,2},{1,3},{2,0},{3,1},{4,6},{5,7},{6,4},{7,5},{8,10},{9,11},{10,... | collective-permute-start | bytes 344072 | tf_op jit(solution)/shard_map/ppermute | solution.py:464
  40.2 2.2 %sampled.2.refs_0_ = f32[3,8192]{1,0:T(4,128)S(1)} custom-call(s32[1]{0:T(128)} %bitcast.place_ref, s32[4,8192]{1,0:T(4,128)S(1)} %copy-done, f32[1,8192]{1,0:T(1,128)S(1)} %bitcast.11, f32[1,224,128]{2,1,0:T(8,128)S(1)} %bitcast.7), custom_call_target="tpu_custom_call" | custom-call | flops 1610612736 | bytes 1048576 | tf_op jit(solution)/shard_map/sampled/pallas_call | solution.py:596
  42.4 0.8 %collective-permute-done.10 = f32[1,224,128]{2,1,0:T(8,128)S(1)} collective-permute-done((f32[1,224,128]{2,1,0:T(8,128)S(1)}, f32[1,224,128]{2,1,0:T(8,128)S(1)}, u32[]{:S(2)}, u32[]{:S(2)}) %collective-permute-start.10) | collective-permute-done | bytes 114720 | tf_op jit(solution)/shard_map/ppermute | solution.py:464
  43.2 0.0 copy-start.1
  43.2 0.0 copy-start.3
  43.3 1.5 %collective-permute-start.11 = (f32[2,352,128]{2,1,0:T(8,128)S(1)}, f32[2,352,128]{2,1,0:T(8,128)S(1)}, u32[]{:S(2)}, u32[]{:S(2)}) collective-permute-start(f32[2,352,128]{2,1,0:T(8,128)S(1)} %pad_maximum_fusion), channel_id=1, source_target_pairs={{0,1},{1,0},{2,3},{3,2},{4,5},{5,4},{6,7},{7,6},{8,9},{9,8},{10,11... | collective-permute-start | bytes 1081352 | tf_op jit(solution)/shard_map/ppermute | solution.py:464
  44.8 2.2 %sampled.3.refs_2_ = f32[3,8192]{1,0:T(4,128)S(1)} custom-call(s32[1]{0:T(128)} %bitcast.place_ref, s32[4,8192]{1,0:T(4,128)S(1)} %copy-done, f32[1,8192]{1,0:T(1,128)S(1)} %bitcast.12, f32[2,224,128]{2,1,0:T(8,128)S(1)} %pad_maximum_fusion.1.held_ref.refs_3_, f32[3,8192]{1,0:T(4,128)S(1)} %sampled.2.refs_0_), custom_call_target="tpu_custom_call" | custom-call | flops 1610612736 | bytes 1048576 | tf_op jit(solution)/shard_map/sampled/pallas_call | solution.py:596
  47.0 0.0 collective-permute-done.11.refs_4_
  47.0 0.0 copy-done.1
  47.0 0.0 copy-done.3
  47.0 5.9 %drag.1 = (f32[4,16,256]{2,1,0:T(8,128)}, f32[3,8192]{1,0:T(4,128)}) custom-call(s32[1]{0:T(128)} %bitcast.place_ref, s32[1]{0:T(128)S(6)} %copy.7.count_ref, s32[4,8192]{1,0:T(4,128)S(1)} %copy-done, f32[1,8192]{1,0:T(1,128)S(1)} %bitcast.13, f32[1,8192]{1,0:T(1,128)S(1)} %bitcast.15, f32[3,8192]{1,0:T(4,128)S(1)} %copy-done.1, ...), custom_call_target="tpu_custom_call" | custom-call | tf_op jit(solution)/shard_map/drag/pallas_call | solution.py:619
  (3 shorter events, 0.1 us)
Async XLA Ops:
  2.4 6.0 %collective-permute-start = (f32[4,8192]{1,0:T(4,128)S(1)}, f32[4,8192]{1,0:T(4,128)S(1)}, u32[]{:S(2)}, u32[]{:S(2)}) collective-permute-start(f32[4,8192]{1,0:T(4,128)S(1)} %grains.1.grain_ref), channel_id=1, source_target_pairs={{0,2},{1,3},{2,0},{3,1},{4,6},{5,7},{6,4},{7,5},{8,10},{9,11},{10,... | collective-permute-start | bytes 393224 | tf_op jit(solution)/shard_map/ppermute | solution.py:464
  3.7 2.9 %collective-permute-start.1 = (f32[4,8192]{1,0:T(4,128)S(1)}, f32[4,8192]{1,0:T(4,128)S(1)}, u32[]{:S(2)}, u32[]{:S(2)}) collective-permute-start(f32[4,8192]{1,0:T(4,128)S(1)} %grains.1.grain_ref), channel_id=1, source_target_pairs={{0,1},{1,0},{2,3},{3,2},{4,5},{5,4},{6,7},{7,6},{8,9},{9,8},{10,11... | collective-permute-start | bytes 393224 | tf_op jit(solution)/shard_map/ppermute | solution.py:464
  8.5 2.0 %collective-permute-start.2 = (f32[4,8192]{1,0:T(4,128)S(1)}, f32[4,8192]{1,0:T(4,128)S(1)}, u32[]{:S(2)}, u32[]{:S(2)}) collective-permute-start(f32[4,8192]{1,0:T(4,128)S(1)} %collective-permute-done.grain_ref), channel_id=1, source_target_pairs={{0,1},{1,0},{2,3},{3,2},{4,5},{5,4},{6,7},{7,6},{8,9},{9,8},{10,11... | collective-permute-start | bytes 393224 | tf_op jit(solution)/shard_map/ppermute | solution.py:464
  12.8 8.8 %collective-permute-start.3 = (f32[384,128]{1,0:T(8,128)S(1)}, f32[384,128]{1,0:T(8,128)S(1)}, u32[]{:S(2)}, u32[]{:S(2)}) collective-permute-start(f32[384,128]{1,0:T(8,128)S(1)} %get-tuple-element.22.own_ref), channel_id=1, source_target_pairs={{4,8},{12,16},{20,24},{8,4},{16,12},{24,20},{5,9},{13,17},{21,25},... | collective-permute-start | bytes 589832 | tf_op jit(solution)/shard_map/ppermute | solution.py:473
  15.8 10.8 %collective-permute-start.4 = (f32[384,128]{1,0:T(8,128)S(1)}, f32[384,128]{1,0:T(8,128)S(1)}, u32[]{:S(2)}, u32[]{:S(2)}) collective-permute-start(f32[384,128]{1,0:T(8,128)S(1)} %get-tuple-element.22.own_ref), channel_id=1, source_target_pairs={{0,4},{8,12},{16,20},{24,28},{4,0},{12,8},{20,16},{28,24},{1,5},{9... | collective-permute-start | bytes 589832 | tf_op jit(solution)/shard_map/ppermute | solution.py:473
  17.2 8.1 %collective-permute-start.5 = (f32[320,128]{1,0:T(8,128)S(1)}, f32[320,128]{1,0:T(8,128)S(1)}, u32[]{:S(2)}, u32[]{:S(2)}) collective-permute-start(f32[320,128]{1,0:T(8,128)S(1)} %get-tuple-element.25), channel_id=1, source_target_pairs={{8,16},{12,20},{16,8},{20,12},{9,17},{13,21},{17,9},{21,13},{10,18... | collective-permute-start | bytes 491528 | tf_op jit(solution)/shard_map/ppermute | solution.py:473
  20.5 4.9 %collective-permute-start.6 = (f32[320,128]{1,0:T(8,128)S(1)}, f32[320,128]{1,0:T(8,128)S(1)}, u32[]{:S(2)}, u32[]{:S(2)}) collective-permute-start(f32[320,128]{1,0:T(8,128)S(1)} %get-tuple-element.25), channel_id=1, source_target_pairs={{0,8},{4,12},{16,24},{20,28},{8,0},{12,4},{24,16},{28,20},{1,9},{5... | collective-permute-start | bytes 491528 | tf_op jit(solution)/shard_map/ppermute | solution.py:473
  21.6 7.5 %collective-permute-start.7 = (f32[1,128,128]{2,1,0:T(8,128)S(1)}, f32[1,128,128]{2,1,0:T(8,128)S(1)}, u32[]{:S(2)}, u32[]{:S(2)}) collective-permute-start(f32[1,128,128]{2,1,0:T(8,128)S(1)} %bitcast.16), channel_id=1, source_target_pairs={{0,2},{1,3},{2,0},{3,1},{4,6},{5,7},{6,4},{7,5},{8,10},{9,11},{10,... | collective-permute-start | bytes 196616 | tf_op jit(solution)/shard_map/ppermute | solution.py:464
  29.1 4.8 %copy-start = (s32[4,8192]{1,0:T(4,128)S(1)}, s32[4,8192]{1,0:T(4,128)}, u32[]{:S(2)}) copy-start(s32[4,8192]{1,0:T(4,128)} %cell_ref.7) | copy-start | bytes 393220
  29.1 4.8 %copy-start.2 = (f32[8192]{0:T(1024)S(1)}, f32[8192]{0:T(1024)}, u32[]{:S(2)}) copy-start(f32[8192]{0:T(1024)} %param.7) | copy-start | bytes 98308
  29.1 6.7 %collective-permute-start.8 = (f32[160,128]{1,0:T(8,128)S(1)}, f32[160,128]{1,0:T(8,128)S(1)}, u32[]{:S(2)}, u32[]{:S(2)}) collective-permute-start(f32[160,128]{1,0:T(8,128)S(1)} %get-tuple-element.33.refs_0_), channel_id=1, source_target_pairs={{4,8},{12,16},{20,24},{8,4},{16,12},{24,20},{5,9},{13,17},{21,25},... | collective-permute-start | bytes 245768 | tf_op jit(solution)/shard_map/ppermute | solution.py:473
  32.5 5.6 %collective-permute-start.9 = (f32[160,128]{1,0:T(8,128)S(1)}, f32[160,128]{1,0:T(8,128)S(1)}, u32[]{:S(2)}, u32[]{:S(2)}) collective-permute-start(f32[160,128]{1,0:T(8,128)S(1)} %get-tuple-element.33.refs_0_), channel_id=1, source_target_pairs={{0,4},{8,12},{16,20},{24,28},{4,0},{12,8},{20,16},{28,24},{1,5},{9... | collective-permute-start | bytes 245768 | tf_op jit(solution)/shard_map/ppermute | solution.py:473
  39.0 4.2 %collective-permute-start.10 = (f32[1,224,128]{2,1,0:T(8,128)S(1)}, f32[1,224,128]{2,1,0:T(8,128)S(1)}, u32[]{:S(2)}, u32[]{:S(2)}) collective-permute-start(f32[1,224,128]{2,1,0:T(8,128)S(1)} %bitcast.6), channel_id=1, source_target_pairs={{0,2},{1,3},{2,0},{3,1},{4,6},{5,7},{6,4},{7,5},{8,10},{9,11},{10,... | collective-permute-start | bytes 344072 | tf_op jit(solution)/shard_map/ppermute | solution.py:464
  43.2 3.7 %copy-start.1 = (f32[3,8192]{1,0:T(4,128)S(1)}, f32[3,8192]{1,0:T(4,128)}, u32[]{:S(2)}) copy-start(f32[3,8192]{1,0:T(4,128)} %refs_0_.3) | copy-start | bytes 294916
  43.2 3.7 %copy-start.3 = (f32[8192]{0:T(1024)S(1)}, f32[8192]{0:T(1024)}, u32[]{:S(2)}) copy-start(f32[8192]{0:T(1024)} %param.8) | copy-start | bytes 98308
  43.3 3.7 %collective-permute-start.11 = (f32[2,352,128]{2,1,0:T(8,128)S(1)}, f32[2,352,128]{2,1,0:T(8,128)S(1)}, u32[]{:S(2)}, u32[]{:S(2)}) collective-permute-start(f32[2,352,128]{2,1,0:T(8,128)S(1)} %pad_maximum_fusion), channel_id=1, source_target_pairs={{0,1},{1,0},{2,3},{3,2},{4,5},{5,4},{6,7},{7,6},{8,9},{9,8},{10,11... | collective-permute-start | bytes 1081352 | tf_op jit(solution)/shard_map/ppermute | solution.py:464

commit v9 on v8

--- a/solution.py
+++ b/solution.py
@@ -238,7 +238,7 @@
 
 
 def swap_plan(depth):
-    return [(distance, matching) for distance in range(1, depth + 1) for matching in (1, 0)]
+    return [(distance, matching) for distance in range(1, depth + 1) for matching in ((1, 0) if distance == 1 else (0, 1))]
 
 
 def framed(last, first, own):

time: 53.1 us -> 53.1 us (level)
  no operation moved by 1% of the time
where the time goes in v9:
time: 53.1 us; the launch traced here: 52.9 us
  Pallas kernels  24.7 us (47%)
  starting transfers between devices  18.9 us (36%)
  waiting for transfers between devices  7.78 us (15%)
  between operations  1.5 us (3%)
    ppermute x6, starting transfers between devices, swapped(): lax.ppermute(value, 'slab', pairs + [(high, low) for low, high in pairs])  12.4 us
    ppermute x6, waiting for transfers between devices, swapped(): lax.ppermute(value, 'slab', pairs + [(high, low) for low, high in pairs])  6.87 us
    ppermute x6, starting transfers between devices, over_quad(): return lax.ppermute(value, 'quad', pairs)  6.51 us
    pallas_call x1, Pallas kernels, body(): pl.pallas_call(functools.partial(drag_kernel, quads, grain_chunk), out_sh...  5.89 us
    pallas_call x3, Pallas kernels, deposited(): pl.pallas_call(functools.partial(deposit_kernel, quads, deposit_chunk), o...  5.68 us
    pallas_call x2, Pallas kernels, sampled_from(): pl.pallas_call(functools.partial(sampled_kernel, quads, grain_chunk, plac...  4.37 us
    pallas_call x1, Pallas kernels, body(): pl.pallas_call(functools.partial(relax_kernel, quads), out_shape=[cells(p...  2.42 us
    pallas_call x1, Pallas kernels, body(): pl.pallas_call(functools.partial(coefficient_kernel, quads, deposit_chunk...  2.33 us
  transfers between devices with their start and end apart: 12, of which 5 were waited for; matrix products, arithmetic and copies ran while one was open for 0% of the time, Pallas kernels for 27%

profile of v9, /device:TPU:9, one launch (start us, length us, event | category | flops | bytes accessed | tf_op | source)
XLA Modules:
  0.0 52.9 jit_solution(7018240784617156262)
XLA Ops:
  1.3 1.1 %grains.1.grain_ref = f32[4,8192]{1,0:T(4,128)S(1)} custom-call(s32[1]{0:T(128)S(6)} %copy.7.count_ref, s32[4,8192]{1,0:T(4,128)} %cell_ref.7, f32[1,8192]{1,0:T(1,128)} %bitcast.9, f32[1,8192]{1,0:T(1,128)} %bitcast.14, f32[3,8192]{1,0:T(4,128)} %refs_0_.3), custom_call_target="tpu_custom_call" | custom-call | tf_op jit(solution)/shard_map/grains/pallas_call | solution.py:486
  2.4 1.3 %collective-permute-start = (f32[4,8192]{1,0:T(4,128)S(1)}, f32[4,8192]{1,0:T(4,128)S(1)}, u32[]{:S(2)}, u32[]{:S(2)}) collective-permute-start(f32[4,8192]{1,0:T(4,128)S(1)} %grains.1.grain_ref), channel_id=1, source_target_pairs={{0,2},{1,3},{2,0},{3,1},{4,6},{5,7},{6,4},{7,5},{8,10},{9,11},{10,... | collective-permute-start | bytes 393224 | tf_op jit(solution)/shard_map/ppermute | solution.py:464
  3.7 1.0 %collective-permute-start.1 = (f32[4,8192]{1,0:T(4,128)S(1)}, f32[4,8192]{1,0:T(4,128)S(1)}, u32[]{:S(2)}, u32[]{:S(2)}) collective-permute-start(f32[4,8192]{1,0:T(4,128)S(1)} %grains.1.grain_ref), channel_id=1, source_target_pairs={{0,1},{1,0},{2,3},{3,2},{4,5},{5,4},{6,7},{7,6},{8,9},{9,8},{10,11... | collective-permute-start | bytes 393224 | tf_op jit(solution)/shard_map/ppermute | solution.py:464
  4.6 1.9 %deposit.3.refs_0_ = f32[384,256]{1,0:T(8,128)S(1)} custom-call(s32[1]{0:T(128)} %bitcast.place_ref, f32[4,8192]{1,0:T(4,128)S(1)} %grains.1.grain_ref), custom_call_target="tpu_custom_call" | custom-call | flops 1610612736 | bytes 1048576 | tf_op jit(solution)/shard_map/deposit/pallas_call | solution.py:516
  6.5 0.0 collective-permute-done.1.grain_ref
  6.5 1.9 %deposit.4.refs_0_ = f32[384,256]{1,0:T(8,128)S(1)} custom-call(s32[1]{0:T(128)} %bitcast.place_ref, f32[4,8192]{1,0:T(4,128)S(1)} %collective-permute-done.1.grain_ref, f32[384,256]{1,0:T(8,128)S(1)} %deposit.3.refs_0_), custom_call_target="tpu_custom_call" | custom-call | flops 1610612736 | bytes 1048576 | tf_op jit(solution)/shard_map/deposit/pallas_call | solution.py:516
  8.5 0.0 collective-permute-done.grain_ref
  8.5 0.1 collective-permute-start.2
  8.5 1.9 %deposit.5.refs_1_ = f32[384,256]{1,0:T(8,128)S(1)} custom-call(s32[1]{0:T(128)} %bitcast.place_ref, f32[4,8192]{1,0:T(4,128)S(1)} %collective-permute-done.grain_ref, f32[384,256]{1,0:T(8,128)S(1)} %deposit.4.refs_0_), custom_call_target="tpu_custom_call" | custom-call | flops 1610612736 | bytes 1048576 | tf_op jit(solution)/shard_map/deposit/pallas_call | solution.py:516
  10.4 0.0 collective-permute-done.2.refs_0_
  10.5 2.3 %coefficients.1 = (f32[384,128]{1,0:T(8,128)S(1)}, f32[320,128]{1,0:T(8,128)S(1)}, f32[128,128]{1,0:T(8,128)S(1)}) custom-call(s32[1]{0:T(128)} %bitcast.place_ref, f32[4,8192]{1,0:T(4,128)S(1)} %collective-permute-done.2.refs_0_, f32[384,256]{1,0:T(8,128)S(1)} %deposit.5.refs_1_), custom_call_target="tpu_custom_call" | custom-call | tf_op jit(solution)/shard_map/coefficients/pallas_call | solution.py:535
  12.8 3.0 %collective-permute-start.3 = (f32[384,128]{1,0:T(8,128)S(1)}, f32[384,128]{1,0:T(8,128)S(1)}, u32[]{:S(2)}, u32[]{:S(2)}) collective-permute-start(f32[384,128]{1,0:T(8,128)S(1)} %get-tuple-element.22.own_ref), channel_id=1, source_target_pairs={{4,8},{12,16},{20,24},{8,4},{16,12},{24,20},{5,9},{13,17},{21,25},... | collective-permute-start | bytes 589832 | tf_op jit(solution)/shard_map/ppermute | solution.py:473
  15.8 1.4 %collective-permute-start.4 = (f32[384,128]{1,0:T(8,128)S(1)}, f32[384,128]{1,0:T(8,128)S(1)}, u32[]{:S(2)}, u32[]{:S(2)}) collective-permute-start(f32[384,128]{1,0:T(8,128)S(1)} %get-tuple-element.22.own_ref), channel_id=1, source_target_pairs={{0,4},{8,12},{16,20},{24,28},{4,0},{12,8},{20,16},{28,24},{1,5},{9... | collective-permute-start | bytes 589832 | tf_op jit(solution)/shard_map/ppermute | solution.py:473
  17.2 0.2 collective-permute-start.5
  17.4 3.0 %collective-permute-start.6 = (f32[320,128]{1,0:T(8,128)S(1)}, f32[320,128]{1,0:T(8,128)S(1)}, u32[]{:S(2)}, u32[]{:S(2)}) collective-permute-start(f32[320,128]{1,0:T(8,128)S(1)} %get-tuple-element.25), channel_id=1, source_target_pairs={{8,16},{12,20},{16,8},{20,12},{9,17},{13,21},{17,9},{21,13},{10,18... | collective-permute-start | bytes 491528 | tf_op jit(solution)/shard_map/ppermute | solution.py:473
  20.5 1.1 %collective-permute-done.3.refs_0_ = f32[384,128]{1,0:T(8,128)S(1)} collective-permute-done((f32[384,128]{1,0:T(8,128)S(1)}, f32[384,128]{1,0:T(8,128)S(1)}, u32[]{:S(2)}, u32[]{:S(2)}) %collective-permute-start.3) | collective-permute-done | bytes 196640 | tf_op jit(solution)/shard_map/ppermute | solution.py:473
  21.6 1.6 %collective-permute-start.7 = (f32[1,128,128]{2,1,0:T(8,128)S(1)}, f32[1,128,128]{2,1,0:T(8,128)S(1)}, u32[]{:S(2)}, u32[]{:S(2)}) collective-permute-start(f32[1,128,128]{2,1,0:T(8,128)S(1)} %bitcast.16), channel_id=1, source_target_pairs={{0,2},{1,3},{2,0},{3,1},{4,6},{5,7},{6,4},{7,5},{8,10},{9,11},{10,... | collective-permute-start | bytes 196616 | tf_op jit(solution)/shard_map/ppermute | solution.py:464
  23.2 0.0 collective-permute-done.5.refs_2_
  23.2 1.6 %collective-permute-done.6.refs_3_ = f32[320,128]{1,0:T(8,128)S(1)} collective-permute-done((f32[320,128]{1,0:T(8,128)S(1)}, f32[320,128]{1,0:T(8,128)S(1)}, u32[]{:S(2)}, u32[]{:S(2)}) %collective-permute-start.6) | collective-permute-done | bytes 163872 | tf_op jit(solution)/shard_map/ppermute | solution.py:473
  24.9 1.8 %collective-permute-done.4.refs_1_ = f32[384,128]{1,0:T(8,128)S(1)} collective-permute-done((f32[384,128]{1,0:T(8,128)S(1)}, f32[384,128]{1,0:T(8,128)S(1)}, u32[]{:S(2)}, u32[]{:S(2)}) %collective-permute-start.4) | collective-permute-done | bytes 196640 | tf_op jit(solution)/shard_map/ppermute | solution.py:473
  26.6 2.4 %relax.1 = (f32[160,128]{1,0:T(8,128)S(1)}, f32[20,64,128]{2,1,0:T(8,128)S(1)}, f32[20,64,128]{2,1,0:T(8,128)S(1)}) custom-call(s32[1]{0:T(128)} %bitcast.3.slab_ref, f32[384,128]{1,0:T(8,128)S(1)} %get-tuple-element.22.own_ref, f32[384,128]{1,0:T(8,128)S(1)} %collective-permute-done.3.refs_0_, f32[384,128]{1,0:T(8,128)S(1)} %collective-permute-done.4.refs_1_, ...), custom_call_target="tpu_custom_call" | custom-call | tf_op jit(solution)/shard_map/relax/pallas_call | solution.py:557
  29.1 0.0 copy-start
  29.1 0.0 copy-start.2
  29.1 0.0 collective-permute-done.7
  29.1 3.3 %collective-permute-start.8 = (f32[160,128]{1,0:T(8,128)S(1)}, f32[160,128]{1,0:T(8,128)S(1)}, u32[]{:S(2)}, u32[]{:S(2)}) collective-permute-start(f32[160,128]{1,0:T(8,128)S(1)} %get-tuple-element.33.refs_0_), channel_id=1, source_target_pairs={{4,8},{12,16},{20,24},{8,4},{16,12},{24,20},{5,9},{13,17},{21,25},... | collective-permute-start | bytes 245768 | tf_op jit(solution)/shard_map/ppermute | solution.py:473
  32.5 1.4 %collective-permute-start.9 = (f32[160,128]{1,0:T(8,128)S(1)}, f32[160,128]{1,0:T(8,128)S(1)}, u32[]{:S(2)}, u32[]{:S(2)}) collective-permute-start(f32[160,128]{1,0:T(8,128)S(1)} %get-tuple-element.33.refs_0_), channel_id=1, source_target_pairs={{0,4},{8,12},{16,20},{24,28},{4,0},{12,8},{20,16},{28,24},{1,5},{9... | collective-permute-start | bytes 245768 | tf_op jit(solution)/shard_map/ppermute | solution.py:473
  33.9 0.0 copy-done
  33.9 0.0 copy-done.2
  33.9 1.9 %solid.1.refs_1_ = f32[1,8192]{1,0:T(1,128)S(1)} custom-call(s32[1]{0:T(128)} %bitcast.place_ref, s32[4,8192]{1,0:T(4,128)S(1)} %copy-done, f32[1,8192]{1,0:T(1,128)S(1)} %bitcast.10, f32[2,128,128]{2,1,0:T(8,128)S(1)} %pad_maximum_fusion.2.held_ref), custom_call_target="tpu_custom_call" | custom-call | flops 1073741824 | bytes 1048576 | tf_op jit(solution)/shard_map/solid/pallas_call | solution.py:571
  35.8 0.0 collective-permute-done.8.refs_1_
  35.8 2.3 %collective-permute-done.9.refs_2_ = f32[160,128]{1,0:T(8,128)S(1)} collective-permute-done((f32[160,128]{1,0:T(8,128)S(1)}, f32[160,128]{1,0:T(8,128)S(1)}, u32[]{:S(2)}, u32[]{:S(2)}) %collective-permute-start.9) | collective-permute-done | bytes 81952 | tf_op jit(solution)/shard_map/ppermute | solution.py:473
  38.1 0.9 %finish.1 = f32[224,128]{1,0:T(8,128)S(1)} custom-call(s32[1]{0:T(128)} %bitcast.3.slab_ref, f32[20,64,128]{2,1,0:T(8,128)S(1)} %get-tuple-element.31.offset_ref, f32[20,64,128]{2,1,0:T(8,128)S(1)} %get-tuple-element.32.gain_ref, f32[160,128]{1,0:T(8,128)S(1)} %get-tuple-element.33.refs_0_, f32[160,128]{1,0:T(8,128)S(1)} %collective-permute-done.8.refs_1_, ...), custom_call_target="tpu_custom_call" | custom-call | tf_op jit(solution)/shard_map/finish/pallas_call | solution.py:585
  39.1 1.2 %collective-permute-start.10 = (f32[1,224,128]{2,1,0:T(8,128)S(1)}, f32[1,224,128]{2,1,0:T(8,128)S(1)}, u32[]{:S(2)}, u32[]{:S(2)}) collective-permute-start(f32[1,224,128]{2,1,0:T(8,128)S(1)} %bitcast.6), channel_id=1, source_target_pairs={{0,2},{1,3},{2,0},{3,1},{4,6},{5,7},{6,4},{7,5},{8,10},{9,11},{10,... | collective-permute-start | bytes 344072 | tf_op jit(solution)/shard_map/ppermute | solution.py:464
  40.2 2.2 %sampled.2.refs_0_ = f32[3,8192]{1,0:T(4,128)S(1)} custom-call(s32[1]{0:T(128)} %bitcast.place_ref, s32[4,8192]{1,0:T(4,128)S(1)} %copy-done, f32[1,8192]{1,0:T(1,128)S(1)} %bitcast.11, f32[1,224,128]{2,1,0:T(8,128)S(1)} %bitcast.7), custom_call_target="tpu_custom_call" | custom-call | flops 1610612736 | bytes 1048576 | tf_op jit(solution)/shard_map/sampled/pallas_call | solution.py:596
  42.4 0.9 %collective-permute-done.10 = f32[1,224,128]{2,1,0:T(8,128)S(1)} collective-permute-done((f32[1,224,128]{2,1,0:T(8,128)S(1)}, f32[1,224,128]{2,1,0:T(8,128)S(1)}, u32[]{:S(2)}, u32[]{:S(2)}) %collective-permute-start.10) | collective-permute-done | bytes 114720 | tf_op jit(solution)/shard_map/ppermute | solution.py:464
  43.4 0.0 copy-start.1
  43.4 0.0 copy-start.3
  43.4 1.4 %collective-permute-start.11 = (f32[2,352,128]{2,1,0:T(8,128)S(1)}, f32[2,352,128]{2,1,0:T(8,128)S(1)}, u32[]{:S(2)}, u32[]{:S(2)}) collective-permute-start(f32[2,352,128]{2,1,0:T(8,128)S(1)} %pad_maximum_fusion), channel_id=1, source_target_pairs={{0,1},{1,0},{2,3},{3,2},{4,5},{5,4},{6,7},{7,6},{8,9},{9,8},{10,11... | collective-permute-start | bytes 1081352 | tf_op jit(solution)/shard_map/ppermute | solution.py:464
  44.8 2.2 %sampled.3.refs_2_ = f32[3,8192]{1,0:T(4,128)S(1)} custom-call(s32[1]{0:T(128)} %bitcast.place_ref, s32[4,8192]{1,0:T(4,128)S(1)} %copy-done, f32[1,8192]{1,0:T(1,128)S(1)} %bitcast.12, f32[2,224,128]{2,1,0:T(8,128)S(1)} %pad_maximum_fusion.1.held_ref.refs_3_, f32[3,8192]{1,0:T(4,128)S(1)} %sampled.2.refs_0_), custom_call_target="tpu_custom_call" | custom-call | flops 1610612736 | bytes 1048576 | tf_op jit(solution)/shard_map/sampled/pallas_call | solution.py:596
  47.0 0.0 collective-permute-done.11.refs_4_
  47.0 0.0 copy-done.1
  47.0 0.0 copy-done.3
  47.1 5.9 %drag.1 = (f32[4,16,256]{2,1,0:T(8,128)}, f32[3,8192]{1,0:T(4,128)}) custom-call(s32[1]{0:T(128)} %bitcast.place_ref, s32[1]{0:T(128)S(6)} %copy.7.count_ref, s32[4,8192]{1,0:T(4,128)S(1)} %copy-done, f32[1,8192]{1,0:T(1,128)S(1)} %bitcast.13, f32[1,8192]{1,0:T(1,128)S(1)} %bitcast.15, f32[3,8192]{1,0:T(4,128)S(1)} %copy-done.1, ...), custom_call_target="tpu_custom_call" | custom-call | tf_op jit(solution)/shard_map/drag/pallas_call | solution.py:619
  (3 shorter events, 0.1 us)
Async XLA Ops:
  2.4 6.0 %collective-permute-start = (f32[4,8192]{1,0:T(4,128)S(1)}, f32[4,8192]{1,0:T(4,128)S(1)}, u32[]{:S(2)}, u32[]{:S(2)}) collective-permute-start(f32[4,8192]{1,0:T(4,128)S(1)} %grains.1.grain_ref), channel_id=1, source_target_pairs={{0,2},{1,3},{2,0},{3,1},{4,6},{5,7},{6,4},{7,5},{8,10},{9,11},{10,... | collective-permute-start | bytes 393224 | tf_op jit(solution)/shard_map/ppermute | solution.py:464
  3.7 2.9 %collective-permute-start.1 = (f32[4,8192]{1,0:T(4,128)S(1)}, f32[4,8192]{1,0:T(4,128)S(1)}, u32[]{:S(2)}, u32[]{:S(2)}) collective-permute-start(f32[4,8192]{1,0:T(4,128)S(1)} %grains.1.grain_ref), channel_id=1, source_target_pairs={{0,1},{1,0},{2,3},{3,2},{4,5},{5,4},{6,7},{7,6},{8,9},{9,8},{10,11... | collective-permute-start | bytes 393224 | tf_op jit(solution)/shard_map/ppermute | solution.py:464
  8.5 2.0 %collective-permute-start.2 = (f32[4,8192]{1,0:T(4,128)S(1)}, f32[4,8192]{1,0:T(4,128)S(1)}, u32[]{:S(2)}, u32[]{:S(2)}) collective-permute-start(f32[4,8192]{1,0:T(4,128)S(1)} %collective-permute-done.grain_ref), channel_id=1, source_target_pairs={{0,1},{1,0},{2,3},{3,2},{4,5},{5,4},{6,7},{7,6},{8,9},{9,8},{10,11... | collective-permute-start | bytes 393224 | tf_op jit(solution)/shard_map/ppermute | solution.py:464
  12.8 8.8 %collective-permute-start.3 = (f32[384,128]{1,0:T(8,128)S(1)}, f32[384,128]{1,0:T(8,128)S(1)}, u32[]{:S(2)}, u32[]{:S(2)}) collective-permute-start(f32[384,128]{1,0:T(8,128)S(1)} %get-tuple-element.22.own_ref), channel_id=1, source_target_pairs={{4,8},{12,16},{20,24},{8,4},{16,12},{24,20},{5,9},{13,17},{21,25},... | collective-permute-start | bytes 589832 | tf_op jit(solution)/shard_map/ppermute | solution.py:473
  15.8 10.8 %collective-permute-start.4 = (f32[384,128]{1,0:T(8,128)S(1)}, f32[384,128]{1,0:T(8,128)S(1)}, u32[]{:S(2)}, u32[]{:S(2)}) collective-permute-start(f32[384,128]{1,0:T(8,128)S(1)} %get-tuple-element.22.own_ref), channel_id=1, source_target_pairs={{0,4},{8,12},{16,20},{24,28},{4,0},{12,8},{20,16},{28,24},{1,5},{9... | collective-permute-start | bytes 589832 | tf_op jit(solution)/shard_map/ppermute | solution.py:473
  17.2 6.0 %collective-permute-start.5 = (f32[320,128]{1,0:T(8,128)S(1)}, f32[320,128]{1,0:T(8,128)S(1)}, u32[]{:S(2)}, u32[]{:S(2)}) collective-permute-start(f32[320,128]{1,0:T(8,128)S(1)} %get-tuple-element.25), channel_id=1, source_target_pairs={{0,8},{4,12},{16,24},{20,28},{8,0},{12,4},{24,16},{28,20},{1,9},{5... | collective-permute-start | bytes 491528 | tf_op jit(solution)/shard_map/ppermute | solution.py:473
  17.4 7.4 %collective-permute-start.6 = (f32[320,128]{1,0:T(8,128)S(1)}, f32[320,128]{1,0:T(8,128)S(1)}, u32[]{:S(2)}, u32[]{:S(2)}) collective-permute-start(f32[320,128]{1,0:T(8,128)S(1)} %get-tuple-element.25), channel_id=1, source_target_pairs={{8,16},{12,20},{16,8},{20,12},{9,17},{13,21},{17,9},{21,13},{10,18... | collective-permute-start | bytes 491528 | tf_op jit(solution)/shard_map/ppermute | solution.py:473
  21.6 7.5 %collective-permute-start.7 = (f32[1,128,128]{2,1,0:T(8,128)S(1)}, f32[1,128,128]{2,1,0:T(8,128)S(1)}, u32[]{:S(2)}, u32[]{:S(2)}) collective-permute-start(f32[1,128,128]{2,1,0:T(8,128)S(1)} %bitcast.16), channel_id=1, source_target_pairs={{0,2},{1,3},{2,0},{3,1},{4,6},{5,7},{6,4},{7,5},{8,10},{9,11},{10,... | collective-permute-start | bytes 196616 | tf_op jit(solution)/shard_map/ppermute | solution.py:464
  29.1 4.8 %copy-start = (s32[4,8192]{1,0:T(4,128)S(1)}, s32[4,8192]{1,0:T(4,128)}, u32[]{:S(2)}) copy-start(s32[4,8192]{1,0:T(4,128)} %cell_ref.7) | copy-start | bytes 393220
  29.1 4.8 %copy-start.2 = (f32[8192]{0:T(1024)S(1)}, f32[8192]{0:T(1024)}, u32[]{:S(2)}) copy-start(f32[8192]{0:T(1024)} %param.7) | copy-start | bytes 98308
  29.1 6.7 %collective-permute-start.8 = (f32[160,128]{1,0:T(8,128)S(1)}, f32[160,128]{1,0:T(8,128)S(1)}, u32[]{:S(2)}, u32[]{:S(2)}) collective-permute-start(f32[160,128]{1,0:T(8,128)S(1)} %get-tuple-element.33.refs_0_), channel_id=1, source_target_pairs={{4,8},{12,16},{20,24},{8,4},{16,12},{24,20},{5,9},{13,17},{21,25},... | collective-permute-start | bytes 245768 | tf_op jit(solution)/shard_map/ppermute | solution.py:473
  32.5 5.7 %collective-permute-start.9 = (f32[160,128]{1,0:T(8,128)S(1)}, f32[160,128]{1,0:T(8,128)S(1)}, u32[]{:S(2)}, u32[]{:S(2)}) collective-permute-start(f32[160,128]{1,0:T(8,128)S(1)} %get-tuple-element.33.refs_0_), channel_id=1, source_target_pairs={{0,4},{8,12},{16,20},{24,28},{4,0},{12,8},{20,16},{28,24},{1,5},{9... | collective-permute-start | bytes 245768 | tf_op jit(solution)/shard_map/ppermute | solution.py:473
  39.1 4.3 %collective-permute-start.10 = (f32[1,224,128]{2,1,0:T(8,128)S(1)}, f32[1,224,128]{2,1,0:T(8,128)S(1)}, u32[]{:S(2)}, u32[]{:S(2)}) collective-permute-start(f32[1,224,128]{2,1,0:T(8,128)S(1)} %bitcast.6), channel_id=1, source_target_pairs={{0,2},{1,3},{2,0},{3,1},{4,6},{5,7},{6,4},{7,5},{8,10},{9,11},{10,... | collective-permute-start | bytes 344072 | tf_op jit(solution)/shard_map/ppermute | solution.py:464
  43.4 3.7 %copy-start.1 = (f32[3,8192]{1,0:T(4,128)S(1)}, f32[3,8192]{1,0:T(4,128)}, u32[]{:S(2)}) copy-start(f32[3,8192]{1,0:T(4,128)} %refs_0_.3) | copy-start | bytes 294916
  43.4 3.7 %copy-start.3 = (f32[8192]{0:T(1024)S(1)}, f32[8192]{0:T(1024)}, u32[]{:S(2)}) copy-start(f32[8192]{0:T(1024)} %param.8) | copy-start | bytes 98308
  43.4 3.6 %collective-permute-start.11 = (f32[2,352,128]{2,1,0:T(8,128)S(1)}, f32[2,352,128]{2,1,0:T(8,128)S(1)}, u32[]{:S(2)}, u32[]{:S(2)}) collective-permute-start(f32[2,352,128]{2,1,0:T(8,128)S(1)} %pad_maximum_fusion), channel_id=1, source_target_pairs={{0,1},{1,0},{2,3},{3,2},{4,5},{5,4},{6,7},{7,6},{8,9},{9,8},{10,11... | collective-permute-start | bytes 1081352 | tf_op jit(solution)/shard_map/ppermute | solution.py:464

commit v10 on v9

--- a/solution.py
+++ b/solution.py
@@ -454,7 +454,7 @@
     weight = grain_weight.reshape(1, grains)
     volume = grain_volume.reshape(1, grains)
 
-    grain_chunk = min(grains, 512)
+    grain_chunk = min(grains, 1024)
 
     def cells(*shape):
         return jax.ShapeDtypeStruct(shape, jnp.float32)

time: 53.1 us -> 53.1 us (level)
  no operation moved by 1% of the time
where the time goes in v10:
time: 53.1 us; the launch traced here: 52.9 us
  Pallas kernels  24.6 us (46%)
  starting transfers between devices  18.9 us (36%)
  waiting for transfers between devices  7.83 us (15%)
  between operations  1.5 us (3%)
    ppermute x6, starting transfers between devices, swapped(): lax.ppermute(value, 'slab', pairs + [(high, low) for low, high in pairs])  12.4 us
    ppermute x6, waiting for transfers between devices, swapped(): lax.ppermute(value, 'slab', pairs + [(high, low) for low, high in pairs])  6.89 us
    ppermute x6, starting transfers between devices, over_quad(): return lax.ppermute(value, 'quad', pairs)  6.51 us
    pallas_call x1, Pallas kernels, body(): pl.pallas_call(functools.partial(drag_kernel, quads, grain_chunk), out_sh...  5.89 us
    pallas_call x3, Pallas kernels, deposited(): pl.pallas_call(functools.partial(deposit_kernel, quads, deposit_chunk), o...  5.68 us
    pallas_call x2, Pallas kernels, sampled_from(): pl.pallas_call(functools.partial(sampled_kernel, quads, grain_chunk, plac...  4.32 us
    pallas_call x1, Pallas kernels, body(): pl.pallas_call(functools.partial(relax_kernel, quads), out_shape=[cells(p...  2.42 us
    pallas_call x1, Pallas kernels, body(): pl.pallas_call(functools.partial(coefficient_kernel, quads, deposit_chunk...  2.33 us
  transfers between devices with their start and end apart: 12, of which 5 were waited for; matrix products, arithmetic and copies ran while one was open for 0% of the time, Pallas kernels for 27%

profile of v10, /device:TPU:9, one launch (start us, length us, event | category | flops | bytes accessed | tf_op | source)
XLA Modules:
  0.0 52.9 jit_solution(18117630952038422282)
XLA Ops:
  1.3 1.1 %grains.1.grain_ref = f32[4,8192]{1,0:T(4,128)S(1)} custom-call(s32[1]{0:T(128)S(6)} %copy.7.count_ref, s32[4,8192]{1,0:T(4,128)} %cell_ref.7, f32[1,8192]{1,0:T(1,128)} %bitcast.9, f32[1,8192]{1,0:T(1,128)} %bitcast.14, f32[3,8192]{1,0:T(4,128)} %refs_0_.3), custom_call_target="tpu_custom_call" | custom-call | tf_op jit(solution)/shard_map/grains/pallas_call | solution.py:486
  2.4 1.3 %collective-permute-start = (f32[4,8192]{1,0:T(4,128)S(1)}, f32[4,8192]{1,0:T(4,128)S(1)}, u32[]{:S(2)}, u32[]{:S(2)}) collective-permute-start(f32[4,8192]{1,0:T(4,128)S(1)} %grains.1.grain_ref), channel_id=1, source_target_pairs={{0,2},{1,3},{2,0},{3,1},{4,6},{5,7},{6,4},{7,5},{8,10},{9,11},{10,... | collective-permute-start | bytes 393224 | tf_op jit(solution)/shard_map/ppermute | solution.py:464
  3.7 1.0 %collective-permute-start.1 = (f32[4,8192]{1,0:T(4,128)S(1)}, f32[4,8192]{1,0:T(4,128)S(1)}, u32[]{:S(2)}, u32[]{:S(2)}) collective-permute-start(f32[4,8192]{1,0:T(4,128)S(1)} %grains.1.grain_ref), channel_id=1, source_target_pairs={{0,1},{1,0},{2,3},{3,2},{4,5},{5,4},{6,7},{7,6},{8,9},{9,8},{10,11... | collective-permute-start | bytes 393224 | tf_op jit(solution)/shard_map/ppermute | solution.py:464
  4.6 1.9 %deposit.3.refs_0_ = f32[384,256]{1,0:T(8,128)S(1)} custom-call(s32[1]{0:T(128)} %bitcast.place_ref, f32[4,8192]{1,0:T(4,128)S(1)} %grains.1.grain_ref), custom_call_target="tpu_custom_call" | custom-call | flops 1610612736 | bytes 1048576 | tf_op jit(solution)/shard_map/deposit/pallas_call | solution.py:516
  6.5 0.0 collective-permute-done.1.grain_ref
  6.5 1.9 %deposit.4.refs_0_ = f32[384,256]{1,0:T(8,128)S(1)} custom-call(s32[1]{0:T(128)} %bitcast.place_ref, f32[4,8192]{1,0:T(4,128)S(1)} %collective-permute-done.1.grain_ref, f32[384,256]{1,0:T(8,128)S(1)} %deposit.3.refs_0_), custom_call_target="tpu_custom_call" | custom-call | flops 1610612736 | bytes 1048576 | tf_op jit(solution)/shard_map/deposit/pallas_call | solution.py:516
  8.5 0.0 collective-permute-done.grain_ref
  8.5 0.1 collective-permute-start.2
  8.5 1.9 %deposit.5.refs_1_ = f32[384,256]{1,0:T(8,128)S(1)} custom-call(s32[1]{0:T(128)} %bitcast.place_ref, f32[4,8192]{1,0:T(4,128)S(1)} %collective-permute-done.grain_ref, f32[384,256]{1,0:T(8,128)S(1)} %deposit.4.refs_0_), custom_call_target="tpu_custom_call" | custom-call | flops 1610612736 | bytes 1048576 | tf_op jit(solution)/shard_map/deposit/pallas_call | solution.py:516
  10.4 0.0 collective-permute-done.2.refs_0_
  10.5 2.3 %coefficients.1 = (f32[384,128]{1,0:T(8,128)S(1)}, f32[320,128]{1,0:T(8,128)S(1)}, f32[128,128]{1,0:T(8,128)S(1)}) custom-call(s32[1]{0:T(128)} %bitcast.place_ref, f32[4,8192]{1,0:T(4,128)S(1)} %collective-permute-done.2.refs_0_, f32[384,256]{1,0:T(8,128)S(1)} %deposit.5.refs_1_), custom_call_target="tpu_custom_call" | custom-call | tf_op jit(solution)/shard_map/coefficients/pallas_call | solution.py:535
  12.8 3.0 %collective-permute-start.3 = (f32[384,128]{1,0:T(8,128)S(1)}, f32[384,128]{1,0:T(8,128)S(1)}, u32[]{:S(2)}, u32[]{:S(2)}) collective-permute-start(f32[384,128]{1,0:T(8,128)S(1)} %get-tuple-element.22.own_ref), channel_id=1, source_target_pairs={{4,8},{12,16},{20,24},{8,4},{16,12},{24,20},{5,9},{13,17},{21,25},... | collective-permute-start | bytes 589832 | tf_op jit(solution)/shard_map/ppermute | solution.py:473
  15.8 1.4 %collective-permute-start.4 = (f32[384,128]{1,0:T(8,128)S(1)}, f32[384,128]{1,0:T(8,128)S(1)}, u32[]{:S(2)}, u32[]{:S(2)}) collective-permute-start(f32[384,128]{1,0:T(8,128)S(1)} %get-tuple-element.22.own_ref), channel_id=1, source_target_pairs={{0,4},{8,12},{16,20},{24,28},{4,0},{12,8},{20,16},{28,24},{1,5},{9... | collective-permute-start | bytes 589832 | tf_op jit(solution)/shard_map/ppermute | solution.py:473
  17.2 0.2 collective-permute-start.5
  17.4 3.0 %collective-permute-start.6 = (f32[320,128]{1,0:T(8,128)S(1)}, f32[320,128]{1,0:T(8,128)S(1)}, u32[]{:S(2)}, u32[]{:S(2)}) collective-permute-start(f32[320,128]{1,0:T(8,128)S(1)} %get-tuple-element.25), channel_id=1, source_target_pairs={{8,16},{12,20},{16,8},{20,12},{9,17},{13,21},{17,9},{21,13},{10,18... | collective-permute-start | bytes 491528 | tf_op jit(solution)/shard_map/ppermute | solution.py:473
  20.5 1.1 %collective-permute-done.3.refs_0_ = f32[384,128]{1,0:T(8,128)S(1)} collective-permute-done((f32[384,128]{1,0:T(8,128)S(1)}, f32[384,128]{1,0:T(8,128)S(1)}, u32[]{:S(2)}, u32[]{:S(2)}) %collective-permute-start.3) | collective-permute-done | bytes 196640 | tf_op jit(solution)/shard_map/ppermute | solution.py:473
  21.6 1.6 %collective-permute-start.7 = (f32[1,128,128]{2,1,0:T(8,128)S(1)}, f32[1,128,128]{2,1,0:T(8,128)S(1)}, u32[]{:S(2)}, u32[]{:S(2)}) collective-permute-start(f32[1,128,128]{2,1,0:T(8,128)S(1)} %bitcast.16), channel_id=1, source_target_pairs={{0,2},{1,3},{2,0},{3,1},{4,6},{5,7},{6,4},{7,5},{8,10},{9,11},{10,... | collective-permute-start | bytes 196616 | tf_op jit(solution)/shard_map/ppermute | solution.py:464
  23.2 0.0 collective-permute-done.5.refs_2_
  23.2 1.6 %collective-permute-done.6.refs_3_ = f32[320,128]{1,0:T(8,128)S(1)} collective-permute-done((f32[320,128]{1,0:T(8,128)S(1)}, f32[320,128]{1,0:T(8,128)S(1)}, u32[]{:S(2)}, u32[]{:S(2)}) %collective-permute-start.6) | collective-permute-done | bytes 163872 | tf_op jit(solution)/shard_map/ppermute | solution.py:473
  24.9 1.8 %collective-permute-done.4.refs_1_ = f32[384,128]{1,0:T(8,128)S(1)} collective-permute-done((f32[384,128]{1,0:T(8,128)S(1)}, f32[384,128]{1,0:T(8,128)S(1)}, u32[]{:S(2)}, u32[]{:S(2)}) %collective-permute-start.4) | collective-permute-done | bytes 196640 | tf_op jit(solution)/shard_map/ppermute | solution.py:473
  26.6 2.4 %relax.1 = (f32[160,128]{1,0:T(8,128)S(1)}, f32[20,64,128]{2,1,0:T(8,128)S(1)}, f32[20,64,128]{2,1,0:T(8,128)S(1)}) custom-call(s32[1]{0:T(128)} %bitcast.3.slab_ref, f32[384,128]{1,0:T(8,128)S(1)} %get-tuple-element.22.own_ref, f32[384,128]{1,0:T(8,128)S(1)} %collective-permute-done.3.refs_0_, f32[384,128]{1,0:T(8,128)S(1)} %collective-permute-done.4.refs_1_, ...), custom_call_target="tpu_custom_call" | custom-call | tf_op jit(solution)/shard_map/relax/pallas_call | solution.py:557
  29.1 0.0 copy-start
  29.1 0.0 copy-start.2
  29.1 0.0 collective-permute-done.7
  29.1 3.3 %collective-permute-start.8 = (f32[160,128]{1,0:T(8,128)S(1)}, f32[160,128]{1,0:T(8,128)S(1)}, u32[]{:S(2)}, u32[]{:S(2)}) collective-permute-start(f32[160,128]{1,0:T(8,128)S(1)} %get-tuple-element.33.refs_0_), channel_id=1, source_target_pairs={{4,8},{12,16},{20,24},{8,4},{16,12},{24,20},{5,9},{13,17},{21,25},... | collective-permute-start | bytes 245768 | tf_op jit(solution)/shard_map/ppermute | solution.py:473
  32.5 1.4 %collective-permute-start.9 = (f32[160,128]{1,0:T(8,128)S(1)}, f32[160,128]{1,0:T(8,128)S(1)}, u32[]{:S(2)}, u32[]{:S(2)}) collective-permute-start(f32[160,128]{1,0:T(8,128)S(1)} %get-tuple-element.33.refs_0_), channel_id=1, source_target_pairs={{0,4},{8,12},{16,20},{24,28},{4,0},{12,8},{20,16},{28,24},{1,5},{9... | collective-permute-start | bytes 245768 | tf_op jit(solution)/shard_map/ppermute | solution.py:473
  33.9 0.0 copy-done
  33.9 0.0 copy-done.2
  33.9 1.9 %solid.1.refs_1_ = f32[1,8192]{1,0:T(1,128)S(1)} custom-call(s32[1]{0:T(128)} %bitcast.place_ref, s32[4,8192]{1,0:T(4,128)S(1)} %copy-done, f32[1,8192]{1,0:T(1,128)S(1)} %bitcast.10, f32[2,128,128]{2,1,0:T(8,128)S(1)} %pad_maximum_fusion.2.held_ref), custom_call_target="tpu_custom_call" | custom-call | flops 1073741824 | bytes 1048576 | tf_op jit(solution)/shard_map/solid/pallas_call | solution.py:571
  35.8 0.0 collective-permute-done.8.refs_1_
  35.8 2.3 %collective-permute-done.9.refs_2_ = f32[160,128]{1,0:T(8,128)S(1)} collective-permute-done((f32[160,128]{1,0:T(8,128)S(1)}, f32[160,128]{1,0:T(8,128)S(1)}, u32[]{:S(2)}, u32[]{:S(2)}) %collective-permute-start.9) | collective-permute-done | bytes 81952 | tf_op jit(solution)/shard_map/ppermute | solution.py:473
  38.1 0.9 %finish.1 = f32[224,128]{1,0:T(8,128)S(1)} custom-call(s32[1]{0:T(128)} %bitcast.3.slab_ref, f32[20,64,128]{2,1,0:T(8,128)S(1)} %get-tuple-element.31.offset_ref, f32[20,64,128]{2,1,0:T(8,128)S(1)} %get-tuple-element.32.gain_ref, f32[160,128]{1,0:T(8,128)S(1)} %get-tuple-element.33.refs_0_, f32[160,128]{1,0:T(8,128)S(1)} %collective-permute-done.8.refs_1_, ...), custom_call_target="tpu_custom_call" | custom-call | tf_op jit(solution)/shard_map/finish/pallas_call | solution.py:585
  39.1 1.2 %collective-permute-start.10 = (f32[1,224,128]{2,1,0:T(8,128)S(1)}, f32[1,224,128]{2,1,0:T(8,128)S(1)}, u32[]{:S(2)}, u32[]{:S(2)}) collective-permute-start(f32[1,224,128]{2,1,0:T(8,128)S(1)} %bitcast.6), channel_id=1, source_target_pairs={{0,2},{1,3},{2,0},{3,1},{4,6},{5,7},{6,4},{7,5},{8,10},{9,11},{10,... | collective-permute-start | bytes 344072 | tf_op jit(solution)/shard_map/ppermute | solution.py:464
  40.2 2.2 %sampled.2.refs_0_ = f32[3,8192]{1,0:T(4,128)S(1)} custom-call(s32[1]{0:T(128)} %bitcast.place_ref, s32[4,8192]{1,0:T(4,128)S(1)} %copy-done, f32[1,8192]{1,0:T(1,128)S(1)} %bitcast.11, f32[1,224,128]{2,1,0:T(8,128)S(1)} %bitcast.7), custom_call_target="tpu_custom_call" | custom-call | flops 1610612736 | bytes 1048576 | tf_op jit(solution)/shard_map/sampled/pallas_call | solution.py:596
  42.4 0.9 %collective-permute-done.10 = f32[1,224,128]{2,1,0:T(8,128)S(1)} collective-permute-done((f32[1,224,128]{2,1,0:T(8,128)S(1)}, f32[1,224,128]{2,1,0:T(8,128)S(1)}, u32[]{:S(2)}, u32[]{:S(2)}) %collective-permute-start.10) | collective-permute-done | bytes 114720 | tf_op jit(solution)/shard_map/ppermute | solution.py:464
  43.4 0.0 copy-start.1
  43.4 0.0 copy-start.3
  43.4 1.4 %collective-permute-start.11 = (f32[2,352,128]{2,1,0:T(8,128)S(1)}, f32[2,352,128]{2,1,0:T(8,128)S(1)}, u32[]{:S(2)}, u32[]{:S(2)}) collective-permute-start(f32[2,352,128]{2,1,0:T(8,128)S(1)} %pad_maximum_fusion), channel_id=1, source_target_pairs={{0,1},{1,0},{2,3},{3,2},{4,5},{5,4},{6,7},{7,6},{8,9},{9,8},{10,11... | collective-permute-start | bytes 1081352 | tf_op jit(solution)/shard_map/ppermute | solution.py:464
  44.8 2.2 %sampled.3.refs_2_ = f32[3,8192]{1,0:T(4,128)S(1)} custom-call(s32[1]{0:T(128)} %bitcast.place_ref, s32[4,8192]{1,0:T(4,128)S(1)} %copy-done, f32[1,8192]{1,0:T(1,128)S(1)} %bitcast.12, f32[2,224,128]{2,1,0:T(8,128)S(1)} %pad_maximum_fusion.1.held_ref.refs_3_, f32[3,8192]{1,0:T(4,128)S(1)} %sampled.2.refs_0_), custom_call_target="tpu_custom_call" | custom-call | flops 1610612736 | bytes 1048576 | tf_op jit(solution)/shard_map/sampled/pallas_call | solution.py:596
  47.0 0.0 collective-permute-done.11.refs_4_
  47.0 0.0 copy-done.1
  47.0 0.0 copy-done.3
  47.0 5.9 %drag.1 = (f32[4,16,256]{2,1,0:T(8,128)}, f32[3,8192]{1,0:T(4,128)}) custom-call(s32[1]{0:T(128)} %bitcast.place_ref, s32[1]{0:T(128)S(6)} %copy.7.count_ref, s32[4,8192]{1,0:T(4,128)S(1)} %copy-done, f32[1,8192]{1,0:T(1,128)S(1)} %bitcast.13, f32[1,8192]{1,0:T(1,128)S(1)} %bitcast.15, f32[3,8192]{1,0:T(4,128)S(1)} %copy-done.1, ...), custom_call_target="tpu_custom_call" | custom-call | tf_op jit(solution)/shard_map/drag/pallas_call | solution.py:619
  (3 shorter events, 0.1 us)
Async XLA Ops:
  2.4 6.0 %collective-permute-start = (f32[4,8192]{1,0:T(4,128)S(1)}, f32[4,8192]{1,0:T(4,128)S(1)}, u32[]{:S(2)}, u32[]{:S(2)}) collective-permute-start(f32[4,8192]{1,0:T(4,128)S(1)} %grains.1.grain_ref), channel_id=1, source_target_pairs={{0,2},{1,3},{2,0},{3,1},{4,6},{5,7},{6,4},{7,5},{8,10},{9,11},{10,... | collective-permute-start | bytes 393224 | tf_op jit(solution)/shard_map/ppermute | solution.py:464
  3.7 2.9 %collective-permute-start.1 = (f32[4,8192]{1,0:T(4,128)S(1)}, f32[4,8192]{1,0:T(4,128)S(1)}, u32[]{:S(2)}, u32[]{:S(2)}) collective-permute-start(f32[4,8192]{1,0:T(4,128)S(1)} %grains.1.grain_ref), channel_id=1, source_target_pairs={{0,1},{1,0},{2,3},{3,2},{4,5},{5,4},{6,7},{7,6},{8,9},{9,8},{10,11... | collective-permute-start | bytes 393224 | tf_op jit(solution)/shard_map/ppermute | solution.py:464
  8.5 2.0 %collective-permute-start.2 = (f32[4,8192]{1,0:T(4,128)S(1)}, f32[4,8192]{1,0:T(4,128)S(1)}, u32[]{:S(2)}, u32[]{:S(2)}) collective-permute-start(f32[4,8192]{1,0:T(4,128)S(1)} %collective-permute-done.grain_ref), channel_id=1, source_target_pairs={{0,1},{1,0},{2,3},{3,2},{4,5},{5,4},{6,7},{7,6},{8,9},{9,8},{10,11... | collective-permute-start | bytes 393224 | tf_op jit(solution)/shard_map/ppermute | solution.py:464
  12.8 8.8 %collective-permute-start.3 = (f32[384,128]{1,0:T(8,128)S(1)}, f32[384,128]{1,0:T(8,128)S(1)}, u32[]{:S(2)}, u32[]{:S(2)}) collective-permute-start(f32[384,128]{1,0:T(8,128)S(1)} %get-tuple-element.22.own_ref), channel_id=1, source_target_pairs={{4,8},{12,16},{20,24},{8,4},{16,12},{24,20},{5,9},{13,17},{21,25},... | collective-permute-start | bytes 589832 | tf_op jit(solution)/shard_map/ppermute | solution.py:473
  15.8 10.8 %collective-permute-start.4 = (f32[384,128]{1,0:T(8,128)S(1)}, f32[384,128]{1,0:T(8,128)S(1)}, u32[]{:S(2)}, u32[]{:S(2)}) collective-permute-start(f32[384,128]{1,0:T(8,128)S(1)} %get-tuple-element.22.own_ref), channel_id=1, source_target_pairs={{0,4},{8,12},{16,20},{24,28},{4,0},{12,8},{20,16},{28,24},{1,5},{9... | collective-permute-start | bytes 589832 | tf_op jit(solution)/shard_map/ppermute | solution.py:473
  17.2 6.0 %collective-permute-start.5 = (f32[320,128]{1,0:T(8,128)S(1)}, f32[320,128]{1,0:T(8,128)S(1)}, u32[]{:S(2)}, u32[]{:S(2)}) collective-permute-start(f32[320,128]{1,0:T(8,128)S(1)} %get-tuple-element.25), channel_id=1, source_target_pairs={{0,8},{4,12},{16,24},{20,28},{8,0},{12,4},{24,16},{28,20},{1,9},{5... | collective-permute-start | bytes 491528 | tf_op jit(solution)/shard_map/ppermute | solution.py:473
  17.4 7.4 %collective-permute-start.6 = (f32[320,128]{1,0:T(8,128)S(1)}, f32[320,128]{1,0:T(8,128)S(1)}, u32[]{:S(2)}, u32[]{:S(2)}) collective-permute-start(f32[320,128]{1,0:T(8,128)S(1)} %get-tuple-element.25), channel_id=1, source_target_pairs={{8,16},{12,20},{16,8},{20,12},{9,17},{13,21},{17,9},{21,13},{10,18... | collective-permute-start | bytes 491528 | tf_op jit(solution)/shard_map/ppermute | solution.py:473
  21.6 7.5 %collective-permute-start.7 = (f32[1,128,128]{2,1,0:T(8,128)S(1)}, f32[1,128,128]{2,1,0:T(8,128)S(1)}, u32[]{:S(2)}, u32[]{:S(2)}) collective-permute-start(f32[1,128,128]{2,1,0:T(8,128)S(1)} %bitcast.16), channel_id=1, source_target_pairs={{0,2},{1,3},{2,0},{3,1},{4,6},{5,7},{6,4},{7,5},{8,10},{9,11},{10,... | collective-permute-start | bytes 196616 | tf_op jit(solution)/shard_map/ppermute | solution.py:464
  29.1 4.8 %copy-start = (s32[4,8192]{1,0:T(4,128)S(1)}, s32[4,8192]{1,0:T(4,128)}, u32[]{:S(2)}) copy-start(s32[4,8192]{1,0:T(4,128)} %cell_ref.7) | copy-start | bytes 393220
  29.1 4.8 %copy-start.2 = (f32[8192]{0:T(1024)S(1)}, f32[8192]{0:T(1024)}, u32[]{:S(2)}) copy-start(f32[8192]{0:T(1024)} %param.7) | copy-start | bytes 98308
  29.1 6.7 %collective-permute-start.8 = (f32[160,128]{1,0:T(8,128)S(1)}, f32[160,128]{1,0:T(8,128)S(1)}, u32[]{:S(2)}, u32[]{:S(2)}) collective-permute-start(f32[160,128]{1,0:T(8,128)S(1)} %get-tuple-element.33.refs_0_), channel_id=1, source_target_pairs={{4,8},{12,16},{20,24},{8,4},{16,12},{24,20},{5,9},{13,17},{21,25},... | collective-permute-start | bytes 245768 | tf_op jit(solution)/shard_map/ppermute | solution.py:473
  32.5 5.7 %collective-permute-start.9 = (f32[160,128]{1,0:T(8,128)S(1)}, f32[160,128]{1,0:T(8,128)S(1)}, u32[]{:S(2)}, u32[]{:S(2)}) collective-permute-start(f32[160,128]{1,0:T(8,128)S(1)} %get-tuple-element.33.refs_0_), channel_id=1, source_target_pairs={{0,4},{8,12},{16,20},{24,28},{4,0},{12,8},{20,16},{28,24},{1,5},{9... | collective-permute-start | bytes 245768 | tf_op jit(solution)/shard_map/ppermute | solution.py:473
  39.1 4.3 %collective-permute-start.10 = (f32[1,224,128]{2,1,0:T(8,128)S(1)}, f32[1,224,128]{2,1,0:T(8,128)S(1)}, u32[]{:S(2)}, u32[]{:S(2)}) collective-permute-start(f32[1,224,128]{2,1,0:T(8,128)S(1)} %bitcast.6), channel_id=1, source_target_pairs={{0,2},{1,3},{2,0},{3,1},{4,6},{5,7},{6,4},{7,5},{8,10},{9,11},{10,... | collective-permute-start | bytes 344072 | tf_op jit(solution)/shard_map/ppermute | solution.py:464
  43.4 3.6 %copy-start.1 = (f32[3,8192]{1,0:T(4,128)S(1)}, f32[3,8192]{1,0:T(4,128)}, u32[]{:S(2)}) copy-start(f32[3,8192]{1,0:T(4,128)} %refs_0_.3) | copy-start | bytes 294916
  43.4 3.6 %copy-start.3 = (f32[8192]{0:T(1024)S(1)}, f32[8192]{0:T(1024)}, u32[]{:S(2)}) copy-start(f32[8192]{0:T(1024)} %param.8) | copy-start | bytes 98308
  43.4 3.6 %collective-permute-start.11 = (f32[2,352,128]{2,1,0:T(8,128)S(1)}, f32[2,352,128]{2,1,0:T(8,128)S(1)}, u32[]{:S(2)}, u32[]{:S(2)}) collective-permute-start(f32[2,352,128]{2,1,0:T(8,128)S(1)} %pad_maximum_fusion), channel_id=1, source_target_pairs={{0,1},{1,0},{2,3},{3,2},{4,5},{5,4},{6,7},{7,6},{8,9},{9,8},{10,11... | collective-permute-start | bytes 1081352 | tf_op jit(solution)/shard_map/ppermute | solution.py:464
